TPU v7x, 32 devices: a whole 2x2x4 slice. The times are simulated.
32 devices in a mesh: seq: 8 (over z, x), head: 4 (over y, core).
Axes of the slice: x: 2, y: 2, z: 4, core: 2. Of those that a mesh axis runs over, the one named last changes fastest.
Arguments:
- tokens: bfloat16 [8192, 2048], P('seq'), may hold values from -12 to 12
- cotangent: bfloat16 [8192, 2048], P('seq'), may hold values from -6 to 6
- norm1_gain: float32 [2048], P('seq'), may hold values from 0.5 to 1.5
- w_query: float32 [2048, 2048], P('seq', 'head'), may hold values from -0.125 to 0.125
- w_key: float32 [2048, 2048], P('seq', 'head'), may hold values from -0.125 to 0.125
- w_value: float32 [2048, 4096], P('seq', 'head'), may hold values from -0.125 to 0.125
- w_gate_out: float32 [2048, 4096], P('seq', 'head'), may hold values from -0.125 to 0.125
- w_alpha: float32 [2048, 16], P('seq', 'head'), may hold values from -0.125 to 0.125
- w_beta: float32 [2048, 16], P('seq', 'head'), may hold values from -1 to 1
- conv_query: float32 [4, 16, 128], P(None, 'head', 'seq'), may hold values from -4 to 4
- conv_key: float32 [4, 16, 128], P(None, 'head', 'seq'), may hold values from -4 to 4
- conv_value: float32 [4, 16, 256], P(None, 'head', 'seq'), may hold values from -4 to 4
- a_log: float32 [16], P('seq'), may hold values from -11 to -4
- dt_bias: float32 [16], P('seq'), may hold values from -3 to 1
- out_gain: float32 [256], P('seq'), may hold values from 0.5 to 1.5
- w_out: float32 [4096, 2048], P('head', 'seq'), may hold values from -0.1875 to 0.1875
- norm2_gain: float32 [2048], P('seq'), may hold values from 0.5 to 1.5
- w_gate: float32 [2048, 5504], P('seq', 'head'), may hold values from -0.125 to 0.125
- w_up: float32 [2048, 5504], P('seq', 'head'), may hold values from -0.125 to 0.125
- w_down: float32 [5504, 2048], P('head', 'seq'), may hold values from -0.125 to 0.125
Outputs:
- out: bfloat16 [8192, 2048], P('seq')
- grad_tokens: float32 [8192, 2048], P('seq')
- grad_norm1_gain: float32 [2048], P('seq')
- grad_w_query: float32 [2048, 2048], P('seq', 'head')
- grad_w_key: float32 [2048, 2048], P('seq', 'head')
- grad_w_value: float32 [2048, 4096], P('seq', 'head')
- grad_w_gate_out: float32 [2048, 4096], P('seq', 'head')
- grad_w_alpha: float32 [2048, 16], P('seq', 'head')
- grad_w_beta: float32 [2048, 16], P('seq', 'head')
- grad_conv_query: float32 [4, 16, 128], P(None, 'head', 'seq')
- grad_conv_key: float32 [4, 16, 128], P(None, 'head', 'seq')
- grad_conv_value: float32 [4, 16, 256], P(None, 'head', 'seq')
- grad_a_log: float32 [16], P('seq')
- grad_dt_bias: float32 [16], P('seq')
- grad_out_gain: float32 [256], P('seq')
- grad_w_out: float32 [4096, 2048], P('head', 'seq')
- grad_norm2_gain: float32 [2048], P('seq')
- grad_w_gate: float32 [2048, 5504], P('seq', 'head')
- grad_w_up: float32 [2048, 5504], P('seq', 'head')
- grad_w_down: float32 [5504, 2048], P('head', 'seq')
All inputs are finite; a program needn't handle non-finite values.
Results may differ from a plain program's by a relative error of at most 0.03.
Values may be sent and summed in bfloat16 or wider, within the bound.
No kernel may reach another device: no remote copies, remote signals or barrier semaphores. Data moves between devices by JAX's collectives and lax.ppermute only.
A program may use at most 512 MiB of HBM per device.

v0:
```python
import jax
import jax.numpy as jnp
from jax import lax
from jax.sharding import PartitionSpec as P

BLOCK = 64


highest = lax.Precision.HIGHEST
eps_norm = 1e-06


def passed_along(block, axis, distance):
    devices = range(lax.axis_size(axis))
    route = [(i - distance, i) for i in devices if i - distance in devices]
    return lax.ppermute(block, axis, route)


def product(left_side, right_side):
    return jnp.dot(left_side, right_side, preferred_element_type=jnp.float32)


def product_left(left_side, right_side):
    return lax.dot_general(
        left_side, right_side, (((0,), (0,)), ((), ())), preferred_element_type=jnp.float32
    )


def product_right(left_side, right_side):
    return lax.dot_general(
        left_side, right_side, (((1,), (1,)), ((), ())), preferred_element_type=jnp.float32
    )


def rms_scale(values, scale_gain):
    return (
        values
        * lax.rsqrt(jnp.mean(values * values, axis=-1, keepdims=True) + eps_norm)
        * scale_gain
    )


def unit_rows(values):
    return values * lax.rsqrt(jnp.sum(values * values, axis=-1, keepdims=True) + eps_norm)


def swiglu(gate_act, up_act):
    return jax.nn.silu(gate_act) * up_act


def out_gate(outputs, gate_pre, gain_out):
    gated_out = rms_scale(outputs, gain_out) * jax.nn.silu(gate_pre).reshape(outputs.shape)
    return gated_out.reshape(outputs.shape[0], -1)


def conv_features(
    ext_query,
    ext_key,
    ext_value,
    alpha_pre,
    beta_pre,
    filt_query,
    filt_key,
    filt_value,
    rate_log,
    bias_here,
):
    row_count = alpha_pre.shape[0]
    heads_here = alpha_pre.shape[1]

    def causal(extended, filters):
        flat_taps = filters.reshape(4, -1)
        running = flat_taps[0] * extended[0:row_count]
        for offset in range(1, 4):
            running = running + flat_taps[offset] * extended[offset : offset + row_count]
        return jax.nn.silu(running).reshape(row_count, heads_here, -1)

    queries = causal(ext_query, filt_query)
    queries = unit_rows(queries) * queries.shape[2] ** (-0.5)
    key_rows = unit_rows(causal(ext_key, filt_key))
    values = causal(ext_value, filt_value)
    log_decay = -jnp.exp(rate_log) * jax.nn.softplus(alpha_pre + bias_here)
    strength = jax.nn.sigmoid(beta_pre)
    return (queries, key_rows, values, log_decay, strength)


def block_rule(queries, key_rows, values, log_decay, strength):
    row_count, heads_here, key_size = queries.shape
    value_size = values.shape[2]
    blocks = row_count // BLOCK
    augmented = jnp.concatenate(
        [values, jnp.zeros((row_count, heads_here, key_size), jnp.float32)], axis=2
    )

    def to_blocks(member):
        shaped = member.reshape((blocks, BLOCK) + member.shape[1:])
        return jnp.swapaxes(shaped, 1, 2)

    initial = jnp.concatenate(
        [
            jnp.zeros((heads_here, value_size, key_size), jnp.float32),
            jnp.broadcast_to(
                jnp.eye(key_size, dtype=jnp.float32), (heads_here, key_size, key_size)
            ),
        ],
        axis=1,
    )
    positions = jnp.arange(BLOCK)
    lower_mask = positions[:, None] >= positions[None, :]
    strict_mask = positions[:, None] > positions[None, :]
    unit_lower = jnp.eye(BLOCK, dtype=jnp.float32)

    def block_step(state_now, block_data):
        q_blk, k_blk, v_blk, g_blk, b_blk = block_data
        cumulative = jnp.cumsum(g_blk, axis=1)
        log_gap = cumulative[:, :, None] - cumulative[:, None, :]
        decay_ratio = jnp.where(lower_mask, jnp.exp(jnp.where(lower_mask, log_gap, 0.0)), 0.0)
        key_gram = jnp.einsum("hik,hjk->hij", k_blk, k_blk, precision=highest)
        coupling = (
            jnp.where(strict_mask, b_blk[:, :, None] * decay_ratio * key_gram, 0.0) + unit_lower
        )
        growth = jnp.exp(cumulative)[:, :, None]
        from_state = jnp.einsum("hck,hrk->hcr", k_blk, state_now, precision=highest)
        right_side = b_blk[:, :, None] * (v_blk - growth * from_state)
        errors = jax.scipy.linalg.solve_triangular(
            coupling, right_side, lower=True, unit_diagonal=True
        )
        query_key = jnp.einsum("hik,hjk->hij", q_blk, k_blk, precision=highest) * decay_ratio
        out_blk = growth * jnp.einsum(
            "hck,hrk->hcr", q_blk, state_now, precision=highest
        ) + jnp.einsum("hij,hjr->hir", query_key, errors, precision=highest)
        tail_decay = jnp.exp(cumulative[:, -1:] - cumulative)[:, :, None]
        state_next = jnp.exp(cumulative[:, -1])[:, None, None] * state_now + jnp.einsum(
            "hcr,hck->hrk", errors, tail_decay * k_blk, precision=highest
        )
        return (state_next, out_blk)

    final_state, outputs = lax.scan(
        block_step,
        initial,
        (
            to_blocks(queries),
            to_blocks(key_rows),
            to_blocks(augmented),
            to_blocks(log_decay),
            to_blocks(strength),
        ),
    )
    outputs = jnp.swapaxes(outputs, 1, 2).reshape(row_count, heads_here, value_size + key_size)
    return (outputs[:, :, :value_size], outputs[:, :, value_size:], final_state)


def on_device(
    tokens,
    cotangent,
    norm1_gain,
    w_query,
    w_key,
    w_value,
    w_gate_out,
    w_alpha,
    w_beta,
    conv_query,
    conv_key,
    conv_value,
    a_log,
    dt_bias,
    out_gain,
    w_out,
    norm2_gain,
    w_gate,
    w_up,
    w_down,
):
    gathered = (
        lax.all_gather(norm1_gain.astype(jnp.bfloat16), "seq", axis=0, tiled=True),
        lax.all_gather(w_query.astype(jnp.bfloat16), "seq", axis=0, tiled=True),
        lax.all_gather(w_key.astype(jnp.bfloat16), "seq", axis=0, tiled=True),
        lax.all_gather(w_value.astype(jnp.bfloat16), "seq", axis=0, tiled=True),
        lax.all_gather(w_gate_out.astype(jnp.bfloat16), "seq", axis=0, tiled=True),
        lax.all_gather(w_alpha.astype(jnp.bfloat16), "seq", axis=0, tiled=True),
        lax.all_gather(w_beta.astype(jnp.bfloat16), "seq", axis=0, tiled=True),
        lax.all_gather(conv_query.astype(jnp.bfloat16), "seq", axis=2, tiled=True),
        lax.all_gather(conv_key.astype(jnp.bfloat16), "seq", axis=2, tiled=True),
        lax.all_gather(conv_value.astype(jnp.bfloat16), "seq", axis=2, tiled=True),
        lax.all_gather(a_log.astype(jnp.bfloat16), "seq", axis=0, tiled=True),
        lax.all_gather(dt_bias.astype(jnp.bfloat16), "seq", axis=0, tiled=True),
        lax.all_gather(out_gain.astype(jnp.bfloat16), "seq", axis=0, tiled=True),
        lax.all_gather(w_out.astype(jnp.bfloat16), "seq", axis=1, tiled=True),
        lax.all_gather(norm2_gain.astype(jnp.bfloat16), "seq", axis=0, tiled=True),
        lax.all_gather(w_gate.astype(jnp.bfloat16), "seq", axis=0, tiled=True),
        lax.all_gather(w_up.astype(jnp.bfloat16), "seq", axis=0, tiled=True),
        lax.all_gather(w_down.astype(jnp.bfloat16), "seq", axis=1, tiled=True),
    )
    gain_first = gathered[0].astype(jnp.float32)
    query_weight, key_weight, value_weight, gate_weight = (
        gathered[1],
        gathered[2],
        gathered[3],
        gathered[4],
    )
    alpha_weight, beta_weight = (gathered[5], gathered[6])
    filt_query = gathered[7].astype(jnp.float32)
    filt_key = gathered[8].astype(jnp.float32)
    filt_value = gathered[9].astype(jnp.float32)
    rate_all = gathered[10].astype(jnp.float32)
    bias_all = gathered[11].astype(jnp.float32)
    gain_out = gathered[12].astype(jnp.float32)
    out_weight = gathered[13]
    gain_second = gathered[14].astype(jnp.float32)
    mlp_gate, mlp_up, mlp_down = (gathered[15], gathered[16], gathered[17])
    row_count = tokens.shape[0]
    heads_here = alpha_weight.shape[1]
    total_heads = rate_all.shape[0]
    value_size = filt_value.shape[2]
    head_start = lax.axis_index("head") * heads_here
    rate_here = lax.dynamic_slice_in_dim(rate_all, head_start, heads_here)
    bias_here = lax.dynamic_slice_in_dim(bias_all, head_start, heads_here)
    inputs = tokens.astype(jnp.float32)
    normed_first, norm1_pull = jax.vjp(rms_scale, inputs, gain_first)
    normed_first = normed_first.astype(jnp.bfloat16)
    proj_query = product(normed_first, query_weight).astype(jnp.bfloat16)
    proj_key = product(normed_first, key_weight).astype(jnp.bfloat16)
    proj_value = product(normed_first, value_weight).astype(jnp.bfloat16)
    gate_pre = product(normed_first, gate_weight)
    alpha_pre = product(normed_first, alpha_weight)
    beta_pre = product(normed_first, beta_weight)
    edge_rows = passed_along(
        (proj_query[row_count - 3 :], proj_key[row_count - 3 :], proj_value[row_count - 3 :]),
        "seq",
        1,
    )
    ext_query = jnp.concatenate([edge_rows[0], proj_query], axis=0).astype(jnp.float32)
    ext_key = jnp.concatenate([edge_rows[1], proj_key], axis=0).astype(jnp.float32)
    ext_value = jnp.concatenate([edge_rows[2], proj_value], axis=0).astype(jnp.float32)
    features, conv_pull = jax.vjp(
        conv_features,
        ext_query,
        ext_key,
        ext_value,
        alpha_pre,
        beta_pre,
        filt_query,
        filt_key,
        filt_value,
        rate_here,
        bias_here,
    )
    rule_result, rule_pull = jax.vjp(
        block_rule, features[0], features[1], features[2], features[3], features[4]
    )
    value_out, ident_out, final_state = rule_result
    block_bias = final_state[:, :value_size]
    block_map = final_state[:, value_size:]
    zero_bias = jnp.zeros_like(block_bias)
    seq_count = lax.axis_size("seq")

    def relay_step(step_index, carried):
        advanced = jnp.einsum("hvk,hkj->hvj", carried, block_map, precision=highest) + block_bias
        return passed_along(advanced, "seq", 1)

    incoming = lax.fori_loop(0, seq_count - 1, relay_step, zero_bias)
    outputs = value_out + jnp.einsum("hvk,thk->thv", incoming, ident_out, precision=highest)
    gated_out, gate_pull = jax.vjp(out_gate, outputs, gate_pre, gain_out)
    gated_out = gated_out.astype(jnp.bfloat16)
    attention = lax.psum(product(gated_out, out_weight).astype(jnp.bfloat16), "head").astype(
        jnp.float32
    )
    hidden_state = inputs + attention
    normed_second, norm2_pull = jax.vjp(rms_scale, hidden_state, gain_second)
    normed_second = normed_second.astype(jnp.bfloat16)
    gate_act = product(normed_second, mlp_gate)
    up_act = product(normed_second, mlp_up)
    mixed_hidden, swiglu_pull = jax.vjp(swiglu, gate_act, up_act)
    mixed_hidden = mixed_hidden.astype(jnp.bfloat16)
    branch_part = product(mixed_hidden, mlp_down)
    branch = lax.psum(branch_part.astype(jnp.bfloat16), "head").astype(jnp.float32)
    result = (hidden_state + branch).astype(jnp.bfloat16)
    grad_mlp_down = product_left(mixed_hidden, cotangent)
    grad_mixed = product_right(cotangent, mlp_down)
    grad_gate_act, grad_up_act = swiglu_pull(grad_mixed)
    gate_rounded = grad_gate_act.astype(jnp.bfloat16)
    up_rounded = grad_up_act.astype(jnp.bfloat16)
    grad_mlp_gate = product_left(normed_second, gate_rounded)
    grad_mlp_up = product_left(normed_second, up_rounded)
    grad_normed_second = lax.psum(
        (product_right(gate_rounded, mlp_gate) + product_right(up_rounded, mlp_up)).astype(
            jnp.bfloat16
        ),
        "head",
    ).astype(jnp.float32)
    grad_from_norm2, grad_gain_second = norm2_pull(grad_normed_second)
    grad_hidden = cotangent.astype(jnp.float32) + grad_from_norm2
    attention_rounded = grad_hidden.astype(jnp.bfloat16)
    grad_out_weight = product_left(gated_out, attention_rounded)
    grad_gated = product_right(attention_rounded, out_weight)
    grad_outputs, grad_gate_pre, grad_gain_out = gate_pull(grad_gated)
    grad_ident = jnp.einsum("hvk,thv->thk", incoming, grad_outputs, precision=highest)
    local_pull = jnp.einsum("thv,thk->hvk", grad_outputs, ident_out, precision=highest)

    def relay_back(step_index, carried):
        pulled = jnp.einsum("hvk,hjk->hvj", carried, block_map, precision=highest) + local_pull
        return passed_along(pulled, "seq", -1)

    grad_final = lax.fori_loop(0, seq_count - 1, relay_back, zero_bias)
    grad_map = jnp.einsum("hvk,hvj->hkj", incoming, grad_final, precision=highest)
    grads_rule = rule_pull(
        (grad_outputs, grad_ident, jnp.concatenate([grad_final, grad_map], axis=1))
    )
    grads_conv = conv_pull(grads_rule)
    back_edges = passed_along((grads_conv[0][:3], grads_conv[1][:3], grads_conv[2][:3]), "seq", -1)
    padding = ((row_count - 3, 0), (0, 0))
    grad_query_rows = (grads_conv[0][3:] + jnp.pad(back_edges[0], padding)).astype(jnp.bfloat16)
    grad_key_rows = (grads_conv[1][3:] + jnp.pad(back_edges[1], padding)).astype(jnp.bfloat16)
    grad_value_rows = (grads_conv[2][3:] + jnp.pad(back_edges[2], padding)).astype(jnp.bfloat16)
    grad_alpha_rows = grads_conv[3].astype(jnp.bfloat16)
    grad_beta_rows = grads_conv[4].astype(jnp.bfloat16)
    grad_gate_rows = grad_gate_pre.astype(jnp.bfloat16)
    grad_query_weight = product_left(normed_first, grad_query_rows)
    grad_key_weight = product_left(normed_first, grad_key_rows)
    grad_value_weight = product_left(normed_first, grad_value_rows)
    grad_gate_weight = product_left(normed_first, grad_gate_rows)
    grad_alpha_weight = product_left(normed_first, grad_alpha_rows)
    grad_beta_weight = product_left(normed_first, grad_beta_rows)
    partial_first = product_right(grad_query_rows, query_weight) + product_right(
        grad_key_rows, key_weight
    )
    partial_first = (
        partial_first
        + product_right(grad_value_rows, value_weight)
        + product_right(grad_gate_rows, gate_weight)
    )
    partial_first = (
        partial_first
        + product_right(grad_alpha_rows, alpha_weight)
        + product_right(grad_beta_rows, beta_weight)
    )
    rate_full = lax.dynamic_update_slice_in_dim(
        jnp.zeros((total_heads,), jnp.float32), grads_conv[8], head_start, 0
    )
    bias_full = lax.dynamic_update_slice_in_dim(
        jnp.zeros((total_heads,), jnp.float32), grads_conv[9], head_start, 0
    )
    head_sums = (
        lax.psum(partial_first.astype(jnp.bfloat16), "head").astype(jnp.float32),
        lax.psum(grad_gain_out.astype(jnp.bfloat16), "head").astype(jnp.float32),
        lax.psum(rate_full.astype(jnp.bfloat16), "head").astype(jnp.float32),
        lax.psum(bias_full.astype(jnp.bfloat16), "head").astype(jnp.float32),
    )
    grad_from_norm1, grad_gain_first = norm1_pull(head_sums[0])
    grad_tokens = grad_hidden + grad_from_norm1
    reduced = (
        lax.psum_scatter(
            grad_gain_first.astype(jnp.bfloat16), "seq", scatter_dimension=0, tiled=True
        ).astype(jnp.float32),
        lax.psum_scatter(
            grad_query_weight.astype(jnp.bfloat16), "seq", scatter_dimension=0, tiled=True
        ).astype(jnp.float32),
        lax.psum_scatter(
            grad_key_weight.astype(jnp.bfloat16), "seq", scatter_dimension=0, tiled=True
        ).astype(jnp.float32),
        lax.psum_scatter(
            grad_value_weight.astype(jnp.bfloat16), "seq", scatter_dimension=0, tiled=True
        ).astype(jnp.float32),
        lax.psum_scatter(
            grad_gate_weight.astype(jnp.bfloat16), "seq", scatter_dimension=0, tiled=True
        ).astype(jnp.float32),
        lax.psum_scatter(
            grad_alpha_weight.astype(jnp.bfloat16), "seq", scatter_dimension=0, tiled=True
        ).astype(jnp.float32),
        lax.psum_scatter(
            grad_beta_weight.astype(jnp.bfloat16), "seq", scatter_dimension=0, tiled=True
        ).astype(jnp.float32),
        lax.psum_scatter(
            grads_conv[5].astype(jnp.bfloat16), "seq", scatter_dimension=2, tiled=True
        ).astype(jnp.float32),
        lax.psum_scatter(
            grads_conv[6].astype(jnp.bfloat16), "seq", scatter_dimension=2, tiled=True
        ).astype(jnp.float32),
        lax.psum_scatter(
            grads_conv[7].astype(jnp.bfloat16), "seq", scatter_dimension=2, tiled=True
        ).astype(jnp.float32),
        lax.psum_scatter(
            head_sums[2].astype(jnp.bfloat16), "seq", scatter_dimension=0, tiled=True
        ).astype(jnp.float32),
        lax.psum_scatter(
            head_sums[3].astype(jnp.bfloat16), "seq", scatter_dimension=0, tiled=True
        ).astype(jnp.float32),
        lax.psum_scatter(
            head_sums[1].astype(jnp.bfloat16), "seq", scatter_dimension=0, tiled=True
        ).astype(jnp.float32),
        lax.psum_scatter(
            grad_out_weight.astype(jnp.bfloat16), "seq", scatter_dimension=1, tiled=True
        ).astype(jnp.float32),
        lax.psum_scatter(
            grad_gain_second.astype(jnp.bfloat16), "seq", scatter_dimension=0, tiled=True
        ).astype(jnp.float32),
        lax.psum_scatter(
            grad_mlp_gate.astype(jnp.bfloat16), "seq", scatter_dimension=0, tiled=True
        ).astype(jnp.float32),
        lax.psum_scatter(
            grad_mlp_up.astype(jnp.bfloat16), "seq", scatter_dimension=0, tiled=True
        ).astype(jnp.float32),
        lax.psum_scatter(
            grad_mlp_down.astype(jnp.bfloat16), "seq", scatter_dimension=1, tiled=True
        ).astype(jnp.float32),
    )
    return (result, grad_tokens) + tuple(reduced)


def solution(mesh):
    in_specs = (
        P("seq", None),
        P("seq", None),
        P("seq"),
        P("seq", "head"),
        P("seq", "head"),
        P("seq", "head"),
        P("seq", "head"),
        P("seq", "head"),
        P("seq", "head"),
        P(None, "head", "seq"),
        P(None, "head", "seq"),
        P(None, "head", "seq"),
        P("seq"),
        P("seq"),
        P("seq"),
        P("head", "seq"),
        P("seq"),
        P("seq", "head"),
        P("seq", "head"),
        P("head", "seq"),
    )
    out_specs = (
        P("seq", None),
        P("seq", None),
        P("seq"),
        P("seq", "head"),
        P("seq", "head"),
        P("seq", "head"),
        P("seq", "head"),
        P("seq", "head"),
        P("seq", "head"),
        P(None, "head", "seq"),
        P(None, "head", "seq"),
        P(None, "head", "seq"),
        P("seq"),
        P("seq"),
        P("seq"),
        P("head", "seq"),
        P("seq"),
        P("seq", "head"),
        P("seq", "head"),
        P("head", "seq"),
    )
    return jax.shard_map(
        on_device, mesh=mesh, in_specs=in_specs, out_specs=out_specs, check_vma=False
    )
```

profile of v0, /device:TPU:0, one launch (start us, length us, event | category | flops | bytes accessed | tf_op | source)
XLA Modules:
  0.0 3936.9 jit_solution(15029634339165443870)
XLA Ops:
  18.6 22.2 all-gather
  41.0 31.0 all_gather.59
  72.6 31.1 all_gather.63
  125.0 26.2 all_gather.56
  158.6 26.3 all_gather.58
  188.9 31.5 all_gather.61
  306.5 697.8 %while.108 = (s32[]{:T(128)}, f32[4,384,128]{2,1,0:T(8,128)S(1)}, f32[16,4,64,384]{3,2,1,0:T(8,128)}, f32[16,4,64,64]{3,2,1,0:T(8,128)}, f32[16,4,64,64]{3,2,1,0...) while((s32[]{:T(128)}, f32[4,384,128]{2,1,0:T(8,128)S(1)}, ...), condition=%wide.region_5.6_spmd.clone.clone, body=%wide.region_3.5_spmd.clone.clone.sunk | while | flops 655905344 | bytes 13053405 | solution.py:138
  313.8 21.0 custom-call.47
  400.9 21.0 custom-call.47
  488.2 21.0 custom-call.47
  619.0 21.0 custom-call.47
  662.6 21.0 custom-call.47
  1011.9 106.5 %while.106 = (s32[]{:T(128)}, f32[4,256,128]{2,1,0:T(8,128)S(1)}, f32[4,128,128]{2,1,0:T(8,128)S(1)}, f32[4,256,128]{2,1,0:T(8,128)S(1)}, s32[]{:T(128)}) while((s32[]{:T(128)}, f32[4,256,128]{2,1,0:T(8,128)S(1)}, f32[4,128,128]{2,1,0:T(8,128)S(1)}, f32[4,256,128]{2,1,0:T(8,128)S(1)}, s32[]{:T(128)}) %tuple.242), condition=%wide.region_7.8_spmd, body=%wide.region_6.7_spmd.sunk | while | flops 201457664 | bytes 3932261 | solution.py:262
  1167.9 61.9 %all-reduce.49.cloned.1.call-done = bf16[1024,2048]{1,0:T(8,128)(2,1)} async-done(((bf16[1024,2048]{1,0:T(8,128)(2,1)}), bf16[1024,2048]{1,0:T(8,128)(2,1)}) %all-reduce.49.cloned.1.call-update) | async-done | bytes 4194320 | tf_op jit(solution)/shard_map/psum | solution.py:266
  1239.9 84.9 %all-gather.21.cloned.1.call-done = bf16[2048,1376]{0,1:T(8,128)(2,1)} async-done(((bf16[256,1376]{0,1:T(8,128)(2,1)}), bf16[2048,1376]{0,1:T(8,128)(2,1)}) %all-gather.21.cloned.1.call-update) | async-done | bytes 5636112 | tf_op jit(solution)/shard_map/all_gather | solution.py:191
  1335.6 82.2 %all-gather.23.cloned.1.call-done = bf16[2048,1376]{0,1:T(8,128)(2,1)} async-done(((bf16[256,1376]{0,1:T(8,128)(2,1)}), bf16[2048,1376]{0,1:T(8,128)(2,1)}) %all-gather.23.cloned.1.call-update) | async-done | bytes 5636112 | tf_op jit(solution)/shard_map/all_gather | solution.py:192
  1428.6 82.2 %all-gather.25.cloned.1.call-done = bf16[1376,2048]{1,0:T(8,128)(2,1)} async-done(((bf16[1376,256]{1,0:T(8,128)(2,1)}), bf16[1376,2048]{1,0:T(8,128)(2,1)}) %all-gather.25.cloned.1.call-update) | async-done | bytes 5636112 | tf_op jit(solution)/shard_map/all_gather | solution.py:193
  1557.5 72.0 %all-reduce.51.cloned.1.call-done = bf16[1024,2048]{1,0:T(8,128)(2,1)} async-done(((bf16[1024,2048]{1,0:T(8,128)(2,1)}), bf16[1024,2048]{1,0:T(8,128)(2,1)}) %all-reduce.51.cloned.1.call-update) | async-done | bytes 4194320 | tf_op jit(solution)/shard_map/psum | solution.py:286
  1681.7 99.4 %while.107 = (s32[]{:T(128)}, f32[4,256,128]{2,1,0:T(8,128)S(1)}, f32[4,128,128]{2,1,0:T(8,128)S(1)}, f32[4,256,128]{2,1,0:T(8,128)S(1)}, s32[]{:T(128)}) while((s32[]{:T(128)}, f32[4,256,128]{2,1,0:T(8,128)S(1)}, f32[4,128,128]{2,1,0:T(8,128)S(1)}, f32[4,256,128]{2,1,0:T(8,128)S(1)}, s32[]{:T(128)}) %tuple.301), condition=%wide.region_16.17_spmd, body=%wide.region_15.16_spmd.sunk | while | flops 201457664 | bytes 3932261 | solution.py:305
  1789.0 869.2 %while.109 = (s32[]{:T(128)}, f32[4,384,128]{2,1,0:T(8,128)S(1)}, f32[16,4,64,128]{3,2,1,0:T(8,128)}, f32[16,4,64,128]{3,2,1,0:T(8,128)}, f32[16,4,64,384]{3,2,0...) while((s32[]{:T(128)}, f32[4,384,128]{2,1,0:T(8,128)S(1)}, ...), condition=%wide.region_28.29_spmd.clone.clone, body=%wide.region_17.28_spmd.clone.clone.sunk | while | flops 1324578048 | bytes 20755108 | solution.py:138
  2891.3 63.2 %reduce-scatter.40.cloned.1.call-done = bf16[256,4]{1,0:T(8,128)(2,1)} async-done(((bf16[2048,4]{1,0:T(8,128)(2,1)}), bf16[256,4]{1,0:T(8,128)(2,1)}) %reduce-scatter.40.cloned.1.call-update) | async-done | bytes 2064
  2956.1 63.5 %reduce-scatter.42.cloned.1.call-done = bf16[256,4]{1,0:T(8,128)(2,1)} async-done(((bf16[2048,4]{1,0:T(8,128)(2,1)}), bf16[256,4]{1,0:T(8,128)(2,1)}) %reduce-scatter.42.cloned.1.call-update) | async-done | bytes 2064
  3021.1 68.5 %reduce-scatter.26.cloned.1.call-done = bf16[256,512]{1,0:T(8,128)(2,1)} async-done(((bf16[2048,512]{1,0:T(8,128)(2,1)}), bf16[256,512]{1,0:T(8,128)(2,1)}) %reduce-scatter.26.cloned.1.call-update) | async-done | bytes 262160 | tf_op jit(solution)/shard_map/reduce_scatter | solution.py:359
  3091.3 152.9 %all-reduce.53.cloned.1.call-done = (bf16[1024,2048]{1,0:T(8,128)(2,1)}, bf16[1024,2048]{1,0:T(8,128)(2,1)}) async-done(((bf16[1024,2048]{1,0:T(8,128)(2,1)}, bf16[1024,2048]{1,0:T(8,128)(2,1)}), (bf16[1024,2048]{1,0:T(8,128)(2,1)}, bf16[1024,2048]{1,0:T(8,128)(2,1)})) %all-reduce.53.cloned.1.call-update) | async-done | bytes 8388624 | tf_op jit(solution)/shard_map/psum | solution.py:277
  3250.2 22.3 all-reduce.41
  3272.8 43.5 %reduce-scatter.24.cloned.1.call-done = bf16[256,512]{1,0:T(8,128)(2,1)} async-done(((bf16[2048,512]{1,0:T(8,128)(2,1)}), bf16[256,512]{1,0:T(8,128)(2,1)}) %reduce-scatter.24.cloned.1.call-update) | async-done | bytes 262160 | tf_op jit(solution)/shard_map/reduce_scatter | solution.py:356
  3343.8 63.5 %reduce-scatter.32.cloned.1.call-done = bf16[1024,256]{1,0:T(8,128)(2,1)} async-done(((bf16[1024,2048]{1,0:T(8,128)(2,1)}), bf16[1024,256]{1,0:T(8,128)(2,1)}) %reduce-scatter.32.cloned.1.call-update) | async-done | bytes 524304 | tf_op jit(solution)/shard_map/reduce_scatter | solution.py:392
  3409.5 89.5 %reduce-scatter.30.cloned.1.call-done = bf16[256,1024]{1,0:T(8,128)(2,1)} async-done(((bf16[2048,1024]{1,0:T(8,128)(2,1)}), bf16[256,1024]{1,0:T(8,128)(2,1)}) %reduce-scatter.30.cloned.1.call-update) | async-done | bytes 524304 | tf_op jit(solution)/shard_map/reduce_scatter | solution.py:365
  3501.1 89.2 %reduce-scatter.28.cloned.1.call-done = bf16[256,1024]{1,0:T(8,128)(2,1)} async-done(((bf16[2048,1024]{1,0:T(8,128)(2,1)}), bf16[256,1024]{1,0:T(8,128)(2,1)}) %reduce-scatter.28.cloned.1.call-update) | async-done | bytes 524304 | tf_op jit(solution)/shard_map/reduce_scatter | solution.py:362
  3592.5 110.2 %reduce-scatter.34.cloned.1.call-done = bf16[256,1376]{0,1:T(8,128)(2,1)} async-done(((bf16[2048,1376]{0,1:T(8,128)(2,1)}), bf16[256,1376]{0,1:T(8,128)(2,1)}) %reduce-scatter.34.cloned.1.call-update) | async-done | bytes 704528 | tf_op jit(solution)/shard_map/reduce_scatter | solution.py:398
  3705.0 110.1 %reduce-scatter.36.cloned.1.call-done = bf16[256,1376]{0,1:T(8,128)(2,1)} async-done(((bf16[2048,1376]{0,1:T(8,128)(2,1)}), bf16[256,1376]{0,1:T(8,128)(2,1)}) %reduce-scatter.36.cloned.1.call-update) | async-done | bytes 704528 | tf_op jit(solution)/shard_map/reduce_scatter | solution.py:401
  3817.4 109.9 %reduce-scatter.38.cloned.1.call-done = bf16[1376,256]{1,0:T(8,128)(2,1)} async-done(((bf16[1376,2048]{1,0:T(8,128)(2,1)}), bf16[1376,256]{1,0:T(8,128)(2,1)}) %reduce-scatter.38.cloned.1.call-update) | async-done | bytes 704528 | tf_op jit(solution)/shard_map/reduce_scatter | solution.py:404
  (1600 shorter events, 2270.1 us)
Async XLA Ops:
  7.2 214.7 %all-gather.11.cloned.1.call-start = ((), (), s32[]{:S(2)}) async-start(), calls=%async_computation.13 | async-start | bytes 2359296 | tf_op jit(solution)/shard_map/all_gather | solution.py:178
  9.2 219.3 %all-gather.15.cloned.1.call-start = ((), (), s32[]{:S(2)}) async-start(), calls=%async_computation.15 | async-start | bytes 2359296 | tf_op jit(solution)/shard_map/all_gather | solution.py:177
  11.0 252.9 %all-gather.13.cloned.1.call-start = ((), (), s32[]{:S(2)}) async-start(), calls=%async_computation.14 | async-start | bytes 4718592 | tf_op jit(solution)/shard_map/all_gather | solution.py:179
  13.2 271.4 %all-gather.17.cloned.1.call-start = ((), (), s32[]{:S(2)}) async-start(), calls=%async_computation.16 | async-start | bytes 4718592 | tf_op jit(solution)/shard_map/all_gather | solution.py:180
  14.3 1118.7 %all-gather.19.cloned.1.call-start = ((), (), s32[]{:S(2)}) async-start(), calls=%async_computation.17 | async-start | bytes 4718592 | tf_op jit(solution)/shard_map/all_gather | solution.py:189
  15.2 1214.6 %all-reduce.49.cloned.1.call-start = ((), (), s32[]{:S(2)}) async-start(), calls=%async_computation.18 | async-start | bytes 8388608 | tf_op jit(solution)/shard_map/psum | solution.py:266
  273.3 23.2 collective-permute-start.3
  1039.3 19.8 collective-permute-start
  1059.8 16.7 collective-permute-start
  1077.1 15.8 collective-permute-start
  1142.4 182.3 %all-gather.21.cloned.1.call-start = ((), (), s32[]{:S(2)}) async-start(), calls=%async_computation.19 | async-start | bytes 6340608 | tf_op jit(solution)/shard_map/all_gather | solution.py:191
  1144.7 273.1 %all-gather.23.cloned.1.call-start = ((), (), s32[]{:S(2)}) async-start(), calls=%async_computation.20 | async-start | bytes 6340608 | tf_op jit(solution)/shard_map/all_gather | solution.py:192
  1147.1 363.7 %all-gather.25.cloned.1.call-start = ((), (), s32[]{:S(2)}) async-start(), calls=%async_computation.21 | async-start | bytes 6340608 | tf_op jit(solution)/shard_map/all_gather | solution.py:193
  1148.1 481.4 %all-reduce.51.cloned.1.call-start = ((), (), s32[]{:S(2)}) async-start(), calls=%async_computation.22 | async-start | bytes 8388608 | tf_op jit(solution)/shard_map/psum | solution.py:286
  1545.7 1330.2 %reduce-scatter.46.cloned.1.call-start = ((), (), s32[]{:S(2)}) async-start(), calls=%async_computation.34 | async-start | bytes 36864
  1682.4 15.4 collective-permute-start.1
  1698.4 15.1 collective-permute-start.1
  2693.1 59.6 %collective-permute-start.6 = (f32[3,512]{1,0:T(4,128)S(1)}, f32[3,512]{1,0:T(4,128)S(1)}, u32[]{:S(2)}, u32[]{:S(2)}) collective-permute-start(f32[3,512]{1,0:T(4,128)S(1)} %pad_add_fusion.5), channel_id=1, source_target_pairs={{4,0},{8,4},{12,8},{16,12},{20,16},{24,20},{28,24},{5,1},{9,5},{13... | collective-permute-start | bytes 18440 | tf_op jit(solution)/shard_map/ppermute | solution.py:16
  2711.1 166.3 %reduce-scatter.44.cloned.1.call-start = ((), (), s32[]{:S(2)}) async-start(), calls=%async_computation.33 | async-start | bytes 36864
  2720.0 169.8 %reduce-scatter.48.cloned.1.call-start = ((), (), s32[]{:S(2)}) async-start(), calls=%async_computation.35 | async-start | bytes 73728
  2721.1 233.4 %reduce-scatter.40.cloned.1.call-start = ((), (), s32[]{:S(2)}) async-start(), calls=%async_computation.31 | async-start | bytes 589824
  2728.1 291.4 %reduce-scatter.42.cloned.1.call-start = ((), (), s32[]{:S(2)}) async-start(), calls=%async_computation.32 | async-start | bytes 589824
  2752.7 336.8 %reduce-scatter.26.cloned.1.call-start = ((), (), s32[]{:S(2)}) async-start(), calls=%async_computation.24 | async-start | bytes 2359296 | tf_op jit(solution)/shard_map/reduce_scatter | solution.py:359
  2759.4 484.9 %all-reduce.53.cloned.1.call-start = ((), (), s32[]{:S(2)}) async-start(), calls=%async_computation.36 | async-start | bytes 16777216 | tf_op jit(solution)/shard_map/psum | solution.py:277
  2760.2 19.4 collective-permute-start.7
  2798.5 517.8 %reduce-scatter.24.cloned.1.call-start = ((), (), s32[]{:S(2)}) async-start(), calls=%async_computation.23 | async-start | bytes 2359296 | tf_op jit(solution)/shard_map/reduce_scatter | solution.py:356
  2804.5 602.9 %reduce-scatter.32.cloned.1.call-start = ((), (), s32[]{:S(2)}) async-start(), calls=%async_computation.27 | async-start | bytes 4718592 | tf_op jit(solution)/shard_map/reduce_scatter | solution.py:392
  2818.2 680.8 %reduce-scatter.30.cloned.1.call-start = ((), (), s32[]{:S(2)}) async-start(), calls=%async_computation.26 | async-start | bytes 4718592 | tf_op jit(solution)/shard_map/reduce_scatter | solution.py:365
  2828.1 762.3 %reduce-scatter.28.cloned.1.call-start = ((), (), s32[]{:S(2)}) async-start(), calls=%async_computation.25 | async-start | bytes 4718592 | tf_op jit(solution)/shard_map/reduce_scatter | solution.py:362
  2838.3 864.4 %reduce-scatter.34.cloned.1.call-start = ((), (), s32[]{:S(2)}) async-start(), calls=%async_computation.28 | async-start | bytes 6340608 | tf_op jit(solution)/shard_map/reduce_scatter | solution.py:398
  2850.0 965.1 %reduce-scatter.36.cloned.1.call-start = ((), (), s32[]{:S(2)}) async-start(), calls=%async_computation.29 | async-start | bytes 6340608 | tf_op jit(solution)/shard_map/reduce_scatter | solution.py:401
  2861.7 1065.6 %reduce-scatter.38.cloned.1.call-start = ((), (), s32[]{:S(2)}) async-start(), calls=%async_computation.30 | async-start | bytes 6340608 | tf_op jit(solution)/shard_map/reduce_scatter | solution.py:404
  (144 other events, 7462.0 us)
Sparse Core Ops, SparseCore 0:
  10.7 53.5 all-gather.10
  67.1 48.6 all-gather.14
  118.5 74.8 all-gather.12
  195.9 72.4 all-gather.16
  270.9 74.3 all-gather.18
  1142.5 87.2 all-reduce.48
  1232.6 92.1 all-gather.20
  1327.6 90.1 all-gather.22
  1420.6 90.1 all-gather.24
  1545.8 83.6 all-reduce.50
  2711.2 57.9 reduce-scatter.45
  2772.8 52.5 reduce-scatter.43
  2829.4 60.3 reduce-scatter.47
  2893.5 60.9 reduce-scatter.39
  2958.7 60.8 reduce-scatter.41
  3022.9 66.5 reduce-scatter.25
  3092.0 152.2 all-reduce.52
  3248.2 67.9 reduce-scatter.23
  3319.9 87.4 reduce-scatter.31
  3411.3 87.6 reduce-scatter.29
  3502.7 87.6 reduce-scatter.27
  3594.5 108.1 reduce-scatter.33
  3706.8 108.2 reduce-scatter.35
  3819.0 108.2 reduce-scatter.37
where the time goes:
time: 3960 us; the launch traced here: 3940 us
  waiting for transfers between devices  1510 us (38%)
  other arithmetic  973 us (25%)
  matrix products  942 us (24%)
  blocking collectives  234 us (6%)
  local copies, waits for them, and re-layouts  187 us (5%)
  starting transfers between devices  67.4 us (2%)
    another operation x144, other arithmetic, block_step(): jax.scipy.linalg.solve_triangular(coupling, right_side, lower=True, unit_...  681 us
    psum x1, waiting for transfers between devices, on_device(): lax.psum(branch_part.astype(jnp.bfloat16), 'head').astype(jnp.float32)  153 us
    ppermute x20, waiting for transfers between devices, passed_along(): return lax.ppermute(block, axis, route)  151 us
    unnamed x29, waiting for transfers between devices  138 us
    dot_general x48, matrix products, block_step(): from_state = jnp.einsum('hck,hrk->hcr', k_blk, state_now, precision=highest)  130 us
    dot_general x48, matrix products, block_step(): jnp.einsum('hck,hrk->hcr', q_blk, state_now, precision=highest)  114 us
    reduce_scatter x1, waiting for transfers between devices, on_device(): lax.psum_scatter(grad_mlp_gate.astype(jnp.bfloat16), 'seq', scatter_dimen...  110 us
    reduce_scatter x1, waiting for transfers between devices, on_device(): lax.psum_scatter(grad_mlp_up.astype(jnp.bfloat16), 'seq', scatter_dimensi...  110 us
  transfers between devices with their start and end apart: 44, of which 31 were waited for; matrix products, arithmetic and copies ran while one was open for 27% of the time, Pallas kernels for 0%

commit v1 on v0

v1 whole, which is shorter than its diff:
```python
import functools
import jax
import jax.numpy as jnp
from jax import lax
from jax.experimental import pallas as pl
from jax.experimental.pallas import tpu as pltpu

ROWS = 128
KEY = 128
VAL = 256
HALO = 16
eps_norm = 1e-06
f32 = jnp.float32
bf16 = jnp.bfloat16


def mm(a, b):
    return lax.dot_general(
        a.astype(bf16), b.astype(bf16), (((1,), (0,)), ((), ())), preferred_element_type=f32
    )


def mm_nt(a, b):
    return lax.dot_general(
        a.astype(bf16), b.astype(bf16), (((1,), (1,)), ((), ())), preferred_element_type=f32
    )


def mm_tn(a, b):
    return lax.dot_general(
        a.astype(bf16), b.astype(bf16), (((0,), (0,)), ((), ())), preferred_element_type=f32
    )


def mm_full(a, b):
    return lax.dot_general(
        a, b, (((1,), (0,)), ((), ())), precision=lax.Precision.HIGHEST, preferred_element_type=f32
    )


def sigmoid(x):
    return 1.0 / (1.0 + jnp.exp(-x))


def softplus(x):
    return jnp.maximum(x, 0.0) + jnp.log(1.0 + jnp.exp(-jnp.abs(x)))


def positions():
    rows = lax.broadcasted_iota(jnp.int32, (ROWS, ROWS), 0)
    cols = lax.broadcasted_iota(jnp.int32, (ROWS, ROWS), 1)
    return rows, cols


def decay_terms(heads, ab, par):
    rows, cols = positions()
    log_decay = -par[0:1, :] * softplus(ab + par[1:2, :])
    running = mm_full((rows >= cols).astype(f32), log_decay)
    return log_decay, running, running.T, sigmoid(ab)


def ratio_of(running, running_rows, h, rows, cols):
    gap = running[:, h : h + 1] - running_rows[h : h + 1, :]
    return jnp.where(rows >= cols, jnp.exp(jnp.where(rows >= cols, gap, 0.0)), 0.0)


def conv_at(xs_ref, taps_ref, lo, width):
    total = taps_ref[0:1, lo : lo + width] * xs_ref[HALO - 3 : HALO - 3 + ROWS, lo : lo + width]
    for i in range(1, 4):
        total = total + taps_ref[i : i + 1, lo : lo + width] * (
            xs_ref[HALO - 3 + i : HALO - 3 + i + ROWS, lo : lo + width]
        )
    return total


def forward_kernel(heads, proj_ref, edge_ref, taps_ref, ab_ref, par_ref,
                   value_ref, ident_ref, inv_ref, state_ref, final_ref, xs_ref, s_ref):
    step = pl.program_id(0)
    keys = heads * KEY

    @pl.when(step == 0)
    def _():
        xs_ref[0:HALO, :] = edge_ref[...].astype(f32)
        r, c = positions()
        for h in range(heads):
            s_ref[h, :, 0:VAL] = jnp.zeros((KEY, VAL), f32)
            s_ref[h, :, VAL:] = (r == c).astype(f32)

    @pl.when(step > 0)
    def _():
        xs_ref[0:HALO, :] = xs_ref[ROWS : ROWS + HALO, :]

    xs_ref[HALO : HALO + ROWS, :] = proj_ref[...].astype(f32)
    rows, cols = positions()
    log_decay, running, running_rows, strength = decay_terms(heads, ab_ref[...], par_ref[...])
    every = range(heads)
    q, k, v, ratio, a, p, t, beta, grow = [], [], [], [], [], [], [], [], []
    for h in every:
        u = conv_at(xs_ref, taps_ref, h * KEY, KEY)
        u = u * sigmoid(u)
        q.append(u * (lax.rsqrt(jnp.sum(u * u, axis=1, keepdims=True) + eps_norm) * KEY**-0.5))
        w = conv_at(xs_ref, taps_ref, keys + h * KEY, KEY)
        w = w * sigmoid(w)
        k.append(w * lax.rsqrt(jnp.sum(w * w, axis=1, keepdims=True) + eps_norm))
        x = conv_at(xs_ref, taps_ref, 2 * keys + h * VAL, VAL)
        v.append(x * sigmoid(x))
        beta.append(strength[:, heads + h : heads + h + 1])
        grow.append(jnp.exp(running[:, h : h + 1]))
    for h in every:
        ratio.append(ratio_of(running, running_rows, h, rows, cols))
        gram = mm_nt(k[h], k[h])
        a.append(jnp.where(rows > cols, ratio[h] * gram, 0.0) * beta[h])
        p.append(ratio[h] * mm_nt(q[h], k[h]))
    for h in every:
        first = (rows // 2 == cols // 2) & (rows > cols)
        t.append((rows == cols).astype(f32) - jnp.where(first, a[h], 0.0))
    b = 2
    while b < ROWS:
        low = (rows // (2 * b) == cols // (2 * b)) & ((rows // b) % 2 == 1) & ((cols // b) % 2 == 0)
        inner = [mm(jnp.where(low, a[h], 0.0), t[h]) for h in every]
        t = [t[h] - mm(t[h], inner[h]) for h in every]
        b *= 2
    uw = [
        mm(t[h], jnp.concatenate([beta[h] * v[h], (beta[h] * grow[h]) * k[h]], axis=1))
        for h in every
    ]
    for h in every:
        inv_ref[:, h * KEY : (h + 1) * KEY] = t[h].astype(bf16)
        state_ref[h] = s_ref[h].astype(bf16)
    for h in every:
        state = s_ref[h]
        pred = mm(uw[h][:, VAL:], state)
        err = jnp.concatenate([uw[h][:, :VAL] - pred[:, :VAL], -pred[:, VAL:]], axis=1)
        out = grow[h] * mm(q[h], state) + mm(p[h], err)
        value_ref[:, h * VAL : (h + 1) * VAL] = out[:, :VAL]
        ident_ref[:, h * KEY : (h + 1) * KEY] = out[:, VAL:].astype(bf16)
        end = running[ROWS - 1 : ROWS, h : h + 1]
        tail = jnp.exp(end - running[:, h : h + 1]) * k[h]
        s_ref[h] = jnp.exp(end) * state + mm_tn(tail, err)

    @pl.when(step == pl.num_programs(0) - 1)
    def _():
        final_ref[...] = s_ref[...]


def delta_forward(proj, edge, taps, ab, par):
    tokens = proj.shape[0]
    heads = proj.shape[1] // (2 * KEY + VAL)
    keys, vals = heads * KEY, heads * VAL
    blocks = tokens // ROWS
    width = proj.shape[1]
    whole = lambda *shape: pl.BlockSpec(shape, lambda c: (0,) * len(shape))
    return pl.pallas_call(
        functools.partial(forward_kernel, heads),
        grid=(blocks,),
        in_specs=[
            pl.BlockSpec((ROWS, width), lambda c: (c, 0)),
            whole(HALO, width),
            whole(8, width),
            pl.BlockSpec((ROWS, 128), lambda c: (c, 0)),
            whole(8, 128),
        ],
        out_specs=[
            pl.BlockSpec((ROWS, vals), lambda c: (c, 0)),
            pl.BlockSpec((ROWS, keys), lambda c: (c, 0)),
            pl.BlockSpec((ROWS, keys), lambda c: (c, 0)),
            pl.BlockSpec((None, heads, KEY, VAL + KEY), lambda c: (c, 0, 0, 0)),
            whole(heads, KEY, VAL + KEY),
        ],
        out_shape=[
            jax.ShapeDtypeStruct((tokens, vals), f32),
            jax.ShapeDtypeStruct((tokens, keys), bf16),
            jax.ShapeDtypeStruct((tokens, keys), bf16),
            jax.ShapeDtypeStruct((blocks, heads, KEY, VAL + KEY), bf16),
            jax.ShapeDtypeStruct((heads, KEY, VAL + KEY), f32),
        ],
        scratch_shapes=[
            pltpu.VMEM((HALO + ROWS, width), f32),
            pltpu.VMEM((heads, KEY, VAL + KEY), f32),
        ],
        compiler_params=pltpu.CompilerParams(
            dimension_semantics=("arbitrary",), vmem_limit_bytes=48 * 2**20
        ),
    )(proj, edge, taps, ab, par)


def output_kernel(heads, value_ref, ident_ref, state_ref, gate_ref, gain_ref, out_ref, gated_ref):
    for h in range(heads):
        span = slice(h * VAL, (h + 1) * VAL)
        out = value_ref[:, span] + mm(ident_ref[:, h * KEY : (h + 1) * KEY], state_ref[h])
        out_ref[:, span] = out
        gate = gate_ref[:, span]
        unit = out * lax.rsqrt(jnp.mean(out * out, axis=1, keepdims=True) + eps_norm)
        gated_ref[:, span] = (unit * gain_ref[0:1, :] * (gate * sigmoid(gate))).astype(bf16)


def gated_outputs(value_out, ident, state_in, gate_pre, gain):
    tokens, vals = value_out.shape
    heads = vals // VAL
    rows = 256
    by_rows = lambda width: pl.BlockSpec((rows, width), lambda c: (c, 0))
    return pl.pallas_call(
        functools.partial(output_kernel, heads),
        grid=(tokens // rows,),
        in_specs=[
            by_rows(vals),
            by_rows(heads * KEY),
            pl.BlockSpec((heads, KEY, VAL), lambda c: (0, 0, 0)),
            by_rows(vals),
            pl.BlockSpec((1, VAL), lambda c: (0, 0)),
        ],
        out_specs=[by_rows(vals), by_rows(vals)],
        out_shape=[
            jax.ShapeDtypeStruct((tokens, vals), f32),
            jax.ShapeDtypeStruct((tokens, vals), bf16),
        ],
        compiler_params=pltpu.CompilerParams(
            dimension_semantics=("arbitrary",), vmem_limit_bytes=48 * 2**20
        ),
    )(value_out, ident, state_in, gate_pre, gain)


def gate_back_kernel(heads, grad_ref, out_ref, gate_ref, gain_ref, ident_ref,
                     dout_ref, dgate_ref, dgain_ref, pull_ref):
    @pl.when(pl.program_id(0) == 0)
    def _():
        dgain_ref[...] = jnp.zeros_like(dgain_ref)
        pull_ref[...] = jnp.zeros_like(pull_ref)

    gain = gain_ref[0:1, :]
    for h in range(heads):
        span = slice(h * VAL, (h + 1) * VAL)
        grad, out, gate = grad_ref[:, span], out_ref[:, span], gate_ref[:, span]
        scale = lax.rsqrt(jnp.mean(out * out, axis=1, keepdims=True) + eps_norm)
        unit = out * scale
        sig = sigmoid(gate)
        m = grad * (gate * sig)
        mn = m * unit
        dgain_ref[...] += jnp.sum(mn.reshape(-1, 8, VAL), axis=0)
        mean = jnp.mean(mn * gain, axis=1, keepdims=True)
        dout = (scale * (m * gain - unit * mean)).astype(bf16)
        dout_ref[:, span] = dout
        dgate_ref[:, span] = (
            grad * unit * gain * (sig * (1.0 + gate * (1.0 - sig)))
        ).astype(bf16)
        pull_ref[h] += mm_tn(ident_ref[:, h * KEY : (h + 1) * KEY], dout)


def gate_backward(grad_gated, outputs, gate_pre, gain, ident):
    tokens, vals = outputs.shape
    heads = vals // VAL
    rows = 256
    by_rows = lambda width: pl.BlockSpec((rows, width), lambda c: (c, 0))
    return pl.pallas_call(
        functools.partial(gate_back_kernel, heads),
        grid=(tokens // rows,),
        in_specs=[
            by_rows(vals),
            by_rows(vals),
            by_rows(vals),
            pl.BlockSpec((1, VAL), lambda c: (0, 0)),
            by_rows(heads * KEY),
        ],
        out_specs=[
            by_rows(vals),
            by_rows(vals),
            pl.BlockSpec((8, VAL), lambda c: (0, 0)),
            pl.BlockSpec((heads, KEY, VAL), lambda c: (0, 0, 0)),
        ],
        out_shape=[
            jax.ShapeDtypeStruct((tokens, vals), bf16),
            jax.ShapeDtypeStruct((tokens, vals), bf16),
            jax.ShapeDtypeStruct((8, VAL), f32),
            jax.ShapeDtypeStruct((heads, KEY, VAL), f32),
        ],
        compiler_params=pltpu.CompilerParams(
            dimension_semantics=("arbitrary",), vmem_limit_bytes=48 * 2**20
        ),
    )(grad_gated, outputs, gate_pre, gain, ident)


def backward_kernel(heads, proj_ref, before_ref, edge_ref, taps_ref, ab_ref, par_ref, dout_ref,
                    inv_ref, state_ref, enter_ref, dfinal_ref,
                    dproj_ref, dab_ref, dtaps_ref, dpar_ref, dhead_ref,
                    xs_ref, gs_ref, ds_ref):
    step = pl.program_id(0)
    last = pl.num_programs(0) - 1
    keys = heads * KEY
    width = 2 * keys + heads * VAL

    @pl.when(step == 0)
    def _():
        ds_ref[...] = dfinal_ref[...]
        dtaps_ref[...] = jnp.zeros_like(dtaps_ref)
        dpar_ref[...] = jnp.zeros_like(dpar_ref)
        gs_ref[ROWS : ROWS + 8, :] = jnp.zeros((8, width), f32)

    @pl.when(step > 0)
    def _():
        gs_ref[ROWS : ROWS + 8, :] = gs_ref[0:8, :]

    @pl.when(step == last)
    def _():
        xs_ref[0:HALO, :] = edge_ref[...].astype(f32)

    @pl.when(step < last)
    def _():
        xs_ref[0:HALO, :] = before_ref[...].astype(f32)

    xs_ref[HALO : HALO + ROWS, :] = proj_ref[...].astype(f32)
    rows, cols = positions()
    ab, par = ab_ref[...], par_ref[...]
    log_decay, running, running_rows, strength = decay_terms(heads, ab, par)
    lane = lax.broadcasted_iota(jnp.int32, (ROWS, 128), 1)
    row_at = lax.broadcasted_iota(jnp.int32, (ROWS, 1), 0)
    drunning = jnp.zeros((ROWS, 128), f32)
    dbeta = jnp.zeros((ROWS, 128), f32)

    for h in range(heads):
        qs, ks, vs = h * KEY, keys + h * KEY, 2 * keys + h * VAL
        u = conv_at(xs_ref, taps_ref, qs, KEY)
        su = sigmoid(u)
        wu = u * su
        ru = lax.rsqrt(jnp.sum(wu * wu, axis=1, keepdims=True) + eps_norm)
        q = wu * (ru * KEY**-0.5)
        y = conv_at(xs_ref, taps_ref, ks, KEY)
        sy = sigmoid(y)
        wy = y * sy
        ry = lax.rsqrt(jnp.sum(wy * wy, axis=1, keepdims=True) + eps_norm)
        k = wy * ry
        x = conv_at(xs_ref, taps_ref, vs, VAL)
        sx = sigmoid(x)
        v = x * sx
        qb, kb = q.astype(bf16), k.astype(bf16)
        beta = strength[:, heads + h : heads + h + 1]
        at = running[:, h : h + 1]
        grow = jnp.exp(at)
        end = running[ROWS - 1 : ROWS, h : h + 1]
        tail = jnp.exp(end - at)
        ratio = ratio_of(running, running_rows, h, rows, cols)
        p = ratio * mm_nt(qb, kb)
        t = inv_ref[:, h * KEY : (h + 1) * KEY]
        dout = dout_ref[:, h * VAL : (h + 1) * VAL]
        state = state_ref[h, :, :VAL].astype(f32) + mm(state_ref[h, :, VAL:], enter_ref[h])
        state_b = state.astype(bf16)
        dstate = ds_ref[h]
        dstate_b = dstate.astype(bf16)
        err = mm(t, beta * (v - grow * mm(kb, state_b)))
        err_b = err.astype(bf16)
        derr = mm_tn(p, dout) + mm(tail * k, dstate_b)
        dright = mm_tn(t, derr)
        dright_b = dright.astype(bf16)
        dp = mm_nt(dout, err_b) * ratio
        dp_b = dp.astype(bf16)
        da = jnp.where(rows > cols, mm_nt(dright_b, err_b) * ratio, 0.0) * (-beta)
        da_b = da.astype(bf16)
        back = (beta * grow) * dright
        back_b = back.astype(bf16)
        dq = grow * mm_nt(dout, state_b) + mm(dp_b, kb)
        dk_read = mm(da_b, kb) - mm_nt(back_b, state_b)
        dk_tail = tail * mm_nt(err_b, dstate_b)
        dk_write = mm_tn(dp_b, qb) + mm_tn(da_b, kb) + dk_tail
        dk = dk_read + dk_write
        dv = beta * dright
        to_beta = (1.0 - beta) * jnp.sum(dright * err, axis=1, keepdims=True)
        to_decay = jnp.sum(q * dq + k * (dk_read - dk_write), axis=1, keepdims=True)
        at_end = jnp.exp(end) * jnp.sum(
            jnp.sum(state * dstate, axis=1, keepdims=True), axis=0, keepdims=True
        ) + jnp.sum(jnp.sum(k * dk_tail, axis=1, keepdims=True), axis=0, keepdims=True)
        to_decay = to_decay + jnp.where(row_at == ROWS - 1, at_end, 0.0)
        drunning = jnp.where(lane == h, to_decay, drunning)
        dbeta = jnp.where(lane == heads + h, to_beta, dbeta)
        ds_ref[h] = jnp.exp(end) * dstate + mm_tn(grow * q, dout) - mm_tn(kb, back_b)
        along = jnp.sum(wu * dq, axis=1, keepdims=True)
        du = (KEY**-0.5) * (ru * dq - wu * (ru * ru * ru * along))
        gs_ref[0:ROWS, qs : qs + KEY] = du * (su * (1.0 + u * (1.0 - su)))
        along = jnp.sum(wy * dk, axis=1, keepdims=True)
        dy = ry * dk - wy * (ry * ry * ry * along)
        gs_ref[0:ROWS, ks : ks + KEY] = dy * (sy * (1.0 + y * (1.0 - sy)))
        gs_ref[0:ROWS, vs : vs + VAL] = dv * (sx * (1.0 + x * (1.0 - sx)))

    for lo in range(0, width, 256):
        span = slice(lo, lo + 256)
        grad = gs_ref[0:ROWS, span]
        total = taps_ref[3:4, span] * grad
        for i in range(4):
            moved = xs_ref[HALO - 3 + i : HALO - 3 + i + ROWS, span] * grad
            dtaps_ref[8 * i : 8 * i + 8, span] += jnp.sum(moved.reshape(-1, 8, 256), axis=0)
            if i < 3:
                total = total + taps_ref[i : i + 1, span] * gs_ref[3 - i : 3 - i + ROWS, span]
        dproj_ref[:, span] = total.astype(bf16)

    dlog = mm_full((rows <= cols).astype(f32), drunning)
    dalpha = -dlog * par[0:1, :] * sigmoid(ab + par[1:2, :])
    dab_ref[...] = jnp.where(lane < heads, dalpha, dbeta).astype(bf16)
    dpar_ref[0:8, :] += jnp.sum((dlog * log_decay).reshape(-1, 8, 128), axis=0)
    dpar_ref[8:16, :] += jnp.sum(dalpha.reshape(-1, 8, 128), axis=0)

    @pl.when(step == last)
    def _():
        dhead_ref[...] = gs_ref[0:8, :]


def delta_backward(proj, edge, taps, ab, par, dout, inverse, states, entering, dfinal):
    tokens, width = proj.shape
    heads = width // (2 * KEY + VAL)
    keys, vals = heads * KEY, heads * VAL
    blocks = tokens // ROWS
    whole = lambda *shape: pl.BlockSpec(shape, lambda c: (0,) * len(shape))
    rev = lambda w: pl.BlockSpec((ROWS, w), lambda c: (blocks - 1 - c, 0))
    per = ROWS // HALO
    return pl.pallas_call(
        functools.partial(backward_kernel, heads),
        grid=(blocks,),
        in_specs=[
            rev(width),
            pl.BlockSpec((HALO, width), lambda c: (jnp.maximum((blocks - 1 - c) * per - 1, 0), 0)),
            whole(HALO, width),
            whole(8, width),
            rev(128),
            whole(8, 128),
            rev(vals),
            rev(keys),
            pl.BlockSpec((None, heads, KEY, VAL + KEY), lambda c: (blocks - 1 - c, 0, 0, 0)),
            whole(heads, KEY, VAL),
            whole(heads, KEY, VAL),
        ],
        out_specs=[
            rev(width),
            rev(128),
            whole(32, width),
            whole(16, 128),
            whole(8, width),
        ],
        out_shape=[
            jax.ShapeDtypeStruct((tokens, width), bf16),
            jax.ShapeDtypeStruct((tokens, 128), bf16),
            jax.ShapeDtypeStruct((32, width), f32),
            jax.ShapeDtypeStruct((16, 128), f32),
            jax.ShapeDtypeStruct((8, width), f32),
        ],
        scratch_shapes=[
            pltpu.VMEM((HALO + ROWS, width), f32),
            pltpu.VMEM((ROWS + 8, width), f32),
            pltpu.VMEM((heads, KEY, VAL), f32),
        ],
        compiler_params=pltpu.CompilerParams(
            dimension_semantics=("arbitrary",), vmem_limit_bytes=56 * 2**20
        ),
    )(proj, proj, edge, taps, ab, par, dout, inverse, states, entering, dfinal)


def dot_rows(a, b):
    return lax.dot_general(a, b, (((1,), (0,)), ((), ())), preferred_element_type=f32)


def dot_left(a, b):
    return lax.dot_general(a, b, (((0,), (0,)), ((), ())), preferred_element_type=f32)


def dot_right(a, b):
    return lax.dot_general(a, b, (((1,), (1,)), ((), ())), preferred_element_type=f32)


def head_sum(partial):
    if lax.axis_size("head") != 4:
        return lax.psum(partial.astype(bf16), "head").astype(f32)
    core = lax.axis_index("head") % 2
    half = partial.shape[0] // 2
    both = [(0, 1), (1, 0), (2, 3), (3, 2)]
    away = lax.dynamic_slice_in_dim(partial, (1 - core) * half, half).astype(bf16)
    mine = lax.dynamic_slice_in_dim(partial, core * half, half)
    mine = (mine + lax.ppermute(away, "head", both).astype(f32)).astype(bf16)
    across = lax.ppermute(mine, "head", [(0, 2), (2, 0), (1, 3), (3, 1)])
    mine = (mine.astype(f32) + across.astype(f32)).astype(bf16)
    other = lax.ppermute(mine, "head", both)
    top = jnp.where(core == 0, mine, other)
    bottom = jnp.where(core == 0, other, mine)
    return jnp.concatenate([top, bottom], axis=0).astype(f32)


def batched(a, b):
    return lax.dot_general(a, b, (((2,), (1,)), ((0,), (0,))), preferred_element_type=f32)


def batched_t(a, b):
    return lax.dot_general(a, b, (((1,), (1,)), ((0,), (0,))), preferred_element_type=f32)


def group_sizes():
    count = lax.axis_size("seq")
    across = count // 4 if count % 4 == 0 else 1
    return count, across, count // across


def in_group_order(mine):
    count, across, _ = group_sizes()
    place = lax.axis_index("seq") % across
    held = [mine]
    for turn in range(1, across):
        route = [(i - i % across + (i + turn) % across, i) for i in range(count)]
        held.append(lax.ppermute(mine, "seq", route))
    ordered = []
    for j in range(across):
        pick = (j - place) % across
        chosen = held[0]
        for turn in range(1, across):
            chosen = jnp.where(pick == turn, held[turn], chosen)
        ordered.append(chosen)
    return ordered


def states_in(final):
    count, across, groups = group_sizes()
    place = lax.axis_index("seq") % across
    members = in_group_order(final.astype(bf16))
    total = members[0].astype(f32)
    for member in members[1:]:
        total = batched(member[:, :, VAL:], total.astype(bf16))
        total = total + jnp.pad(member[:, :, :VAL].astype(f32), ((0, 0), (0, 0), (0, KEY)))
    bias, move = total[:, :, :VAL], total[:, :, VAL:].astype(bf16)
    onward = [(i, i + across) for i in range(count - across)]
    state = jnp.zeros_like(bias).astype(bf16)
    for hop in range(groups - 1):
        sent = bias if hop == 0 else batched(move, state) + bias
        state = lax.ppermute(sent.astype(bf16), "seq", onward)
    entering = state
    for j in range(across - 1):
        nxt = batched(members[j][:, :, VAL:], state) + members[j][:, :, :VAL].astype(f32)
        state = nxt.astype(bf16)
        entering = jnp.where(place == j + 1, state, entering)
    return entering, [m[:, :, VAL:] for m in members], move


def states_back(local, moves, move):
    count, across, groups = group_sizes()
    place = lax.axis_index("seq") % across
    members = in_group_order(local.astype(bf16))
    total = members[-1].astype(f32)
    for j in range(across - 2, -1, -1):
        total = batched_t(moves[j], total.astype(bf16)) + members[j].astype(f32)
    onward = [(i + across, i) for i in range(count - across)]
    state = jnp.zeros_like(total).astype(bf16)
    for hop in range(groups - 1):
        sent = total if hop == 0 else batched_t(move, state) + total
        state = lax.ppermute(sent.astype(bf16), "seq", onward)
    leaving = state
    for j in range(across - 1, 0, -1):
        state = (batched_t(moves[j], state) + members[j].astype(f32)).astype(bf16)
        leaving = jnp.where(place == j - 1, state, leaving)
    return leaving.astype(f32)


def on_device(
    tokens, cotangent, norm1_gain, w_query, w_key, w_value, w_gate_out, w_alpha, w_beta,
    conv_query, conv_key, conv_value, a_log, dt_bias, out_gain, w_out, norm2_gain, w_gate, w_up, w_down,
):
    shards = lax.axis_size("seq")
    row_count, model = tokens.shape
    heads = w_alpha.shape[1]
    hidden = w_gate.shape[1]
    padded = -(-hidden // 128) * 128
    keys, vals = heads * KEY, heads * VAL
    width = 2 * keys + vals
    head_at = lax.axis_index("head")
    gather = lambda x, axis: lax.all_gather(x, "seq", axis=axis, tiled=True)

    small = [norm1_gain, norm2_gain, w_alpha, w_beta, conv_query, conv_key, conv_value, a_log, dt_bias, out_gain]
    flat = jnp.concatenate([s.astype(bf16).reshape(-1) for s in small])
    used = flat.shape[0]
    flat = jnp.pad(flat, (0, -used % 1024))
    flat = lax.all_gather(flat, "seq", axis=0, tiled=False).astype(f32)
    parts, at = [], 0
    for s in small:
        parts.append(flat[:, at : at + s.size].reshape((shards,) + s.shape))
        at += s.size
    gain_first, gain_second = parts[0].reshape(-1), parts[1].reshape(-1)
    mix_weight = jnp.concatenate([parts[2].reshape(model, heads), parts[3].reshape(model, heads)], axis=1)
    mix_weight = jnp.pad(mix_weight, ((0, 0), (0, 128 - 2 * heads))).astype(bf16)
    taps = jnp.concatenate(
        [jnp.moveaxis(p, 0, 2).reshape(4, -1) for p in parts[4:7]], axis=1
    )
    taps = jnp.pad(taps, ((0, 4), (0, 0)))
    rate = lax.dynamic_slice_in_dim(parts[7].reshape(-1), head_at * heads, heads)
    bias = lax.dynamic_slice_in_dim(parts[8].reshape(-1), head_at * heads, heads)
    gain_out = parts[9].reshape(1, -1)
    par = jnp.pad(jnp.stack([jnp.exp(rate), bias]), ((0, 6), (0, 128 - heads)))

    proj_weight = gather(jnp.concatenate([w_query, w_key, w_value], axis=1).astype(bf16), 0)
    gate_weight = gather(w_gate_out.astype(bf16), 0)
    out_weight = gather(w_out.astype(bf16), 1)
    widen = ((0, 0), (0, padded - hidden))
    mlp_in = gather(jnp.concatenate([jnp.pad(w_gate, widen), jnp.pad(w_up, widen)], axis=1).astype(bf16), 0)
    mlp_down = gather(jnp.pad(w_down, ((0, padded - hidden), (0, 0))).astype(bf16), 1)

    inputs = tokens.astype(f32)
    scale_first = lax.rsqrt(jnp.mean(inputs * inputs, axis=1, keepdims=True) + eps_norm)
    normed_first = (inputs * scale_first * gain_first).astype(bf16)
    proj = dot_rows(normed_first, proj_weight).astype(bf16)
    mix_pre = dot_rows(normed_first, mix_weight)
    forward = [(i, i + 1) for i in range(shards - 1)]
    backward = [(i + 1, i) for i in range(shards - 1)]
    edge = lax.ppermute(proj[row_count - HALO :], "seq", forward)
    value_out, ident, inverse, states, final = delta_forward(proj, edge, taps, mix_pre, par)
    gate_pre = dot_rows(normed_first, gate_weight)
    entering, moves, move = states_in(final)
    outputs, gated = gated_outputs(value_out, ident, entering, gate_pre, gain_out)
    attention = head_sum(dot_rows(gated, out_weight))
    hidden_state = inputs + attention
    scale_second = lax.rsqrt(jnp.mean(hidden_state * hidden_state, axis=1, keepdims=True) + eps_norm)
    hat_second = hidden_state * scale_second
    normed_second = (hat_second * gain_second).astype(bf16)
    grad_mixed = dot_right(cotangent, mlp_down)
    act = dot_rows(normed_second, mlp_in)
    gate_act, up_act = act[:, :padded], act[:, padded:]
    sig = jax.nn.sigmoid(gate_act)
    mixed = (gate_act * sig * up_act).astype(bf16)
    grad_act = jnp.concatenate(
        [grad_mixed * up_act * sig * (1.0 + gate_act * (1.0 - sig)), grad_mixed * (gate_act * sig)], axis=1
    ).astype(bf16)
    partial_second = dot_right(grad_act, mlp_in)
    grad_normed_second = head_sum(partial_second)
    grad_gain_second = jnp.sum(partial_second * hat_second, axis=0)
    scatter = lambda x, axis: lax.psum_scatter(
        x.astype(bf16), "seq", scatter_dimension=axis, tiled=True
    ).astype(f32)
    grad_down = scatter(dot_left(mixed, cotangent), 1)
    grad_in = scatter(dot_left(normed_second, grad_act), 0)
    branch = head_sum(dot_rows(mixed, mlp_down))
    result = (hidden_state + branch).astype(bf16)
    g = grad_normed_second * gain_second
    grad_hidden = cotangent.astype(f32) + scale_second * (
        g - hat_second * jnp.mean(g * hat_second, axis=1, keepdims=True)
    )
    attention_rounded = grad_hidden.astype(bf16)
    grad_gated = dot_right(attention_rounded, out_weight)
    grad_outputs, grad_gate, grad_gain_out, local_pull = gate_backward(
        grad_gated, outputs, gate_pre, gain_out, ident
    )
    grad_out_weight = scatter(dot_left(gated, attention_rounded), 1)
    grad_gate_weight = scatter(dot_left(normed_first, grad_gate), 0)
    leaving = states_back(local_pull, moves, move)
    grad_proj, grad_mix, grad_taps, grad_par, grad_head = delta_backward(
        proj, edge, taps, mix_pre, par, grad_outputs, inverse, states, entering, leaving
    )
    following = lax.ppermute(grad_head, "seq", backward)
    fixes = []
    for s in range(3):
        fixes.append(sum(taps[3 - j] * following[s - 3 + j] for j in range(3 - s, 4)))
    ending = (grad_proj[row_count - HALO :].astype(f32)
              + jnp.pad(jnp.stack(fixes), ((HALO - 3, 0), (0, 0)))).astype(bf16)
    grad_proj = lax.dynamic_update_slice_in_dim(grad_proj, ending, row_count - HALO, 0)
    partial_first = (
        dot_right(grad_proj, proj_weight) + dot_right(grad_gate, gate_weight) + dot_right(grad_mix, mix_weight)
    )
    grad_normed_first = head_sum(partial_first)
    hat_first = inputs * scale_first
    grad_gain_first = jnp.sum(partial_first * hat_first, axis=0)
    grad_mix_weight = dot_left(normed_first, grad_mix)
    taps_sum = jnp.sum(grad_taps.reshape(4, 8, width), axis=1)
    par_sum = jnp.sum(grad_par.reshape(2, 8, 128), axis=1)
    every = jnp.zeros((2, shards * a_log.shape[0]), f32)
    every = lax.dynamic_update_slice(every, par_sum[:, :heads], (0, head_at * heads))

    def by_shard(x, lo, like):
        block = x[:, lo : lo + like.shape[2] * shards * heads].reshape(4, heads, shards, like.shape[2])
        return jnp.moveaxis(block, 2, 0).reshape(shards, -1)

    summed = [
        grad_gain_first.reshape(shards, -1),
        grad_gain_second.reshape(shards, -1),
        every[0].reshape(shards, -1),
        every[1].reshape(shards, -1),
        jnp.sum(grad_gain_out, axis=0).reshape(shards, -1),
        grad_mix_weight[:, :heads].reshape(shards, -1),
        grad_mix_weight[:, heads : 2 * heads].reshape(shards, -1),
        by_shard(taps_sum, 0, conv_query),
        by_shard(taps_sum, keys, conv_key),
        by_shard(taps_sum, 2 * keys, conv_value),
    ]
    packed = jnp.concatenate(summed, axis=1)
    length = packed.shape[1]
    packed = jnp.pad(packed, ((0, 0), (0, -length % 1024)))
    packed = scatter(packed, 0).reshape(-1)
    shared = sum(s.shape[1] for s in summed[:5])
    head_part = lax.psum(packed[:shared].astype(bf16), "head").astype(f32)
    packed = jnp.concatenate([head_part, packed[shared:]])
    pieces, at = [], 0
    for s in summed:
        pieces.append(packed[at : at + s.shape[1]])
        at += s.shape[1]
    grad_proj_weight = scatter(dot_left(normed_first, grad_proj), 0)
    g = grad_normed_first * gain_first
    grad_tokens = grad_hidden + scale_first * (
        g - hat_first * jnp.mean(g * hat_first, axis=1, keepdims=True)
    )
    return (
        result,
        grad_tokens,
        pieces[0],
        grad_proj_weight[:, :keys],
        grad_proj_weight[:, keys : 2 * keys],
        grad_proj_weight[:, 2 * keys :],
        grad_gate_weight,
        pieces[5].reshape(w_alpha.shape),
        pieces[6].reshape(w_beta.shape),
        pieces[7].reshape(conv_query.shape),
        pieces[8].reshape(conv_key.shape),
        pieces[9].reshape(conv_value.shape),
        pieces[2],
        pieces[3],
        pieces[4],
        grad_out_weight,
        pieces[1],
        grad_in[:, :hidden],
        grad_in[:, padded : padded + hidden],
        grad_down[:hidden],
    )


def solution(mesh):
    P = jax.sharding.PartitionSpec
    rows, vector, filters, turned = P("seq", None), P("seq"), P(None, "head", "seq"), P("head", "seq")
    matrix = P("seq", "head")
    in_specs = (rows, rows, vector) + (matrix,) * 6 + (filters,) * 3 + (vector,) * 3 + (
        turned, vector, matrix, matrix, turned)
    out_specs = (rows, rows, vector) + (matrix,) * 6 + (filters,) * 3 + (vector,) * 3 + (
        turned, vector, matrix, matrix, turned)
    return jax.shard_map(
        on_device, mesh=mesh, in_specs=in_specs, out_specs=out_specs, check_vma=False
    )
```

time: 3960 us -> 1560 us (0.39)
  other arithmetic: 973 us -> 84.3 us
  matrix products: 942 us -> 196 us
  waiting for transfers between devices: 1510 us -> 1040 us
  blocking collectives: 234 us -> 40.3 us
  local copies, waits for them, and re-layouts: 187 us -> 49.2 us
  Pallas kernels: 0 us -> 99.1 us
    another operation x207 -> x7, other arithmetic: 705 us -> 3.77 us  [the longest x144 681 us: block_step(): jax.scipy.linalg.solve_triangular(coupling, right_side, lower=True, unit_...]
    dot_general x352 -> x26, matrix products: 858 us -> 196 us  [the longest x6 66.6 us: dot_left(): lax.dot_general(a, b, (((0,), (0,)), ((), ())), preferred_element_type=f32)]
    psum x3 -> x0, waiting for transfers between devices: 287 us -> none  [the longest x1 153 us: on_device(): lax.psum(branch_part.astype(jnp.bfloat16), 'head').astype(jnp.float32)]
    reduce_scatter x8 -> x5, waiting for transfers between devices: 684 us -> 507 us  [on_device(): lax.psum_scatter(x.astype(bf16), 'seq', scatter_dimension=axis, tiled=True)]
    all_gather x7 -> x1, blocking collectives: 188 us -> 32.9 us  [on_device(): flat = lax.all_gather(flat, 'seq', axis=0, tiled=False).astype(f32)]
    unnamed x29 -> x12, waiting for transfers between devices: 138 us -> 0.18 us
    pallas_call x0 -> x4, Pallas kernels: none -> 99.1 us  [the longest x1 50.5 us: delta_backward(): pl.pallas_call(functools.partial(backward_kernel, heads), grid=(blocks,),...]
    ppermute x20 -> x22, waiting for transfers between devices: 151 us -> 243 us  [the longest x4 177 us: head_sum(): across = lax.ppermute(mine, 'head', [(0, 2), (2, 0), (1, 3), (3, 1)])]
  transfers between devices with their start and end apart: 44 -> 33, of which waited for: 31 -> 25; matrix products, arithmetic and copies ran while one was open for 27% -> 15% of each run, Pallas kernels for 0% -> 6%
where the time goes in v1:
time: 1560 us; the launch traced here: 1550 us
  waiting for transfers between devices  1040 us (67%)
  matrix products  196 us (13%)
  Pallas kernels  99.1 us (6%)
  other arithmetic  84.3 us (5%)
  local copies, waits for them, and re-layouts  49.2 us (3%)
  blocking collectives  40.3 us (3%)
  starting transfers between devices  31.8 us (2%)
  between operations  15.8 us (1%)
    reduce_scatter x5, waiting for transfers between devices, on_device(): lax.psum_scatter(x.astype(bf16), 'seq', scatter_dimension=axis, tiled=True)  507 us
    all_gather x5, waiting for transfers between devices, on_device(): gather = lambda x, axis: lax.all_gather(x, 'seq', axis=axis, tiled=True)  288 us
    ppermute x4, waiting for transfers between devices, head_sum(): across = lax.ppermute(mine, 'head', [(0, 2), (2, 0), (1, 3), (3, 1)])  177 us
    dot_general x6, matrix products, dot_left(): lax.dot_general(a, b, (((0,), (0,)), ((), ())), preferred_element_type=f32)  66.6 us
    dot_general x6, matrix products, dot_right(): lax.dot_general(a, b, (((1,), (1,)), ((), ())), preferred_element_type=f32)  62.6 us
    dot_general x6, matrix products, dot_rows(): lax.dot_general(a, b, (((1,), (0,)), ((), ())), preferred_element_type=f32)  60.2 us
    pallas_call x1, Pallas kernels, delta_backward(): pl.pallas_call(functools.partial(backward_kernel, heads), grid=(blocks,),...  50.5 us
    pallas_call x1, Pallas kernels, delta_forward(): pl.pallas_call(functools.partial(forward_kernel, heads), grid=(blocks,),...  34.4 us
  transfers between devices with their start and end apart: 33, of which 25 were waited for; matrix products, arithmetic and copies ran while one was open for 15% of the time, Pallas kernels for 6%

profile of v1, /device:TPU:0, one launch (start us, length us, event | category | flops | bytes accessed | tf_op | source)
XLA Modules:
  0.0 1553.4 jit_solution(1401917222695931263)
XLA Ops:
  19.1 32.9 %all-gather = bf16[32768]{0:T(1024)(128)(2,1)S(1)} all-gather(bf16[4096]{0:T(1024)(128)(2,1)S(1)} %pad.47), channel_id=2, replica_groups=mesh['seq'=8,'head'=4] {'seq'}, dimensions={0}, use_global_device_ids=true | all-gather | bytes 73728 | tf_op jit(solution)/shard_map/all_gather | solution.py:572
  60.6 79.6 %all-gather.7.cloned.1.call-done = bf16[2048,2048]{1,0:T(8,128)(2,1)} async-done(((bf16[256,2048]{1,0:T(8,128)(2,1)}), bf16[2048,2048]{1,0:T(8,128)(2,1)}) %all-gather.7.cloned.1.call-update) | async-done | bytes 8388624 | tf_op jit(solution)/shard_map/all_gather | solution.py:566
  140.3 12.6 convolution_convert_fusion.3.proj_ref.before_ref
  157.4 34.4 %shard_map.347 = (f32[1024,1024]{1,0:T(8,128)}, bf16[1024,512]{1,0:T(8,128)(2,1)S(1)}, bf16[1024,512]{1,0:T(8,128)(2,1)S(1)}, bf16[8,4,128,384]{3,2,1,0:T(8,128)(2,1)}, f32[4,128,384]{2,1,0:T(8,128)S(1)}) custom-call(bf16[1024,2048]{1,0:T(8,128)(2,1)} %copy-done.14, bf16[16,2048]{1,0:T(8,128)(2,1)S(1)} %collective-permute-done.edge_ref, ...), custom_call_target="tpu_custom_call" | custom-call | tf_op jit(solution)/shard_map/pallas_call | solution.py:153
  195.2 14.0 collective-permute-done.1
  213.8 9.4 collective-permute-done.2
  237.9 10.1 fusion.65.gate_ref
  256.1 47.2 %all-gather.11.cloned.1.call-done = bf16[1024,2048]{1,0:T(8,128)(2,1)} async-done(((bf16[1024,256]{1,0:T(8,128)(2,1)}), bf16[1024,2048]{1,0:T(8,128)(2,1)}) %all-gather.11.cloned.1.call-update) | async-done | bytes 4194320 | tf_op jit(solution)/shard_map/all_gather | solution.py:566
  323.9 46.1 %collective-permute-done.6 = bf16[512,2048]{1,0:T(8,128)(2,1)S(1)} collective-permute-done((bf16[512,2048]{1,0:T(8,128)(2,1)S(1)}, bf16[512,2048]{1,0:T(8,128)(2,1)S(1)}, u32[]{:S(2)}, u32[]{:S(2)}) %collective-permute-start.6) | collective-permute-done | bytes 2097184 | tf_op jit(solution)/shard_map/ppermute | solution.py:474
  379.3 87.8 %all-gather.13.cloned.1.call-done = bf16[2048,2816]{0,1:T(8,128)(2,1)} async-done(((bf16[256,2816]{0,1:T(8,128)(2,1)}), bf16[2048,2816]{0,1:T(8,128)(2,1)}) %all-gather.13.cloned.1.call-update) | async-done | bytes 11534352 | tf_op jit(solution)/shard_map/all_gather | solution.py:566
  467.1 21.3 %fusion.61 = f32[1024,2816]{1,0:T(8,128)} fusion(bf16[2048,2816]{0,1:T(8,128)(2,1)} %all-gather.13.cloned.1.call-done, bf16[1024,2048]{1,0:T(8,128)(2,1)} %param.20, f32[2048]{0:T(1024)S(1)} %bitcast.90, f32[1024]{0:T(1024)S(1)} %add_rsqrt_fusion, bf16[512,2048]{1,0:T(8,128)(2,1)} %copy-done.18, bf16[512,2048]{1,0:T(8,128)(2,1)S(1)} %get-tuple-element.133), kind=kOutput, calls=%fused_computation.157 | convolution fusion | flops 11830034432 | bytes 31469568 | tf_op jit(solution)/shard_map/dot_general | solution.py:454
  488.5 72.9 %all-gather.15.cloned.1.call-done = bf16[1408,2048]{1,0:T(8,128)(2,1)} async-done(((bf16[1408,256]{1,0:T(8,128)(2,1)}), bf16[1408,2048]{1,0:T(8,128)(2,1)}) %all-gather.15.cloned.1.call-update) | async-done | bytes 5767184 | tf_op jit(solution)/shard_map/all_gather | solution.py:566
  561.4 15.6 %fusion.14 = (bf16[1024,1408]{1,0:T(8,128)(2,1)S(1)}, bf16[1024,1408]{1,0:T(8,128)(2,1)S(1)}, bf16[1024,1408]{1,0:T(8,128)(2,1)}) fusion(f32[1024,2816]{1,0:T(8,128)} %fusion.61, bf16[1408,2048]{1,0:T(8,128)(2,1)} %all-gather.15.cloned.1.call-done, bf16[1024,2048]{1,0:T(8,128)(2,1)} %param.21), kind=kOutput, calls=%fused_computation.32 | convolution fusion | flops 5927206912 | bytes 30146560 | tf_op jit(solution)/shard_map/dot_general | solution.py:462
  577.0 17.1 %fusion.17 = f32[1024,2048]{1,0:T(8,128)S(1)} fusion(bf16[2048,2816]{0,1:T(8,128)(2,1)} %all-gather.13.cloned.1.call-done, bf16[1024,1408]{1,0:T(8,128)(2,1)S(1)} %get-tuple-element.123, bf16[1024,1408]{1,0:T(8,128)(2,1)S(1)} %get-tuple-element.122), kind=kOutput, calls=%fused_computation.55 | convolution fusion | flops 11822694400 | bytes 25690112 | tf_op jit(solution)/shard_map/dot_general | solution.py:462
  598.1 8.7 fusion.84
  615.5 40.9 %collective-permute-done.12 = bf16[512,2048]{1,0:T(8,128)(2,1)S(1)} collective-permute-done((bf16[512,2048]{1,0:T(8,128)(2,1)S(1)}, bf16[512,2048]{1,0:T(8,128)(2,1)S(1)}, u32[]{:S(2)}, u32[]{:S(2)}) %collective-permute-start.12) | collective-permute-done | bytes 2097184 | tf_op jit(solution)/shard_map/ppermute | solution.py:474
  657.5 43.5 %collective-permute-done.9 = bf16[512,2048]{1,0:T(8,128)(2,1)S(1)} collective-permute-done((bf16[512,2048]{1,0:T(8,128)(2,1)S(1)}, bf16[512,2048]{1,0:T(8,128)(2,1)S(1)}, u32[]{:S(2)}, u32[]{:S(2)}) %collective-permute-start.9) | collective-permute-done | bytes 2097184 | tf_op jit(solution)/shard_map/ppermute | solution.py:474
  716.1 13.8 multiply_add_fusion
  729.9 11.4 fusion.21.grad_ref
  780.4 10.5 convolution_convert_fusion.1
  792.9 50.5 %shard_map.350 = (bf16[1024,2048]{1,0:T(8,128)(2,1)}, bf16[1024,128]{1,0:T(8,128)(2,1)}, f32[32,2048]{1,0:T(8,128)}, f32[16,128]{1,0:T(8,128)}, f32[8,2048]{1,0:T(8,128)}) custom-call(bf16[1024,2048]{1,0:T(8,128)(2,1)} %copy-done.14, bf16[1024,2048]{1,0:T(8,128)(2,1)} %copy-done.14, bf16[16,2048]{1,0:T(8,128)(2,1)} %copy-done.5, f32[8,2048]{1,0:T(8,128)} %copy-done.4, ...), custom_call_target="tpu_custom_call" | custom-call | tf_op jit(solution)/shard_map/pallas_call | solution.py:412
  852.7 12.8 fusion.85
  873.8 46.2 %collective-permute-done.20 = bf16[512,2048]{1,0:T(8,128)(2,1)S(1)} collective-permute-done((bf16[512,2048]{1,0:T(8,128)(2,1)S(1)}, bf16[512,2048]{1,0:T(8,128)(2,1)S(1)}, u32[]{:S(2)}, u32[]{:S(2)}) %collective-permute-start.20) | collective-permute-done | bytes 2097184 | tf_op jit(solution)/shard_map/ppermute | solution.py:474
  940.9 9.0 convolution_convert_fusion.5
  951.5 9.5 convolution_convert_fusion.4
  962.7 19.3 %convolution_convert_fusion = bf16[2048,2816]{1,0:T(8,128)(2,1)} fusion(bf16[1024,1408]{1,0:T(8,128)(2,1)} %copy-done.62, bf16[1024,1408]{1,0:T(8,128)(2,1)} %copy-done.61, bf16[1024,2048]{1,0:T(8,128)(2,1)} %param.20, f32[2048]{0:T(1024)S(1)} %bitcast.93, f32[1024]{0:T(1024)S(1)} %add_rsqrt_fusion, bf16[512,2048]{1,0:T(8,128)(2,1)} %copy-done.18, ...), kind=kOutput, calls=%fused_computation.7 | convolution fusion | flops 11847335936 | bytes 25702400 | tf_op jit(solution)/shard_map/dot_general | solution.py:458
  982.0 14.6 convolution_convert_fusion.2
  1000.2 10.6 fusion.8
  1026.7 75.4 %reduce-scatter.8.cloned.1.call-done = bf16[256,1024]{1,0:T(8,128)(2,1)} async-done(((bf16[2048,1024]{1,0:T(8,128)(2,1)}), bf16[256,1024]{1,0:T(8,128)(2,1)}) %reduce-scatter.8.cloned.1.call-update) | async-done | bytes 524304 | tf_op jit(solution)/shard_map/reduce_scatter | solution.py:624
  1104.3 90.2 %reduce-scatter.10.cloned.1.call-done = bf16[1024,256]{1,0:T(8,128)(2,1)} async-done(((bf16[1024,2048]{1,0:T(8,128)(2,1)}), bf16[1024,256]{1,0:T(8,128)(2,1)}) %reduce-scatter.10.cloned.1.call-update) | async-done | bytes 524304 | tf_op jit(solution)/shard_map/reduce_scatter | solution.py:624
  1196.6 193.8 %reduce-scatter.12.cloned.1.call-done = bf16[256,2816]{1,0:T(8,128)(2,1)} async-done(((bf16[2048,2816]{1,0:T(8,128)(2,1)}), bf16[256,2816]{1,0:T(8,128)(2,1)}) %reduce-scatter.12.cloned.1.call-update) | async-done | bytes 1441808 | tf_op jit(solution)/shard_map/reduce_scatter | solution.py:624
  1395.0 147.2 %reduce-scatter.6.cloned.1.call-done = bf16[256,2048]{1,0:T(8,128)(2,1)} async-done(((bf16[2048,2048]{1,0:T(8,128)(2,1)}), bf16[256,2048]{1,0:T(8,128)(2,1)}) %reduce-scatter.6.cloned.1.call-update) | async-done | bytes 1048592 | tf_op jit(solution)/shard_map/reduce_scatter | solution.py:624
  (356 shorter events, 228.6 us)
Async XLA Ops:
  7.2 133.1 %all-gather.7.cloned.1.call-start = ((), (), s32[]{:S(2)}) async-start(), calls=%async_computation.5 | async-start | bytes 9437184 | tf_op jit(solution)/shard_map/all_gather | solution.py:566
  11.9 226.0 %all-gather.9.cloned.1.call-start = ((), (), s32[]{:S(2)}) async-start(), calls=%async_computation.6 | async-start | bytes 4718592 | tf_op jit(solution)/shard_map/all_gather | solution.py:566
  14.2 289.1 %all-gather.11.cloned.1.call-start = ((), (), s32[]{:S(2)}) async-start(), calls=%async_computation.7 | async-start | bytes 4718592 | tf_op jit(solution)/shard_map/all_gather | solution.py:566
  16.5 450.7 %all-gather.13.cloned.1.call-start = ((), (), s32[]{:S(2)}) async-start(), calls=%async_computation.8 | async-start | bytes 12976128 | tf_op jit(solution)/shard_map/all_gather | solution.py:566
  17.9 543.5 %all-gather.15.cloned.1.call-start = ((), (), s32[]{:S(2)}) async-start(), calls=%async_computation.9 | async-start | bytes 6488064 | tf_op jit(solution)/shard_map/all_gather | solution.py:566
  152.9 4.5 collective-permute-start
  192.8 16.4 %collective-permute-start.1 = (bf16[4,128,384]{2,1,0:T(8,128)(2,1)S(1)}, bf16[4,128,384]{2,1,0:T(8,128)(2,1)S(1)}, u32[]{:S(2)}, u32[]{:S(2)}) collective-permute-start(bf16[4,128,384]{2,1,0:T(8,128)(2,1)S(1)} %convert_element_type.278), channel_id=1, source_target_pairs={{4,0},{0,4},{12,8},{8,12},{20,16},{16,20},{28,24},{24,28},{5,1},{1... | collective-permute-start | bytes 1179656 | tf_op jit(solution)/shard_map/ppermute | solution.py:502
  210.4 12.8 collective-permute-start.2
  223.4 9.8 collective-permute-start.3
  233.4 15.0 collective-permute-start.4
  314.2 4.5 collective-permute-start.5
  315.2 682.7 %reduce-scatter.14.cloned.1.call-start = ((), (), s32[]{:S(2)}) async-start(), calls=%async_computation.14 | async-start | bytes 6488064 | tf_op jit(solution)/shard_map/reduce_scatter | solution.py:624
  322.2 47.7 %collective-permute-start.6 = (bf16[512,2048]{1,0:T(8,128)(2,1)S(1)}, bf16[512,2048]{1,0:T(8,128)(2,1)S(1)}, u32[]{:S(2)}, u32[]{:S(2)}) collective-permute-start(bf16[512,2048]{1,0:T(8,128)(2,1)S(1)} %add_convert_fusion.8), channel_id=1, source_target_pairs={{0,2},{2,0},{1,3},{3,1},{4,6},{6,4},{5,7},{7,5},{8,10},{10,8},{9,1... | collective-permute-start | bytes 6291464 | tf_op jit(solution)/shard_map/ppermute | solution.py:474
  370.8 4.4 collective-permute-start.7
  594.5 12.7 collective-permute-start.11
  607.1 4.4 collective-permute-start.8
  608.0 48.5 %collective-permute-start.12 = (bf16[512,2048]{1,0:T(8,128)(2,1)S(1)}, bf16[512,2048]{1,0:T(8,128)(2,1)S(1)}, u32[]{:S(2)}, u32[]{:S(2)}) collective-permute-start(bf16[512,2048]{1,0:T(8,128)(2,1)S(1)} %add_convert_fusion.4), channel_id=1, source_target_pairs={{0,2},{2,0},{1,3},{3,1},{4,6},{6,4},{5,7},{7,5},{8,10},{10,8},{9,1... | collective-permute-start | bytes 6291464 | tf_op jit(solution)/shard_map/ppermute | solution.py:474
  614.0 87.0 %collective-permute-start.9 = (bf16[512,2048]{1,0:T(8,128)(2,1)S(1)}, bf16[512,2048]{1,0:T(8,128)(2,1)S(1)}, u32[]{:S(2)}, u32[]{:S(2)}) collective-permute-start(bf16[512,2048]{1,0:T(8,128)(2,1)S(1)} %add_convert_fusion.6), channel_id=1, source_target_pairs={{0,2},{2,0},{1,3},{3,1},{4,6},{6,4},{5,7},{7,5},{8,10},{10,8},{9,1... | collective-permute-start | bytes 6291464 | tf_op jit(solution)/shard_map/ppermute | solution.py:474
  657.4 44.5 %collective-permute-start.13 = (bf16[512,2048]{1,0:T(8,128)(2,1)S(1)}, bf16[512,2048]{1,0:T(8,128)(2,1)S(1)}, u32[]{:S(2)}, u32[]{:S(2)}) collective-permute-start(bf16[512,2048]{1,0:T(8,128)(2,1)S(1)} %add_convert_fusion.3), channel_id=1, source_target_pairs={{0,1},{1,0},{2,3},{3,2},{4,5},{5,4},{6,7},{7,6},{8,9},{9,8},{10,11... | collective-permute-start | bytes 6291464 | tf_op jit(solution)/shard_map/ppermute | solution.py:476
  701.8 10.4 collective-permute-start.10
  750.1 8.0 collective-permute-start.14
  759.2 8.9 collective-permute-start.15
  769.4 8.4 collective-permute-start.16
  779.1 11.9 collective-permute-start.17
  790.9 219.9 %all-reduce.12.cloned.1.call-start = ((), (), s32[]{:S(2)}) async-start(), calls=%async_computation.15 | async-start | bytes 131072
  843.5 7.6 collective-permute-start.18
  872.2 47.7 %collective-permute-start.20 = (bf16[512,2048]{1,0:T(8,128)(2,1)S(1)}, bf16[512,2048]{1,0:T(8,128)(2,1)S(1)}, u32[]{:S(2)}, u32[]{:S(2)}) collective-permute-start(bf16[512,2048]{1,0:T(8,128)(2,1)S(1)} %add_convert_fusion.2), channel_id=1, source_target_pairs={{0,2},{2,0},{1,3},{3,1},{4,6},{6,4},{5,7},{7,5},{8,10},{10,8},{9,1... | collective-permute-start | bytes 6291464 | tf_op jit(solution)/shard_map/ppermute | solution.py:474
  922.2 7.2 collective-permute-start.21
  940.9 161.3 %reduce-scatter.8.cloned.1.call-start = ((), (), s32[]{:S(2)}) async-start(), calls=%async_computation.11 | async-start | bytes 4718592 | tf_op jit(solution)/shard_map/reduce_scatter | solution.py:624
  950.0 244.6 %reduce-scatter.10.cloned.1.call-start = ((), (), s32[]{:S(2)}) async-start(), calls=%async_computation.12 | async-start | bytes 4718592 | tf_op jit(solution)/shard_map/reduce_scatter | solution.py:624
  961.1 429.3 %reduce-scatter.12.cloned.1.call-start = ((), (), s32[]{:S(2)}) async-start(), calls=%async_computation.13 | async-start | bytes 12976128 | tf_op jit(solution)/shard_map/reduce_scatter | solution.py:624
  982.0 560.2 %reduce-scatter.6.cloned.1.call-start = ((), (), s32[]{:S(2)}) async-start(), calls=%async_computation.10 | async-start | bytes 9437184 | tf_op jit(solution)/shard_map/reduce_scatter | solution.py:624
  (66 other events, 1754.2 us)
Sparse Core Ops, SparseCore 0:
  12.0 128.1 all-gather.6
  143.0 79.7 all-gather.8
  225.3 77.8 all-gather.10
  305.2 161.9 all-gather.12
  469.6 91.7 all-gather.14
  791.0 111.8 reduce-scatter.13
  941.0 69.4 all-reduce.11
  1014.2 87.9 reduce-scatter.7
  1106.2 88.2 reduce-scatter.9
  1198.0 192.4 reduce-scatter.11
  1394.1 148.1 reduce-scatter.5

commit v2 on v1

v2 whole, which is shorter than its diff:
```python
import functools
import jax
import jax.numpy as jnp
from jax import lax
from jax.experimental import pallas as pl
from jax.experimental.pallas import tpu as pltpu

ROWS = 128
KEY = 128
VAL = 256
HALO = 16
eps_norm = 1e-06
f32 = jnp.float32
bf16 = jnp.bfloat16


def mm(a, b):
    return lax.dot_general(
        a.astype(bf16), b.astype(bf16), (((1,), (0,)), ((), ())), preferred_element_type=f32
    )


def mm_nt(a, b):
    return lax.dot_general(
        a.astype(bf16), b.astype(bf16), (((1,), (1,)), ((), ())), preferred_element_type=f32
    )


def mm_tn(a, b):
    return lax.dot_general(
        a.astype(bf16), b.astype(bf16), (((0,), (0,)), ((), ())), preferred_element_type=f32
    )


def mm_full(a, b):
    return lax.dot_general(
        a, b, (((1,), (0,)), ((), ())), precision=lax.Precision.HIGHEST, preferred_element_type=f32
    )


def sigmoid(x):
    return 1.0 / (1.0 + jnp.exp(-x))


def softplus(x):
    return jnp.maximum(x, 0.0) + jnp.log(1.0 + jnp.exp(-jnp.abs(x)))


def positions():
    rows = lax.broadcasted_iota(jnp.int32, (ROWS, ROWS), 0)
    cols = lax.broadcasted_iota(jnp.int32, (ROWS, ROWS), 1)
    return rows, cols


def decay_terms(heads, ab, par):
    rows, cols = positions()
    log_decay = -par[0:1, :] * softplus(ab + par[1:2, :])
    running = mm_full((rows >= cols).astype(f32), log_decay)
    return log_decay, running, running.T, sigmoid(ab)


def ratio_of(running, running_rows, h, rows, cols):
    gap = running[:, h : h + 1] - running_rows[h : h + 1, :]
    return jnp.where(rows >= cols, jnp.exp(jnp.where(rows >= cols, gap, 0.0)), 0.0)


def conv_at(xs_ref, taps_ref, base, lo, width):
    total = taps_ref[0:1, lo : lo + width] * xs_ref[base - 3 : base - 3 + ROWS, lo : lo + width]
    for i in range(1, 4):
        total = total + taps_ref[i : i + 1, lo : lo + width] * (
            xs_ref[base - 3 + i : base - 3 + i + ROWS, lo : lo + width]
        )
    return total


def forward_kernel(heads, proj_ref, edge_ref, taps_ref, ab_ref, par_ref,
                   value_ref, ident_ref, inv_ref, state_ref, final_ref, xs_ref, s_ref):
    step = pl.program_id(0)
    keys = heads * KEY

    @pl.when(step == 0)
    def _():
        xs_ref[0:HALO, :] = edge_ref[...].astype(f32)
        r, c = positions()
        for h in range(heads):
            s_ref[h, :, 0:VAL] = jnp.zeros((KEY, VAL), f32)
            s_ref[h, :, VAL:] = (r == c).astype(f32)

    span = proj_ref.shape[0]
    subs = range(span // ROWS)

    @pl.when(step > 0)
    def _():
        xs_ref[0:HALO, :] = xs_ref[span : span + HALO, :]

    xs_ref[HALO : HALO + span, :] = proj_ref[...].astype(f32)
    rows, cols = positions()
    every = [(s, h) for s in subs for h in range(heads)]
    running, running_rows, strength = [], [], []
    for s in subs:
        terms = decay_terms(heads, ab_ref[s * ROWS : (s + 1) * ROWS, :], par_ref[...])
        running.append(terms[1])
        running_rows.append(terms[2])
        strength.append(terms[3])
    q, k, v, a, p, t, beta, grow = {}, {}, {}, {}, {}, {}, {}, {}
    for s, h in every:
        base = HALO + s * ROWS
        u = conv_at(xs_ref, taps_ref, base, h * KEY, KEY)
        u = u * sigmoid(u)
        q[s, h] = u * (lax.rsqrt(jnp.sum(u * u, axis=1, keepdims=True) + eps_norm) * KEY**-0.5)
        w = conv_at(xs_ref, taps_ref, base, keys + h * KEY, KEY)
        w = w * sigmoid(w)
        k[s, h] = w * lax.rsqrt(jnp.sum(w * w, axis=1, keepdims=True) + eps_norm)
        x = conv_at(xs_ref, taps_ref, base, 2 * keys + h * VAL, VAL)
        v[s, h] = x * sigmoid(x)
        beta[s, h] = strength[s][:, heads + h : heads + h + 1]
        grow[s, h] = jnp.exp(running[s][:, h : h + 1])
    for s, h in every:
        ratio = ratio_of(running[s], running_rows[s], h, rows, cols)
        gram = mm_nt(k[s, h], k[s, h])
        a[s, h] = jnp.where(rows > cols, ratio * gram, 0.0) * beta[s, h]
        p[s, h] = ratio * mm_nt(q[s, h], k[s, h])
    first = (rows // 2 == cols // 2) & (rows > cols)
    for e in every:
        t[e] = (rows == cols).astype(f32) - jnp.where(first, a[e], 0.0)
    b = 2
    while b < ROWS:
        low = (rows // (2 * b) == cols // (2 * b)) & ((rows // b) % 2 == 1) & ((cols // b) % 2 == 0)
        inner = {e: mm(jnp.where(low, a[e], 0.0), t[e]) for e in every}
        t = {e: t[e] - mm(t[e], inner[e]) for e in every}
        b *= 2
    uw = {
        e: mm(t[e], jnp.concatenate([beta[e] * v[e], (beta[e] * grow[e]) * k[e]], axis=1))
        for e in every
    }
    for s, h in every:
        inv_ref[s * ROWS : (s + 1) * ROWS, h * KEY : (h + 1) * KEY] = t[s, h].astype(bf16)
    for s, h in every:
        at = slice(s * ROWS, (s + 1) * ROWS)
        state = s_ref[h]
        state_ref[s, h] = state.astype(bf16)
        pred = mm(uw[s, h][:, VAL:], state)
        err = jnp.concatenate([uw[s, h][:, :VAL] - pred[:, :VAL], -pred[:, VAL:]], axis=1)
        out = grow[s, h] * mm(q[s, h], state) + mm(p[s, h], err)
        value_ref[at, h * VAL : (h + 1) * VAL] = out[:, :VAL]
        ident_ref[at, h * KEY : (h + 1) * KEY] = out[:, VAL:].astype(bf16)
        end = running[s][ROWS - 1 : ROWS, h : h + 1]
        tail = jnp.exp(end - running[s][:, h : h + 1]) * k[s, h]
        s_ref[h] = jnp.exp(end) * state + mm_tn(tail, err)

    @pl.when(step == pl.num_programs(0) - 1)
    def _():
        final_ref[...] = s_ref[...]


def sub_blocks(heads):
    return 2


def delta_forward(proj, edge, taps, ab, par):
    tokens = proj.shape[0]
    heads = proj.shape[1] // (2 * KEY + VAL)
    keys, vals = heads * KEY, heads * VAL
    subs = sub_blocks(heads)
    span = subs * ROWS
    blocks = tokens // span
    width = proj.shape[1]
    whole = lambda *shape: pl.BlockSpec(shape, lambda c: (0,) * len(shape))
    return pl.pallas_call(
        functools.partial(forward_kernel, heads),
        grid=(blocks,),
        in_specs=[
            pl.BlockSpec((span, width), lambda c: (c, 0)),
            whole(HALO, width),
            whole(8, width),
            pl.BlockSpec((span, 128), lambda c: (c, 0)),
            whole(8, 128),
        ],
        out_specs=[
            pl.BlockSpec((span, vals), lambda c: (c, 0)),
            pl.BlockSpec((span, keys), lambda c: (c, 0)),
            pl.BlockSpec((span, keys), lambda c: (c, 0)),
            pl.BlockSpec((subs, heads, KEY, VAL + KEY), lambda c: (c, 0, 0, 0)),
            whole(heads, KEY, VAL + KEY),
        ],
        out_shape=[
            jax.ShapeDtypeStruct((tokens, vals), f32),
            jax.ShapeDtypeStruct((tokens, keys), bf16),
            jax.ShapeDtypeStruct((tokens, keys), bf16),
            jax.ShapeDtypeStruct((blocks * subs, heads, KEY, VAL + KEY), bf16),
            jax.ShapeDtypeStruct((heads, KEY, VAL + KEY), f32),
        ],
        scratch_shapes=[
            pltpu.VMEM((HALO + span, width), f32),
            pltpu.VMEM((heads, KEY, VAL + KEY), f32),
        ],
        compiler_params=pltpu.CompilerParams(
            dimension_semantics=("arbitrary",), vmem_limit_bytes=48 * 2**20
        ),
    )(proj, edge, taps, ab, par)


UNIT = 2 * ROWS


def placed_rows(order_ref, sub):
    flip = order_ref[order_ref.shape[0] - 1]
    return pl.ds(pl.multiple_of((flip + sub - 2 * flip * sub) * ROWS, ROWS), ROWS)


def reorder_kernel(order_ref, *refs):
    count = len(refs) // 2
    for in_ref, out_ref in zip(refs[:count], refs[count:]):
        for sub in range(2):
            out_ref[placed_rows(order_ref, sub), :] = in_ref[sub * ROWS : (sub + 1) * ROWS, :]


def reordered(order, *arrays):
    tokens = arrays[0].shape[0]
    return pl.pallas_call(
        reorder_kernel,
        grid_spec=pltpu.PrefetchScalarGridSpec(
            num_scalar_prefetch=1,
            grid=(tokens // UNIT,),
            in_specs=[pl.BlockSpec((UNIT, a.shape[1]), lambda c, order: (order[c], 0)) for a in arrays],
            out_specs=[pl.BlockSpec((UNIT, a.shape[1]), lambda c, order: (c, 0)) for a in arrays],
        ),
        out_shape=[jax.ShapeDtypeStruct(a.shape, a.dtype) for a in arrays],
        compiler_params=pltpu.CompilerParams(
            dimension_semantics=("arbitrary",), vmem_limit_bytes=32 * 2**20
        ),
    )(order, *arrays)


def output_kernel(heads, order_ref, value_ref, ident_ref, state_ref, gate_ref, gain_ref, out_ref, gated_ref):
    for h in range(heads):
        span = slice(h * VAL, (h + 1) * VAL)
        out = value_ref[:, span] + mm(ident_ref[:, h * KEY : (h + 1) * KEY], state_ref[h])
        out_ref[:, span] = out
        gate = gate_ref[:, span]
        unit = out * lax.rsqrt(jnp.mean(out * out, axis=1, keepdims=True) + eps_norm)
        gated = (unit * gain_ref[0:1, :] * (gate * sigmoid(gate))).astype(bf16)
        for sub in range(2):
            gated_ref[placed_rows(order_ref, sub), span] = gated[sub * ROWS : (sub + 1) * ROWS]


def gated_outputs(order, value_out, ident, state_in, gate_pre, gain):
    tokens, vals = value_out.shape
    heads = vals // VAL
    placed = lambda width: pl.BlockSpec((UNIT, width), lambda c, order: (order[c], 0))
    return pl.pallas_call(
        functools.partial(output_kernel, heads),
        grid_spec=pltpu.PrefetchScalarGridSpec(
            num_scalar_prefetch=1,
            grid=(tokens // UNIT,),
            in_specs=[
                placed(vals),
                placed(heads * KEY),
                pl.BlockSpec((heads, KEY, VAL), lambda c, order: (0, 0, 0)),
                placed(vals),
                pl.BlockSpec((1, VAL), lambda c, order: (0, 0)),
            ],
            out_specs=[placed(vals), pl.BlockSpec((UNIT, vals), lambda c, order: (c, 0))],
        ),
        out_shape=[
            jax.ShapeDtypeStruct((tokens, vals), f32),
            jax.ShapeDtypeStruct((tokens, vals), bf16),
        ],
        compiler_params=pltpu.CompilerParams(
            dimension_semantics=("arbitrary",), vmem_limit_bytes=48 * 2**20
        ),
    )(order, value_out, ident, state_in, gate_pre, gain)


def gate_back_kernel(heads, order_ref, grad_ref, out_ref, gate_ref, gain_ref, ident_ref,
                     dout_ref, dgate_ref, dgain_ref, pull_ref):
    @pl.when(pl.program_id(0) == 0)
    def _():
        dgain_ref[...] = jnp.zeros_like(dgain_ref)
        pull_ref[...] = jnp.zeros_like(pull_ref)

    gain = gain_ref[0:1, :]
    for h in range(heads):
        span = slice(h * VAL, (h + 1) * VAL)
        grad = jnp.concatenate([grad_ref[placed_rows(order_ref, sub), span] for sub in range(2)], axis=0)
        out, gate = out_ref[:, span], gate_ref[:, span]
        scale = lax.rsqrt(jnp.mean(out * out, axis=1, keepdims=True) + eps_norm)
        unit = out * scale
        sig = sigmoid(gate)
        m = grad * (gate * sig)
        mn = m * unit
        dgain_ref[...] += jnp.sum(mn.reshape(-1, 8, VAL), axis=0)
        mean = jnp.mean(mn * gain, axis=1, keepdims=True)
        dout = (scale * (m * gain - unit * mean)).astype(bf16)
        dout_ref[:, span] = dout
        dgate = (grad * unit * gain * (sig * (1.0 + gate * (1.0 - sig)))).astype(bf16)
        for sub in range(2):
            dgate_ref[placed_rows(order_ref, sub), span] = dgate[sub * ROWS : (sub + 1) * ROWS]
        pull_ref[h] += mm_tn(ident_ref[:, h * KEY : (h + 1) * KEY], dout)


def gate_backward(order, grad_gated, outputs, gate_pre, gain, ident):
    tokens, vals = outputs.shape
    heads = vals // VAL
    placed = lambda width: pl.BlockSpec((UNIT, width), lambda c, order: (order[c], 0))
    return pl.pallas_call(
        functools.partial(gate_back_kernel, heads),
        grid_spec=pltpu.PrefetchScalarGridSpec(
            num_scalar_prefetch=1,
            grid=(tokens // UNIT,),
            in_specs=[
                pl.BlockSpec((UNIT, vals), lambda c, order: (c, 0)),
                placed(vals),
                placed(vals),
                pl.BlockSpec((1, VAL), lambda c, order: (0, 0)),
                placed(heads * KEY),
            ],
            out_specs=[
                placed(vals),
                pl.BlockSpec((UNIT, vals), lambda c, order: (c, 0)),
                pl.BlockSpec((8, VAL), lambda c, order: (0, 0)),
                pl.BlockSpec((heads, KEY, VAL), lambda c, order: (0, 0, 0)),
            ],
        ),
        out_shape=[
            jax.ShapeDtypeStruct((tokens, vals), bf16),
            jax.ShapeDtypeStruct((tokens, vals), bf16),
            jax.ShapeDtypeStruct((8, VAL), f32),
            jax.ShapeDtypeStruct((heads, KEY, VAL), f32),
        ],
        compiler_params=pltpu.CompilerParams(
            dimension_semantics=("arbitrary",), vmem_limit_bytes=48 * 2**20
        ),
    )(order, grad_gated, outputs, gate_pre, gain, ident)


def backward_kernel(heads, order_ref, proj_ref, before_ref, edge_ref, taps_ref, ab_ref, par_ref, dout_ref,
                    inv_ref, state_ref, enter_ref, dfinal_ref,
                    dproj_ref, dab_ref, dtaps_ref, dpar_ref, dhead_ref,
                    xs_ref, gs_ref, ds_ref):
    step = pl.program_id(0)
    last = pl.num_programs(0) - 1
    keys = heads * KEY
    width = 2 * keys + heads * VAL
    span = proj_ref.shape[0]

    @pl.when(step == 0)
    def _():
        ds_ref[...] = dfinal_ref[...]
        dtaps_ref[...] = jnp.zeros_like(dtaps_ref)
        dpar_ref[...] = jnp.zeros_like(dpar_ref)
        gs_ref[span : span + 8, :] = jnp.zeros((8, width), f32)

    @pl.when(step > 0)
    def _():
        gs_ref[span : span + 8, :] = gs_ref[0:8, :]

    @pl.when(step == last)
    def _():
        xs_ref[0:HALO, :] = edge_ref[...].astype(f32)

    @pl.when(step < last)
    def _():
        xs_ref[0:HALO, :] = before_ref[...].astype(f32)

    xs_ref[HALO : HALO + span, :] = proj_ref[...].astype(f32)
    rows, cols = positions()
    par = par_ref[...]
    lane = lax.broadcasted_iota(jnp.int32, (ROWS, 128), 1)
    row_at = lax.broadcasted_iota(jnp.int32, (ROWS, 1), 0)
    for s in reversed(range(span // ROWS)):
        at = slice(s * ROWS, (s + 1) * ROWS)
        ab = ab_ref[at, :]
        log_decay, running, running_rows, strength = decay_terms(heads, ab, par)
        drunning = jnp.zeros((ROWS, 128), f32)
        dbeta = jnp.zeros((ROWS, 128), f32)

        for h in range(heads):
            qs, ks, vs = h * KEY, keys + h * KEY, 2 * keys + h * VAL
            u = conv_at(xs_ref, taps_ref, HALO + s * ROWS, qs, KEY)
            su = sigmoid(u)
            wu = u * su
            ru = lax.rsqrt(jnp.sum(wu * wu, axis=1, keepdims=True) + eps_norm)
            q = wu * (ru * KEY**-0.5)
            y = conv_at(xs_ref, taps_ref, HALO + s * ROWS, ks, KEY)
            sy = sigmoid(y)
            wy = y * sy
            ry = lax.rsqrt(jnp.sum(wy * wy, axis=1, keepdims=True) + eps_norm)
            k = wy * ry
            x = conv_at(xs_ref, taps_ref, HALO + s * ROWS, vs, VAL)
            sx = sigmoid(x)
            v = x * sx
            qb, kb = q.astype(bf16), k.astype(bf16)
            beta = strength[:, heads + h : heads + h + 1]
            passed = running[:, h : h + 1]
            grow = jnp.exp(passed)
            end = running[ROWS - 1 : ROWS, h : h + 1]
            tail = jnp.exp(end - passed)
            ratio = ratio_of(running, running_rows, h, rows, cols)
            p = ratio * mm_nt(qb, kb)
            t = inv_ref[at, h * KEY : (h + 1) * KEY]
            dout = dout_ref[at, h * VAL : (h + 1) * VAL]
            state = state_ref[s, h, :, :VAL].astype(f32) + mm(state_ref[s, h, :, VAL:], enter_ref[h])
            state_b = state.astype(bf16)
            dstate = ds_ref[h]
            dstate_b = dstate.astype(bf16)
            err = mm(t, beta * (v - grow * mm(kb, state_b)))
            err_b = err.astype(bf16)
            derr = mm_tn(p, dout) + mm(tail * k, dstate_b)
            dright = mm_tn(t, derr)
            dright_b = dright.astype(bf16)
            dp = mm_nt(dout, err_b) * ratio
            dp_b = dp.astype(bf16)
            da = jnp.where(rows > cols, mm_nt(dright_b, err_b) * ratio, 0.0) * (-beta)
            da_b = da.astype(bf16)
            back = (beta * grow) * dright
            back_b = back.astype(bf16)
            dq = grow * mm_nt(dout, state_b) + mm(dp_b, kb)
            dk_read = mm(da_b, kb) - mm_nt(back_b, state_b)
            dk_tail = tail * mm_nt(err_b, dstate_b)
            dk_write = mm_tn(dp_b, qb) + mm_tn(da_b, kb) + dk_tail
            dk = dk_read + dk_write
            dv = beta * dright
            to_beta = (1.0 - beta) * jnp.sum(dright * err, axis=1, keepdims=True)
            to_decay = jnp.sum(q * dq + k * (dk_read - dk_write), axis=1, keepdims=True)
            at_end = jnp.exp(end) * jnp.sum(
                jnp.sum(state * dstate, axis=1, keepdims=True), axis=0, keepdims=True
            ) + jnp.sum(jnp.sum(k * dk_tail, axis=1, keepdims=True), axis=0, keepdims=True)
            to_decay = to_decay + jnp.where(row_at == ROWS - 1, at_end, 0.0)
            drunning = jnp.where(lane == h, to_decay, drunning)
            dbeta = jnp.where(lane == heads + h, to_beta, dbeta)
            ds_ref[h] = jnp.exp(end) * dstate + mm_tn(grow * q, dout) - mm_tn(kb, back_b)
            along = jnp.sum(wu * dq, axis=1, keepdims=True)
            du = (KEY**-0.5) * (ru * dq - wu * (ru * ru * ru * along))
            gs_ref[at, qs : qs + KEY] = du * (su * (1.0 + u * (1.0 - su)))
            along = jnp.sum(wy * dk, axis=1, keepdims=True)
            dy = ry * dk - wy * (ry * ry * ry * along)
            gs_ref[at, ks : ks + KEY] = dy * (sy * (1.0 + y * (1.0 - sy)))
            gs_ref[at, vs : vs + VAL] = dv * (sx * (1.0 + x * (1.0 - sx)))

        dlog = mm_full((rows <= cols).astype(f32), drunning)
        dalpha = -dlog * par[0:1, :] * sigmoid(ab + par[1:2, :])
        dab_ref[placed_rows(order_ref, s), :] = jnp.where(lane < heads, dalpha, dbeta).astype(bf16)
        dpar_ref[0:8, :] += jnp.sum((dlog * log_decay).reshape(-1, 8, 128), axis=0)
        dpar_ref[8:16, :] += jnp.sum(dalpha.reshape(-1, 8, 128), axis=0)

    for lo in range(0, width, 256):
        lanes = slice(lo, lo + 256)
        grad = gs_ref[0:span, lanes]
        total = taps_ref[3:4, lanes] * grad
        for i in range(4):
            moved = xs_ref[HALO - 3 + i : HALO - 3 + i + span, lanes] * grad
            dtaps_ref[8 * i : 8 * i + 8, lanes] += jnp.sum(moved.reshape(-1, 8, 256), axis=0)
            if i < 3:
                total = total + taps_ref[i : i + 1, lanes] * gs_ref[3 - i : 3 - i + span, lanes]
        total = total.astype(bf16)
        for s in range(2):
            dproj_ref[placed_rows(order_ref, s), lanes] = total[s * ROWS : (s + 1) * ROWS]

    @pl.when(step == last)
    def _():
        dhead_ref[...] = gs_ref[0:8, :]


def delta_backward(order, proj, edge, taps, ab, par, dout, inverse, states, entering, dfinal):
    tokens, width = proj.shape
    heads = width // (2 * KEY + VAL)
    keys, vals = heads * KEY, heads * VAL
    subs = sub_blocks(heads)
    span = subs * ROWS
    blocks = tokens // span
    whole = lambda *shape: pl.BlockSpec(shape, lambda c, order: (0,) * len(shape))
    rev = lambda w: pl.BlockSpec((span, w), lambda c, order: (blocks - 1 - c, 0))
    sent = lambda w: pl.BlockSpec((span, w), lambda c, order: (order[blocks + blocks - 1 - c], 0))
    per = span // HALO
    return pl.pallas_call(
        functools.partial(backward_kernel, heads),
        grid_spec=pltpu.PrefetchScalarGridSpec(
            num_scalar_prefetch=1,
            grid=(blocks,),
            in_specs=[
                rev(width),
                pl.BlockSpec((HALO, width), lambda c, order: (jnp.maximum((blocks - 1 - c) * per - 1, 0), 0)),
                whole(HALO, width),
                whole(8, width),
                rev(128),
                whole(8, 128),
                rev(vals),
                rev(keys),
                pl.BlockSpec((subs, heads, KEY, VAL + KEY), lambda c, order: (blocks - 1 - c, 0, 0, 0)),
                whole(heads, KEY, VAL),
                whole(heads, KEY, VAL),
            ],
            out_specs=[
                sent(width),
                sent(128),
                whole(32, width),
                whole(16, 128),
                whole(8, width),
            ],
            scratch_shapes=[
                pltpu.VMEM((HALO + span, width), f32),
                pltpu.VMEM((span + 8, width), f32),
                pltpu.VMEM((heads, KEY, VAL), f32),
            ],
        ),
        out_shape=[
            jax.ShapeDtypeStruct((tokens, width), bf16),
            jax.ShapeDtypeStruct((tokens, 128), bf16),
            jax.ShapeDtypeStruct((32, width), f32),
            jax.ShapeDtypeStruct((16, 128), f32),
            jax.ShapeDtypeStruct((8, width), f32),
        ],
        compiler_params=pltpu.CompilerParams(
            dimension_semantics=("arbitrary",), vmem_limit_bytes=56 * 2**20
        ),
    )(order, proj, proj, edge, taps, ab, par, dout, inverse, states, entering, dfinal)


def dot_rows(a, b):
    return lax.dot_general(a, b, (((1,), (0,)), ((), ())), preferred_element_type=f32)


def dot_left(a, b):
    return lax.dot_general(a, b, (((0,), (0,)), ((), ())), preferred_element_type=f32)


def dot_right(a, b):
    return lax.dot_general(a, b, (((1,), (1,)), ((), ())), preferred_element_type=f32)


def batched(a, b):
    return lax.dot_general(a, b, (((2,), (1,)), ((0,), (0,))), preferred_element_type=f32)


def batched_t(a, b):
    return lax.dot_general(a, b, (((1,), (1,)), ((0,), (0,))), preferred_element_type=f32)


def tie(first, *then):
    return lax.optimization_barrier((first, *then))[0] if then else first


def fold_of():
    return 2 if lax.axis_size("seq") == 8 and lax.axis_size("head") == 4 else 1


def lines_of():
    fold = fold_of()
    return [list(range(x, lax.axis_size("seq"), fold)) for x in range(fold)]


def side_of():
    return lax.axis_index("seq") % fold_of()


def swap_pair(v):
    return lax.ppermute(v, "seq", [(i, i ^ 1) for i in range(lax.axis_size("seq"))])


def swap_chip(v):
    return lax.ppermute(v, "head", [(i, i ^ 2) for i in range(4)])


def swap_core(v):
    return lax.ppermute(v, "head", [(i, i ^ 1) for i in range(4)])


def pick(v, at, axis=0):
    half = v.shape[axis] // 2
    return lax.dynamic_slice_in_dim(v, at * half, half, axis)


def join(at, mine, other, axis=0):
    first, second = jnp.where(at == 0, mine, other), jnp.where(at == 0, other, mine)
    return jnp.concatenate([first, second], axis=axis)


def plus(a, b):
    return (a.astype(f32) + b.astype(f32)).astype(bf16)


def place_of():
    core, chip = lax.axis_index("head") % 2, lax.axis_index("head") // 2
    return core, chip, side_of()


def unit_order(count):
    if fold_of() == 1:
        same = [jnp.int32(i) for i in range(count)]
        return same, same, jnp.int32(0)
    core, chip, side = place_of()
    bits = [(i // 4, i // 2 % 2, i % 2) for i in range(8)]
    at_place = [((s ^ side) * 4 + (c ^ core) * 2 + kind).astype(jnp.int32) for c, kind, s in bits]
    of_unit = [((c ^ core) * 4 + kind * 2 + (s ^ side)).astype(jnp.int32) for s, c, kind in bits]
    return at_place, of_unit, chip.astype(jnp.int32)


def chip_sum(away, near):
    if fold_of() == 1:
        return jnp.concatenate([near, away], axis=0).astype(bf16)
    return plus(near, swap_core(away.astype(bf16)))


def summed_rows(mine, beside=(), later=()):
    if fold_of() == 1:
        return [lax.psum(mine, "head")]
    n = mine.shape[0] // 8
    blocks = [mine[i * n : (i + 1) * n] for i in range(8)]
    a = plus(mine[: 2 * n], swap_pair(mine[2 * n : 4 * n]))
    keep, give = (jnp.concatenate([blocks[4 + i], blocks[6 + i]], axis=0) for i in range(2))
    b = plus(keep, swap_chip(give))
    a, b = tie(a, *beside), tie(b, *beside)
    a, b = plus(a[:n], swap_chip(a[n:])), plus(b[:n], swap_pair(b[n:]))
    return [tie(a, *later), tie(b, *later)]


def all_rows(pieces, beside=()):
    if fold_of() == 1:
        return pieces[0]
    a, b = pieces
    a = jnp.concatenate([a, swap_chip(a)], axis=0)
    b = jnp.concatenate([b, swap_pair(b)], axis=0)
    a, b = tie(a, *beside), tie(b, *beside)
    far = swap_chip(b)
    n = far.shape[0] // 2
    b = jnp.concatenate([b[:n], far[:n], b[n:], far[n:]], axis=0)
    near = [a, swap_pair(a), b]
    return jnp.concatenate(near + [swap_core(v) for v in near], axis=0)


def own_tokens(pieces, *beside):
    if fold_of() == 1:
        return pieces[0]
    core, chip, _ = place_of()
    near = jnp.concatenate([join(chip, v, swap_chip(v)) for v in pieces], axis=0)
    near = tie(near, *beside)
    return join(core, near, swap_core(near))


def own_blocks(v):
    if fold_of() == 1:
        return [v]
    core, chip, _ = place_of()
    n = v.shape[0] // 8
    return [lax.dynamic_slice_in_dim(v, core * 4 * n + kind * 2 * n + chip * n, n) for kind in range(2)]


def line_total(v):
    fold, step = fold_of(), fold_of()
    while step < lax.axis_size("seq"):
        v = v + lax.ppermute(v, "seq", [(i, i ^ step) for i in range(lax.axis_size("seq"))])
        step *= 2
    return v


def shards_of(v):
    count, step = lax.axis_size("seq"), 1
    held = v[None]
    while step < count:
        held = jnp.concatenate(
            [held, lax.ppermute(held, "seq", [(i, i ^ step) for i in range(count)])], axis=0
        )
        step *= 2
    me = lax.axis_index("seq")
    return jnp.concatenate([lax.dynamic_slice_in_dim(held, me ^ i, 1) for i in range(count)], axis=0)


def pair_rows(v, *after):
    if fold_of() == 1:
        return v
    core = lax.axis_index("head") % 2
    got = tie(swap_pair(pick(v, core)), *after)
    return join(side_of(), v, join(core, got, swap_core(got)))


def my_part(v):
    if fold_of() == 1:
        return v, None
    half = v.shape[0] // 2
    at = side_of()
    return jnp.where(at == 0, v[:half], v[half:]), jnp.where(at == 0, v[half:], v[:half])


def side_parts(masters):
    parts = [my_part(m.astype(bf16)) for m in masters]
    mine = jnp.concatenate([p[0] for p in parts], axis=0)
    if fold_of() == 2:
        away = jnp.concatenate([p[1] for p in parts], axis=0)
        mine = join(side_of(), mine, swap_pair(away), axis=1)
    return mine


def gathered(mine):
    return lax.all_gather(mine, "seq", axis=1, tiled=True, axis_index_groups=lines_of())


def line_scatter(grad):
    return lax.psum_scatter(grad, "seq", scatter_dimension=1, tiled=True, axis_index_groups=lines_of())


def columns_of_sides(summed):
    if fold_of() == 1:
        return [summed.astype(f32)]
    at = side_of()
    mine, other = pick(summed, at, 1), swap_pair(pick(summed, 1 - at, 1))
    return [jnp.where(at == 0, mine, other).astype(f32), jnp.where(at == 0, other, mine).astype(f32)]


def both(sides, lo, hi):
    return jnp.concatenate([s[lo:hi] for s in sides], axis=0)


def states_in(final):
    fold, count = fold_of(), lax.axis_size("seq")
    onward = [(i, i + fold) for i in range(count - fold)]
    bias, move = final[:, :, :VAL], final[:, :, VAL:].astype(bf16)
    state = jnp.zeros_like(bias).astype(bf16)
    for hop in range(count // fold - 1):
        sent = bias if hop == 0 else batched(move, state) + bias
        state = lax.ppermute(sent.astype(bf16), "seq", onward)
    return state, move


def states_back(local, move):
    fold, count = fold_of(), lax.axis_size("seq")
    onward = [(i + fold, i) for i in range(count - fold)]
    state = jnp.zeros_like(local).astype(bf16)
    for hop in range(count // fold - 1):
        sent = local if hop == 0 else batched_t(move, state) + local
        state = lax.ppermute(sent.astype(bf16), "seq", onward)
    return state.astype(f32)


def on_device(
    tokens, cotangent, norm1_gain, w_query, w_key, w_value, w_gate_out, w_alpha, w_beta,
    conv_query, conv_key, conv_value, a_log, dt_bias, out_gain, w_out, norm2_gain, w_gate, w_up, w_down,
):
    fold, side = fold_of(), side_of()
    shards = lax.axis_size("seq")
    model = tokens.shape[1]
    share = model // shards
    all_heads = w_alpha.shape[1]
    heads = all_heads // fold
    hidden = w_gate.shape[1] // fold
    keys, vals = heads * KEY, heads * VAL
    width = 2 * keys + vals
    head_at = lax.axis_index("head") * all_heads + side * heads

    proj_parts = side_parts([w_query.T, w_key.T, w_value.T])
    proj_weight = gathered(proj_parts)
    mid_weight = gathered(side_parts([w_gate_out.T, w_out]))
    gate_weight, out_weight = mid_weight[:vals], mid_weight[vals:]
    mlp_parts = side_parts([w_gate.T, w_up.T, w_down])
    mlp_weight = gathered(mlp_parts)
    mlp_gate, mlp_up, mlp_down = (mlp_weight[i * hidden : (i + 1) * hidden] for i in range(3))
    mlp_in = mlp_weight[: 2 * hidden]

    small = [norm1_gain, norm2_gain, w_alpha, w_beta, conv_query, conv_key, conv_value, a_log, dt_bias, out_gain]
    flat = jnp.concatenate([s.astype(bf16).reshape(-1) for s in small])
    flat = shards_of(jnp.pad(flat, (0, -flat.shape[0] % 1024))).astype(f32)
    parts, at = [], 0
    for s in small:
        parts.append(flat[:, at : at + s.size].reshape((shards,) + s.shape))
        at += s.size
    gain_first, gain_second = parts[0].reshape(-1), parts[1].reshape(-1)
    of_side = lambda v, axis: lax.dynamic_slice_in_dim(v, side * heads, heads, axis)
    mix_weight = jnp.concatenate(
        [of_side(parts[2].reshape(model, all_heads), 1), of_side(parts[3].reshape(model, all_heads), 1)], axis=1
    )
    mix_weight = jnp.pad(mix_weight, ((0, 0), (0, 128 - 2 * heads))).astype(bf16)
    taps = jnp.concatenate(
        [of_side(jnp.moveaxis(p, 0, 2).reshape(4, all_heads, -1), 1).reshape(4, -1) for p in parts[4:7]], axis=1
    )
    taps = jnp.pad(taps, ((0, 4), (0, 0)))
    rate = lax.dynamic_slice_in_dim(parts[7].reshape(-1), head_at, heads)
    bias = lax.dynamic_slice_in_dim(parts[8].reshape(-1), head_at, heads)
    gain_out = parts[9].reshape(1, -1)
    par = jnp.pad(jnp.stack([jnp.exp(rate), bias]), ((0, 6), (0, 128 - heads)))

    inputs = pair_rows(tie(tokens, proj_parts)).astype(f32)
    row_count = inputs.shape[0]
    scale_first = lax.rsqrt(jnp.mean(inputs * inputs, axis=1, keepdims=True) + eps_norm)
    normed_first = (inputs * scale_first * gain_first).astype(bf16)
    proj = dot_right(normed_first, proj_weight).astype(bf16)
    mix_pre = dot_rows(normed_first, mix_weight)
    forward = [(i, i + fold) for i in range(shards - fold)]
    backward = [(i + fold, i) for i in range(shards - fold)]
    edge = lax.ppermute(proj[row_count - HALO :], "seq", forward)
    value_out, ident, inverse, states, final = delta_forward(proj, edge, taps, mix_pre, par)
    gate_pre = dot_right(normed_first, gate_weight)
    entering, move = states_in(final)
    order = unit_order(row_count // UNIT)
    places = jnp.stack(order[0] + order[1] + [order[2]])
    both_cot = pair_rows(tie(cotangent, proj), final)
    both_cot, turned_first = reordered(places, both_cot, normed_first)
    entering = tie(entering, both_cot)
    outputs, gated = gated_outputs(places, value_out, ident, entering, gate_pre, gain_out)
    half = row_count // 2
    attention = summed_rows(chip_sum(dot_rows(gated[half:], out_weight), dot_rows(gated[:half], out_weight)))
    own_inputs = own_blocks(tokens)
    hidden_state = [x.astype(f32) + v.astype(f32) for x, v in zip(own_inputs, attention)]
    scale_second = [lax.rsqrt(jnp.mean(v * v, axis=1, keepdims=True) + eps_norm) for v in hidden_state]
    hat_second = [v * r for v, r in zip(hidden_state, scale_second)]
    normed_second = all_rows([(v * gain_second).astype(bf16) for v in hat_second], (mlp_weight,) if fold == 2 else ())
    act = dot_right(mlp_in, normed_second)
    gate_act, up_act = act[:hidden], act[hidden:]
    sig = jax.nn.sigmoid(gate_act)
    mixed = (gate_act * sig * up_act).astype(bf16)
    grad_mixed = dot_right(mlp_down, both_cot)
    grad_act = jnp.concatenate(
        [grad_mixed * up_act * sig * (1.0 + gate_act * (1.0 - sig)), grad_mixed * (gate_act * sig)], axis=0
    ).astype(bf16)
    mine = chip_sum(dot_left(grad_act[:, half:], mlp_in), dot_left(grad_act[:, :half], mlp_in))
    in_grad = dot_rows(tie(grad_act, mine), normed_second).astype(bf16)
    down_grad = dot_rows(tie(mixed, in_grad), both_cot).astype(bf16)
    in_sum = line_scatter(in_grad)
    down_sum = line_scatter(tie(down_grad, in_sum))
    grad_normed_second = summed_rows(mine, *(((in_grad,), (down_grad,)) if fold == 2 else ()))
    grad_hidden = []
    for d, v, hat, r in zip(own_blocks(cotangent), grad_normed_second, hat_second, scale_second):
        g = v.astype(f32) * gain_second
        grad_hidden.append(d.astype(f32) + r * (g - hat * jnp.mean(g * hat, axis=1, keepdims=True)))
    attention_rounded = [v.astype(bf16) for v in grad_hidden]
    grad_gain_second = jnp.sum(
        mlp_in.astype(f32) * lax.optimization_barrier(in_grad).astype(f32), axis=0
    ) / gain_second
    near_rounded = own_tokens(attention_rounded)
    attention_rounded = tie(all_rows(attention_rounded), in_sum)
    grad_gated = dot_right(attention_rounded, out_weight)
    mixed = tie(mixed, grad_gated)
    branch = summed_rows(chip_sum(dot_left(mixed[:, half:], mlp_down), dot_left(mixed[:, :half], mlp_down)))
    result = own_tokens([(v + w.astype(f32)).astype(bf16) for v, w in zip(hidden_state, branch)])
    grad_outputs, grad_gate, grad_gain_out, local_pull = gate_backward(
        places, grad_gated, outputs, gate_pre, gain_out, ident
    )
    out_grad = dot_left(gated, attention_rounded).astype(bf16)
    gate_grad = dot_left(grad_gate, turned_first).astype(bf16)
    leaving = states_back(local_pull, move)
    leaving = tie(leaving, out_grad, gate_grad, down_sum)
    mid_sum = line_scatter(jnp.concatenate([out_grad, gate_grad], axis=0))
    grad_proj, grad_mix, grad_taps, grad_par, grad_head = delta_backward(
        places, proj, edge, taps, mix_pre, par, grad_outputs, inverse, states, entering, leaving
    )
    following = lax.ppermute(grad_head, "seq", backward)
    fixes = []
    for s in range(3):
        fixes.append(sum(taps[3 - j] * following[s - 3 + j] for j in range(3 - s, 4)))
    at_end = order[1][-1] * UNIT + (1 ^ order[2]) * ROWS + ROWS - HALO
    ending = lax.dynamic_slice_in_dim(grad_proj, at_end, HALO).astype(f32)
    ending = (ending + jnp.pad(jnp.stack(fixes), ((HALO - 3, 0), (0, 0)))).astype(bf16)
    grad_proj = lax.dynamic_update_slice_in_dim(grad_proj, ending, at_end, 0)
    mix_turned = mix_weight.T
    first = lambda lo, hi: (
        dot_rows(grad_proj[lo:hi], proj_weight)
        + dot_rows(grad_gate[lo:hi], gate_weight)
        + dot_rows(grad_mix[lo:hi], mix_turned)
    )
    mine = chip_sum(first(half, row_count), first(0, half))
    proj_grad = dot_left(tie(grad_proj, mine), turned_first).astype(bf16)
    last_sum = line_scatter(tie(proj_grad, mid_sum))
    grad_normed_first = summed_rows(mine, (proj_grad,) if fold == 2 else ())
    grad_taps, grad_par, grad_mix, gate_grad = (
        tie(v, grad_normed_first[0]) for v in (grad_taps, grad_par, grad_mix, gate_grad)
    )
    grad_normed_first = own_tokens(grad_normed_first, last_sum).astype(f32)
    taps_sum = jnp.sum(grad_taps.reshape(4, 8, width), axis=1)
    par_sum = jnp.sum(grad_par.reshape(2, 8, 128), axis=1)
    every = jnp.zeros((2, shards * a_log.shape[0]), f32)
    every = lax.dynamic_update_slice(every, par_sum[:, :heads], (0, head_at))

    def by_shard(lo, like):
        block = taps_sum[:, lo : lo + like.shape[2] * shards * heads].reshape(4, heads, shards, like.shape[2])
        return jnp.moveaxis(block, 2, 0).reshape(shards, -1)

    few = jnp.concatenate(
        [every[0].reshape(shards, -1), every[1].reshape(shards, -1), jnp.sum(grad_gain_out, axis=0).reshape(shards, -1)],
        axis=1,
    )
    few = jnp.pad(few, ((0, 0), (0, share - few.shape[1]))).reshape(1, model)
    of_taps = jnp.concatenate(
        [by_shard(0, conv_query), by_shard(keys, conv_key), by_shard(2 * keys, conv_value)], axis=1
    ).reshape(shards, heads, share)
    of_taps = jnp.moveaxis(of_taps, 1, 0).reshape(heads, model)
    mix_grad = dot_left(grad_mix, turned_first)
    done_grad, done_gate = (tie(proj_grad, grad_mix), gate_grad)
    products = (
        jnp.sum(proj_weight.astype(f32) * done_grad.astype(f32), axis=0)
        + jnp.sum(gate_weight.astype(f32) * done_gate.astype(f32), axis=0)
        + jnp.sum(mix_turned.astype(f32) * mix_grad, axis=0)
    )
    extra = jnp.concatenate(
        [mix_grad[: 2 * heads], of_taps, (products / gain_first)[None], grad_gain_second[None], few], axis=0
    )
    extra = line_total(extra)
    extra_sides = columns_of_sides(lax.dynamic_slice_in_dim(extra, lax.axis_index("seq") // fold * fold * share, fold * share, 1))
    grad_down, grad_mid, grad_last = columns_of_sides(down_sum), columns_of_sides(mid_sum), columns_of_sides(last_sum)
    grad_in = columns_of_sides(in_sum)

    small_at = 2 * heads
    shared = sum(s[small_at + heads : small_at + heads + 3] for s in extra_sides)
    if fold == 2:
        shared = shared + swap_core(shared)
        shared = shared + swap_chip(shared)
    else:
        shared = lax.psum(shared, "head")
    few = shared[2]
    n_rate, n_gain = a_log.shape[0], out_gain.shape[0]
    filters = []
    for like, lo in ((conv_query, 0), (conv_key, 1), (conv_value, 2)):
        n = 4 * heads * like.shape[2]
        start = (0, 4 * heads * conv_query.shape[2], 8 * heads * conv_query.shape[2])[lo]
        filters.append(jnp.concatenate(
            [s[small_at : small_at + heads].reshape(-1)[start : start + n].reshape(4, heads, -1) for s in extra_sides],
            axis=1,
        ))
    own_inputs = tokens.astype(f32)
    own_scale = lax.rsqrt(jnp.mean(own_inputs * own_inputs, axis=1, keepdims=True) + eps_norm)
    own_hat = own_inputs * own_scale
    g = grad_normed_first * gain_first
    grad_tokens = near_rounded.astype(f32) + own_scale * (
        g - own_hat * jnp.mean(g * own_hat, axis=1, keepdims=True)
    )
    return (
        result,
        grad_tokens,
        shared[0],
        both(grad_last, 0, keys).T,
        both(grad_last, keys, 2 * keys).T,
        both(grad_last, 2 * keys, width).T,
        both(grad_mid, vals, 2 * vals).T,
        both(extra_sides, 0, heads).T,
        both(extra_sides, heads, 2 * heads).T,
        filters[0],
        filters[1],
        filters[2],
        few[:n_rate],
        few[n_rate : 2 * n_rate],
        few[2 * n_rate : 2 * n_rate + n_gain],
        both(grad_mid, 0, vals),
        shared[1],
        both(grad_in, 0, hidden).T,
        both(grad_in, hidden, 2 * hidden).T,
        both(grad_down, 0, hidden),
    )


def solution(mesh):
    P = jax.sharding.PartitionSpec
    rows, vector, filters, turned = P("seq", None), P("seq"), P(None, "head", "seq"), P("head", "seq")
    matrix = P("seq", "head")
    placed = (rows, rows, vector) + (matrix,) * 6 + (filters,) * 3 + (vector,) * 3 + (
        turned, vector, matrix, matrix, turned)
    return jax.shard_map(
        on_device, mesh=mesh, in_specs=placed, out_specs=placed, check_vma=False
    )
```

time: 1560 us -> 982 us (0.63)
  waiting for transfers between devices: 1040 us -> 310 us
  other arithmetic: 84.3 us -> 163 us
  starting transfers between devices: 31.8 us -> 80.6 us
  blocking collectives: 40.3 us -> 0 us
  local copies, waits for them, and re-layouts: 49.2 us -> 86.8 us
  Pallas kernels: 99.1 us -> 115 us
    reduce_scatter x5 -> x4, waiting for transfers between devices: 507 us -> 14.9 us  [line_scatter(): lax.psum_scatter(grad, 'seq', scatter_dimension=1, tiled=True, axis_index...]
    all_gather x5 -> x3, waiting for transfers between devices: 288 us -> 18.3 us  [gathered(): lax.all_gather(mine, 'seq', axis=1, tiled=True, axis_index_groups=lines_o...]
    ppermute x14 -> x61, waiting for transfers between devices: 209 us -> 266 us  [the longest x22 140 us: swap_pair(): lax.ppermute(v, 'seq', [(i, i ^ 1) for i in range(lax.axis_size('seq'))])]
    ppermute x14 -> x61, starting transfers between devices: 10.7 us -> 58.6 us  [the longest x22 30.5 us: swap_pair(): lax.ppermute(v, 'seq', [(i, i ^ 1) for i in range(lax.axis_size('seq'))])]
    concatenate x2 -> x32, other arithmetic: 2.31 us -> 39.1 us  [the longest x5 14.6 us: join(): return jnp.concatenate([first, second], axis=axis)]
    all_gather x1 -> x0, blocking collectives: 32.9 us -> none  [on_device(): flat = lax.all_gather(flat, 'seq', axis=0, tiled=False).astype(f32)]
    convert_element_type x16 -> x25, other arithmetic: 22.4 us -> 48.1 us  [the longest x13 26.3 us: plus(): return (a.astype(f32) + b.astype(f32)).astype(bf16)]
    select_n x5 -> x26, other arithmetic: 9.48 us -> 31.6 us  [the longest x16 27.5 us: join(): jnp.where(at == 0, mine, other)]
  transfers between devices with their start and end apart: 33 -> 76, of which waited for: 25 -> 34; matrix products, arithmetic and copies ran while one was open for 15% -> 36% of each run, Pallas kernels for 6% -> 12%
where the time goes in v2:
time: 982 us; the launch traced here: 975 us
  waiting for transfers between devices  310 us (32%)
  matrix products  203 us (21%)
  other arithmetic  163 us (17%)
  Pallas kernels  115 us (12%)
  local copies, waits for them, and re-layouts  86.8 us (9%)
  starting transfers between devices  80.6 us (8%)
  between operations  16.8 us (2%)
    ppermute x22, waiting for transfers between devices, swap_pair(): lax.ppermute(v, 'seq', [(i, i ^ 1) for i in range(lax.axis_size('seq'))])  140 us
    ppermute x18, waiting for transfers between devices, swap_chip(): return lax.ppermute(v, 'head', [(i, i ^ 2) for i in range(4)])  84 us
    dot_general x5, matrix products, dot_right(): lax.dot_general(a, b, (((1,), (1,)), ((), ())), preferred_element_type=f32)  70.3 us
    dot_general x11, matrix products, dot_rows(): lax.dot_general(a, b, (((1,), (0,)), ((), ())), preferred_element_type=f32)  68.2 us
    dot_general x8, matrix products, dot_left(): lax.dot_general(a, b, (((0,), (0,)), ((), ())), preferred_element_type=f32)  60.2 us
    pallas_call x1, Pallas kernels, delta_backward(): pl.pallas_call(functools.partial(backward_kernel, heads), grid_spec=pltpu...  52.4 us
    unnamed x268, local copies, waits for them, and re-layouts  41.4 us
    pallas_call x1, Pallas kernels, delta_forward(): pl.pallas_call(functools.partial(forward_kernel, heads), grid=(blocks,),...  35.1 us
  transfers between devices with their start and end apart: 76, of which 34 were waited for; matrix products, arithmetic and copies ran while one was open for 36% of the time, Pallas kernels for 12%

profile of v2, /device:TPU:0, one launch (start us, length us, event | category | flops | bytes accessed | tf_op | source)
XLA Modules:
  0.0 975.1 jit_solution(7764152613857754482)
XLA Ops:
  16.0 12.0 %collective-permute-done = bf16[1024,256]{1,0:T(8,128)(2,1)} collective-permute-done((bf16[1024,256]{1,0:T(8,128)(2,1)}, bf16[1024,256]{1,0:T(8,128)(2,1)}, u32[]{:S(2)}, u32[]{:S(2)}) %collective-permute-start) | collective-permute-done | bytes 524320 | tf_op jit(solution)/shard_map/ppermute | solution.py:558
  57.6 35.1 %collective-permute-done.1 = bf16[512,2048]{1,0:T(8,128)(2,1)} collective-permute-done((bf16[512,2048]{1,0:T(8,128)(2,1)S(1)}, bf16[512,2048]{1,0:T(8,128)(2,1)}, u32[]{:S(2)}, u32[]{:S(2)}) %collective-permute-start.1) | collective-permute-done | bytes 2097184 | tf_op jit(solution)/shard_map/ppermute | solution.py:558
  109.8 11.3 %fusion.2.refs_1_ = bf16[2048,2048]{1,0:T(8,128)(2,1)} fusion(f32[2048]{0:T(1024)S(1)} %bitcast.166, f32[2048]{0:T(1024)S(1)} %add_rsqrt_fusion, bf16[1024,2048]{1,0:T(8,128)(2,1)S(1)} %get-tuple-element.186, bf16[1024,2048]{1,0:T(8,128)(2,1)S(1)} %get-tuple-element.185), kind=kLoop, calls=%fused_computation.4 | loop fusion | flops 29360128 | bytes 16793600 | tf_op jit(solution)/shard_map/convert_element_type | solution.py:784
  121.1 14.7 %convolution_convert_fusion.5.proj_ref.before_ref = bf16[2048,1024]{1,0:T(8,128)(2,1)} fusion(bf16[2048,2048]{1,0:T(8,128)(2,1)} %fusion.2.refs_1_, bf16[1024,2048]{1,0:T(8,128)(2,1)} %all-gather.4.cloned.1.call-done), kind=kOutput, calls=%fused_computation.49 | convolution fusion | flops 8592031744 | bytes 16777216 | tf_op jit(solution)/shard_map/dot_general | solution.py:529
  150.3 35.1 %shard_map.347 = (f32[2048,512]{1,0:T(8,128)}, bf16[2048,256]{1,0:T(8,128)(2,1)S(1)}, bf16[2048,256]{1,0:T(8,128)(2,1)S(1)}, bf16[16,2,128,384]{3,2,1,0:T(8,128)(2,1)}, f32[2,128,384]{2,1,0:T(8,128)S(1)}) custom-call(bf16[2048,1024]{1,0:T(8,128)(2,1)} %convolution_convert_fusion.5.proj_ref.before_ref, bf16[16,1024]{1,0:T(8,128)(2,1)S(1)} %collective-permute-done.6.edge_ref, ...), custom_call_target="tpu_custom_call" | custom-call | tf_op jit(solution)/shard_map/pallas_call | solution.py:169
  202.0 11.7 %fusion.46.gate_ref = f32[2048,512]{1,0:T(8,128)} fusion(bf16[2048,2048]{1,0:T(8,128)(2,1)} %fusion.2.refs_1_, bf16[1024,2048]{1,0:T(8,128)(2,1)} %all-gather.6.cloned.1.call-done), kind=kOutput, calls=%fused_computation.106 | convolution fusion | flops 4294967296 | bytes 14680064 | tf_op jit(solution)/shard_map/dot_general | solution.py:529
  272.6 21.6 %collective-permute-done.14 = bf16[256,2048]{1,0:T(8,128)(2,1)S(1)} collective-permute-done((bf16[256,2048]{1,0:T(8,128)(2,1)S(1)}, bf16[256,2048]{1,0:T(8,128)(2,1)S(1)}, u32[]{:S(2)}, u32[]{:S(2)}) %collective-permute-start.14) | collective-permute-done | bytes 1048608 | tf_op jit(solution)/shard_map/ppermute | solution.py:558
  318.5 10.0 %collective-permute-done.17 = bf16[128,2048]{1,0:T(8,128)(2,1)S(1)} collective-permute-done((bf16[128,2048]{1,0:T(8,128)(2,1)S(1)}, bf16[128,2048]{1,0:T(8,128)(2,1)S(1)}, u32[]{:S(2)}, u32[]{:S(2)}) %collective-permute-start.17) | collective-permute-done | bytes 524320 | tf_op jit(solution)/shard_map/ppermute | solution.py:562
  329.5 18.3 %all-gather.8.cloned.1.call-done = bf16[2064,2048]{1,0:T(8,128)(2,1)} async-done(((bf16[2064,512]{1,0:T(8,128)(2,1)}), bf16[2064,2048]{1,0:T(8,128)(2,1)}) %all-gather.8.cloned.1.call-update) | async-done | bytes 8454160 | tf_op jit(solution)/shard_map/all_gather | solution.py:695
  354.3 18.8 %collective-permute-done.18 = bf16[256,2048]{1,0:T(8,128)(2,1)S(1)} collective-permute-done((bf16[256,2048]{1,0:T(8,128)(2,1)}, bf16[256,2048]{1,0:T(8,128)(2,1)S(1)}, u32[]{:S(2)}, u32[]{:S(2)}) %collective-permute-start.18) | collective-permute-done | bytes 1048608 | tf_op jit(solution)/shard_map/ppermute | solution.py:558
  386.4 19.4 %fusion.14 = f32[1376,2048]{1,0:T(8,128)} fusion(bf16[2048,2048]{1,0:T(8,128)(2,1)} %constant_dynamic-update-slice_fusion.3, bf16[2064,2048]{1,0:T(8,128)(2,1)} %all-gather.8.cloned.1.call-done), kind=kOutput, calls=%fused_computation.53 | convolution fusion | flops 11542724608 | bytes 25296896 | tf_op jit(solution)/shard_map/dot_general | solution.py:529
  405.8 14.1 %multiply_convert_fusion = (bf16[688,2048]{1,0:T(8,128)(2,1)}, bf16[688,2048]{1,0:T(8,128)(2,1)}, bf16[688,2048]{1,0:T(8,128)(2,1)}) fusion(f32[1376,2048]{1,0:T(8,128)} %fusion.14, bf16[2048,2048]{1,0:T(8,128)(2,1)S(1)} %bitcast.150, bf16[2064,2048]{1,0:T(8,128)(2,1)} %all-gather.8.cloned.1.call-done), kind=kOutput, calls=%fused_computation.30 | convolution fusion | flops 5792497664 | bytes 30932992 | tf_op jit(solution)/shard_map/dot_general | solution.py:529
  419.8 11.6 %convolution_convert_fusion.3 = bf16[1024,2048]{1,0:T(8,128)(2,1)} fusion(bf16[2064,2048]{1,0:T(8,128)(2,1)} %all-gather.8.cloned.1.call-done, bf16[688,2048]{1,0:T(8,128)(2,1)} %get-tuple-element.181, bf16[688,2048]{1,0:T(8,128)(2,1)} %get-tuple-element.180), kind=kOutput, calls=%fused_computation.47 | convolution fusion | flops 5779095552 | bytes 15466496 | tf_op jit(solution)/shard_map/dot_general | solution.py:525
  439.0 10.0 %add_convert_fusion.3 = bf16[1024,2048]{1,0:T(8,128)(2,1)S(1)} fusion(bf16[1024,2048]{1,0:T(8,128)(2,1)} %collective-permute-done.26, bf16[2064,2048]{1,0:T(8,128)(2,1)} %all-gather.8.cloned.1.call-done, bf16[688,2048]{1,0:T(8,128)(2,1)} %get-tuple-element.181, bf16[688,2048]{1,0:T(8,128)(2,1)S(1)} %copy-done.50), kind=kOutput, calls=%fused_computation.22 | convolution fusion | flops 5783289856 | bytes 19660800 | tf_op jit(solution)/shard_map/dot_general | solution.py:525
  455.3 16.0 %convolution_convert_fusion = bf16[1376,2048]{1,0:T(8,128)(2,1)} fusion(bf16[1376,2048]{1,0:T(8,128)(2,1)S(1)} %pad_maximum_fusion.2, bf16[2048,2048]{1,0:T(8,128)(2,1)} %constant_dynamic-update-slice_fusion.3), kind=kOutput, calls=%fused_computation.24 | convolution fusion | flops 11545542656 | bytes 19660800 | tf_op jit(solution)/shard_map/dot_general | solution.py:521
  488.2 10.9 %convolution_convert_fusion.6 = bf16[688,2048]{1,0:T(8,128)(2,1)} fusion(bf16[688,2048]{1,0:T(8,128)(2,1)S(1)} %copy-done.102, bf16[2048,2048]{1,0:T(8,128)(2,1)} %copy-done.11), kind=kOutput, calls=%fused_computation.55 | convolution fusion | flops 5772771328 | bytes 14024704 | tf_op jit(solution)/shard_map/dot_general | solution.py:521
  507.4 11.8 %collective-permute-done.29 = bf16[128,2048]{1,0:T(8,128)(2,1)S(1)} collective-permute-done((bf16[128,2048]{1,0:T(8,128)(2,1)S(1)}, bf16[128,2048]{1,0:T(8,128)(2,1)S(1)}, u32[]{:S(2)}, u32[]{:S(2)}) %collective-permute-start.29) | collective-permute-done | bytes 524320 | tf_op jit(solution)/shard_map/ppermute | solution.py:562
  523.7 20.2 %collective-permute-done.30 = bf16[256,2048]{1,0:T(8,128)(2,1)} collective-permute-done((bf16[256,2048]{1,0:T(8,128)(2,1)}, bf16[256,2048]{1,0:T(8,128)(2,1)}, u32[]{:S(2)}, u32[]{:S(2)}) %collective-permute-start.30) | collective-permute-done | bytes 1048608 | tf_op jit(solution)/shard_map/ppermute | solution.py:558
  549.5 10.3 %collective-permute-done.33 = bf16[128,2048]{1,0:T(8,128)(2,1)S(1)} collective-permute-done((bf16[128,2048]{1,0:T(8,128)(2,1)S(1)}, bf16[128,2048]{1,0:T(8,128)(2,1)S(1)}, u32[]{:S(2)}, u32[]{:S(2)}) %collective-permute-start.33) | collective-permute-done | bytes 524320 | tf_op jit(solution)/shard_map/ppermute | solution.py:558
  566.7 16.3 %collective-permute-done.34 = bf16[256,2048]{1,0:T(8,128)(2,1)} collective-permute-done((bf16[256,2048]{1,0:T(8,128)(2,1)}, bf16[256,2048]{1,0:T(8,128)(2,1)}, u32[]{:S(2)}, u32[]{:S(2)}) %collective-permute-start.34) | collective-permute-done | bytes 1048608 | tf_op jit(solution)/shard_map/ppermute | solution.py:562
  602.6 10.5 %fusion.33.grad_ref = f32[2048,512]{1,0:T(8,128)} fusion(bf16[2048,2048]{1,0:T(8,128)(2,1)} %constant_dynamic-update-slice_fusion.12, bf16[1024,2048]{1,0:T(8,128)(2,1)S(1)} %copy-done.64), kind=kOutput, calls=%fused_computation.93 | convolution fusion | flops 4294967296 | bytes 14680064 | tf_op jit(solution)/shard_map/dot_general | solution.py:529
  620.5 10.2 %shard_map.350 = (bf16[2048,512]{1,0:T(8,128)(2,1)S(1)}, bf16[2048,512]{1,0:T(8,128)(2,1)S(1)}, f32[8,256]{1,0:T(8,128)S(1)}, f32[2,128,256]{2,1,0:T(8,128)S(1)}) custom-call(s32[17]{0:T(128)S(1)} %stack.86.order_ref, f32[2048,512]{1,0:T(8,128)} %fusion.33.grad_ref, f32[2048,512]{1,0:T(8,128)} %get-tuple-element.83.out_ref, f32[2048,512]{1,0:T(8,128)} %fusion.46.gate_ref, ...), custom_call_target="tpu_custom_call" | custom-call | tf_op jit(solution)/shard_map/pallas_call | solution.py:306
  634.0 9.0 convolution_convert_fusion.8
  691.4 52.4 %shard_map.351 = (bf16[2048,1024]{1,0:T(8,128)(2,1)}, bf16[2048,128]{1,0:T(8,128)(2,1)}, f32[32,1024]{1,0:T(8,128)}, f32[16,128]{1,0:T(8,128)}, f32[8,1024]{1,0:T(8,128)}) custom-call(s32[17]{0:T(128)} %copy-done.10, bf16[2048,1024]{1,0:T(8,128)(2,1)} %convolution_convert_fusion.5.proj_ref.before_ref, ...), custom_call_target="tpu_custom_call" | custom-call | tf_op jit(solution)/shard_map/pallas_call | solution.py:476
  762.8 9.9 %collective-permute-done.42 = bf16[256,2048]{1,0:T(8,128)(2,1)S(1)} collective-permute-done((bf16[256,2048]{1,0:T(8,128)(2,1)}, bf16[256,2048]{1,0:T(8,128)(2,1)S(1)}, u32[]{:S(2)}, u32[]{:S(2)}) %collective-permute-start.42) | collective-permute-done | bytes 1048608 | tf_op jit(solution)/shard_map/ppermute | solution.py:562
  791.9 9.2 collective-permute-done.44
  806.8 10.7 %add_convert_fusion = bf16[1024,2048]{1,0:T(8,128)(2,1)} fusion(bf16[1024,2048]{1,0:T(8,128)(2,1)} %collective-permute-done.52, f32[1024,2048]{1,0:T(8,128)S(1)} %fusion.63, f32[1024,2048]{1,0:T(8,128)} %fusion.31, f32[1024,2048]{1,0:T(8,128)} %fusion.44), kind=kLoop, calls=%fused_computation.19 | loop fusion | flops 10485760 | bytes 33554432 | tf_op jit(solution)/shard_map/convert_element_type | solution.py:580
  824.5 10.5 %convolution_convert_fusion.1 = bf16[1024,2048]{1,0:T(8,128)(2,1)} fusion(bf16[2048,1024]{1,0:T(8,128)(2,1)S(1)} %copy-done.96, bf16[2048,2048]{1,0:T(8,128)(2,1)S(1)} %bitcast.146), kind=kOutput, calls=%fused_computation.45 | convolution fusion | flops 8592031744 | bytes 16777216 | tf_op jit(solution)/shard_map/dot_general | solution.py:525
  879.7 10.6 %collective-permute-done.61 = f32[9,2048]{1,0:T(8,128)S(1)} collective-permute-done((f32[9,2048]{1,0:T(8,128)S(1)}, f32[9,2048]{1,0:T(8,128)S(1)}, u32[]{:S(2)}, u32[]{:S(2)}) %collective-permute-start.61) | collective-permute-done | bytes 73760 | tf_op jit(solution)/shard_map/ppermute | solution.py:652
  903.7 14.9 %reduce-scatter.11.cloned.1.call-done = bf16[1024,512]{1,0:T(8,128)(2,1)} async-done(((bf16[1024,2048]{1,0:T(8,128)(2,1)}), bf16[1024,512]{1,0:T(8,128)(2,1)}) %reduce-scatter.11.cloned.1.call-update) | async-done | bytes 1048592 | tf_op jit(solution)/shard_map/reduce_scatter | solution.py:699
  922.3 11.4 %collective-permute-done.65 = bf16[1024,256]{1,0:T(8,128)(2,1)S(1)} collective-permute-done((bf16[1024,256]{1,0:T(8,128)(2,1)S(1)}, bf16[1024,256]{1,0:T(8,128)(2,1)S(1)}, u32[]{:S(2)}, u32[]{:S(2)}) %collective-permute-start.65) | collective-permute-done | bytes 524320 | tf_op jit(solution)/shard_map/ppermute | solution.py:558
  958.5 9.3 fusion.8
  (673 shorter events, 460.6 us)
Async XLA Ops:
  7.2 113.9 %all-gather.4.cloned.1.call-start = ((), (), s32[]{:S(2)}) async-start(), calls=%async_computation.4 | async-start | bytes 5242880 | tf_op jit(solution)/shard_map/all_gather | solution.py:695
  30.5 171.5 %all-gather.6.cloned.1.call-start = ((), (), s32[]{:S(2)}) async-start(), calls=%async_computation.5 | async-start | bytes 5242880 | tf_op jit(solution)/shard_map/all_gather | solution.py:695
  32.2 66.9 %collective-permute-start.12 = (bf16[1024,256]{1,0:T(8,128)(2,1)}, bf16[1024,256]{1,0:T(8,128)(2,1)}, u32[]{:S(2)}, u32[]{:S(2)}) collective-permute-start(bf16[1024,256]{1,0:T(8,128)(2,1)} %pad_maximum_fusion.30), channel_id=1, source_target_pairs={{0,4},{4,0},{8,12},{12,8},{16,20},{20,16},{24,28},{28,24},{1,5},{5... | collective-permute-start | bytes 1572872 | tf_op jit(solution)/shard_map/ppermute | solution.py:558
  37.3 55.4 %collective-permute-start.1 = (bf16[512,2048]{1,0:T(8,128)(2,1)S(1)}, bf16[512,2048]{1,0:T(8,128)(2,1)}, u32[]{:S(2)}, u32[]{:S(2)}) collective-permute-start(bf16[512,2048]{1,0:T(8,128)(2,1)S(1)} %constant_dynamic-slice_fusion.18), channel_id=1, source_target_pairs={{0,4},{4,0},{8,12},{12,8},{16,20},{20,16},{24,28},{28,24},{1,5},{5... | collective-permute-start | bytes 6291464 | tf_op jit(solution)/shard_map/ppermute | solution.py:558
  51.9 40.8 %collective-permute-start.5 = (bf16[4,4096]{1,0:T(4,128)(2,1)S(1)}, bf16[4,4096]{1,0:T(4,128)(2,1)S(1)}, u32[]{:S(2)}, u32[]{:S(2)}) collective-permute-start(bf16[4,4096]{1,0:T(4,128)(2,1)S(1)} %pad_maximum_fusion.32), channel_id=1, source_target_pairs={{0,16},{4,20},{8,24},{12,28},{16,0},{20,4},{24,8},{28,12},{1,17},{... | collective-permute-start | bytes 98312 | tf_op jit(solution)/shard_map/ppermute | solution.py:662
  55.9 129.5 %collective-permute-start.16 = (bf16[2064,256]{1,0:T(8,128)(2,1)}, bf16[2064,256]{1,0:T(8,128)(2,1)}, u32[]{:S(2)}, u32[]{:S(2)}) collective-permute-start(bf16[2064,256]{1,0:T(8,128)(2,1)} %pad_maximum_fusion.15), channel_id=1, source_target_pairs={{0,4},{4,0},{8,12},{12,8},{16,20},{20,16},{24,28},{28,24},{1,5},{5... | collective-permute-start | bytes 3170312 | tf_op jit(solution)/shard_map/ppermute | solution.py:558
  101.5 246.4 %all-gather.8.cloned.1.call-start = ((), (), s32[]{:S(2)}) async-start(), calls=%async_computation.6 | async-start | bytes 10567680 | tf_op jit(solution)/shard_map/all_gather | solution.py:695
  136.1 49.3 %collective-permute-start.10 = (bf16[512,2048]{1,0:T(8,128)(2,1)S(1)}, bf16[512,2048]{1,0:T(8,128)(2,1)}, u32[]{:S(2)}, u32[]{:S(2)}) collective-permute-start(bf16[512,2048]{1,0:T(8,128)(2,1)S(1)} %constant_dynamic-slice_fusion.5), channel_id=1, source_target_pairs={{0,4},{4,0},{8,12},{12,8},{16,20},{20,16},{24,28},{28,24},{1,5},{5... | collective-permute-start | bytes 6291464 | tf_op jit(solution)/shard_map/ppermute | solution.py:558
  185.4 32.6 %collective-permute-start.11 = (bf16[512,2048]{1,0:T(8,128)(2,1)}, bf16[512,2048]{1,0:T(8,128)(2,1)S(1)}, u32[]{:S(2)}, u32[]{:S(2)}) collective-permute-start(bf16[512,2048]{1,0:T(8,128)(2,1)} %collective-permute-done.10), channel_id=1, source_target_pairs={{0,1},{1,0},{2,3},{3,2},{4,5},{5,4},{6,7},{7,6},{8,9},{9,8},{10,11... | collective-permute-start | bytes 6291464 | tf_op jit(solution)/shard_map/ppermute | solution.py:566
  193.9 405.3 %reduce-scatter.5.cloned.1.call-start = ((), (), s32[]{:S(2)}) async-start(), calls=%async_computation.7 | async-start | bytes 7045120 | tf_op jit(solution)/shard_map/reduce_scatter | solution.py:699
  215.4 32.4 %collective-permute-start.9 = (bf16[2,128,256]{2,1,0:T(8,128)(2,1)}, bf16[2,128,256]{2,1,0:T(8,128)(2,1)S(1)}, u32[]{:S(2)}, u32[]{:S(2)}) collective-permute-start(bf16[2,128,256]{2,1,0:T(8,128)(2,1)} %fusion.49), channel_id=1, source_target_pairs={{0,8},{4,12},{8,16},{12,20},{16,24},{20,28},{1,9},{5,13},{9,17},{1... | collective-permute-start | bytes 393224 | tf_op jit(solution)/shard_map/ppermute | solution.py:721
  268.8 25.4 %collective-permute-start.14 = (bf16[256,2048]{1,0:T(8,128)(2,1)S(1)}, bf16[256,2048]{1,0:T(8,128)(2,1)S(1)}, u32[]{:S(2)}, u32[]{:S(2)}) collective-permute-start(bf16[256,2048]{1,0:T(8,128)(2,1)S(1)} %slice.640), channel_id=1, source_target_pairs={{0,4},{4,0},{8,12},{12,8},{16,20},{20,16},{24,28},{28,24},{1,5},{5... | collective-permute-start | bytes 3145736 | tf_op jit(solution)/shard_map/ppermute | solution.py:558
  271.1 26.3 %collective-permute-start.19 = (bf16[256,2048]{1,0:T(8,128)(2,1)S(1)}, bf16[256,2048]{1,0:T(8,128)(2,1)S(1)}, u32[]{:S(2)}, u32[]{:S(2)}) collective-permute-start(bf16[256,2048]{1,0:T(8,128)(2,1)S(1)} %pad_maximum_fusion.19), channel_id=1, source_target_pairs={{0,2},{1,3},{2,0},{3,1},{4,6},{5,7},{6,4},{7,5},{8,10},{9,11},{10,... | collective-permute-start | bytes 3145736 | tf_op jit(solution)/shard_map/ppermute | solution.py:562
  316.8 32.5 %collective-permute-start.21 = (bf16[128,2048]{1,0:T(8,128)(2,1)S(1)}, bf16[128,2048]{1,0:T(8,128)(2,1)}, u32[]{:S(2)}, u32[]{:S(2)}) collective-permute-start(bf16[128,2048]{1,0:T(8,128)(2,1)S(1)} %get-tuple-element.187), channel_id=1, source_target_pairs={{0,4},{4,0},{8,12},{12,8},{16,20},{20,16},{24,28},{28,24},{1,5},{5... | collective-permute-start | bytes 1572872 | tf_op jit(solution)/shard_map/ppermute | solution.py:558
  452.5 25.5 %collective-permute-start.31 = (bf16[256,2048]{1,0:T(8,128)(2,1)}, bf16[256,2048]{1,0:T(8,128)(2,1)}, u32[]{:S(2)}, u32[]{:S(2)}) collective-permute-start(bf16[256,2048]{1,0:T(8,128)(2,1)} %pad_maximum_fusion.22), channel_id=1, source_target_pairs={{0,2},{1,3},{2,0},{3,1},{4,6},{5,7},{6,4},{7,5},{8,10},{9,11},{10,... | collective-permute-start | bytes 3145736 | tf_op jit(solution)/shard_map/ppermute | solution.py:562
  454.0 29.0 %collective-permute-start.27 = (bf16[256,2048]{1,0:T(8,128)(2,1)}, bf16[256,2048]{1,0:T(8,128)(2,1)}, u32[]{:S(2)}, u32[]{:S(2)}) collective-permute-start(bf16[256,2048]{1,0:T(8,128)(2,1)} %slice.667), channel_id=1, source_target_pairs={{0,4},{4,0},{8,12},{12,8},{16,20},{20,16},{24,28},{28,24},{1,5},{5... | collective-permute-start | bytes 3145736 | tf_op jit(solution)/shard_map/ppermute | solution.py:558
  471.3 220.1 %reduce-scatter.7.cloned.1.call-start = ((), (), s32[]{:S(2)}) async-start(), calls=%async_computation.8 | async-start | bytes 3522560 | tf_op jit(solution)/shard_map/reduce_scatter | solution.py:699
  563.1 31.4 %collective-permute-start.35 = (bf16[256,2048]{1,0:T(8,128)(2,1)}, bf16[256,2048]{1,0:T(8,128)(2,1)S(1)}, u32[]{:S(2)}, u32[]{:S(2)}) collective-permute-start(bf16[256,2048]{1,0:T(8,128)(2,1)} %pad_maximum_fusion.21), channel_id=1, source_target_pairs={{0,1},{1,0},{2,3},{3,2},{4,5},{5,4},{6,7},{7,6},{8,9},{9,8},{10,11... | collective-permute-start | bytes 3145736 | tf_op jit(solution)/shard_map/ppermute | solution.py:566
  563.2 32.4 %collective-permute-start.36 = (bf16[256,2048]{1,0:T(8,128)(2,1)}, bf16[256,2048]{1,0:T(8,128)(2,1)S(1)}, u32[]{:S(2)}, u32[]{:S(2)}) collective-permute-start(bf16[256,2048]{1,0:T(8,128)(2,1)} %collective-permute-done.30), channel_id=1, source_target_pairs={{0,1},{1,0},{2,3},{3,2},{4,5},{5,4},{6,7},{7,6},{8,9},{9,8},{10,11... | collective-permute-start | bytes 3145736 | tf_op jit(solution)/shard_map/ppermute | solution.py:566
  566.6 30.0 %collective-permute-start.47 = (bf16[512,2048]{1,0:T(8,128)(2,1)S(1)}, bf16[512,2048]{1,0:T(8,128)(2,1)S(1)}, u32[]{:S(2)}, u32[]{:S(2)}) collective-permute-start(bf16[512,2048]{1,0:T(8,128)(2,1)S(1)} %pad_maximum_fusion.12), channel_id=1, source_target_pairs={{0,1},{1,0},{2,3},{3,2},{4,5},{5,4},{6,7},{7,6},{8,9},{9,8},{10,11... | collective-permute-start | bytes 6291464 | tf_op jit(solution)/shard_map/ppermute | solution.py:566
  599.3 235.8 %reduce-scatter.9.cloned.1.call-start = ((), (), s32[]{:S(2)}) async-start(), calls=%async_computation.9 | async-start | bytes 5242880 | tf_op jit(solution)/shard_map/reduce_scatter | solution.py:699
  620.0 61.5 %collective-permute-start.38 = (bf16[1024,2048]{1,0:T(8,128)(2,1)}, bf16[1024,2048]{1,0:T(8,128)(2,1)}, u32[]{:S(2)}, u32[]{:S(2)}) collective-permute-start(bf16[1024,2048]{1,0:T(8,128)(2,1)} %convolution_convert_fusion.2), channel_id=1, source_target_pairs={{0,1},{1,0},{2,3},{3,2},{4,5},{5,4},{6,7},{7,6},{8,9},{9,8},{10,11... | collective-permute-start | bytes 12582920 | tf_op jit(solution)/shard_map/ppermute | solution.py:566
  633.0 44.3 %collective-permute-start.67 = (bf16[1376,256]{1,0:T(8,128)(2,1)}, bf16[1376,256]{1,0:T(8,128)(2,1)}, u32[]{:S(2)}, u32[]{:S(2)}) collective-permute-start(bf16[1376,256]{1,0:T(8,128)(2,1)} %constant_dynamic-slice_fusion.1), channel_id=1, source_target_pairs={{0,4},{4,0},{8,12},{12,8},{16,20},{20,16},{24,28},{28,24},{1,5},{5... | collective-permute-start | bytes 2113544 | tf_op jit(solution)/shard_map/ppermute | solution.py:558
  651.8 266.9 %reduce-scatter.11.cloned.1.call-start = ((), (), s32[]{:S(2)}) async-start(), calls=%async_computation.10 | async-start | bytes 5242880 | tf_op jit(solution)/shard_map/reduce_scatter | solution.py:699
  690.3 70.7 %collective-permute-start.39 = (bf16[256,2048]{1,0:T(8,128)(2,1)}, bf16[256,2048]{1,0:T(8,128)(2,1)S(1)}, u32[]{:S(2)}, u32[]{:S(2)}) collective-permute-start(bf16[256,2048]{1,0:T(8,128)(2,1)} %slice.675), channel_id=1, source_target_pairs={{0,4},{4,0},{8,12},{12,8},{16,20},{20,16},{24,28},{28,24},{1,5},{5... | collective-permute-start | bytes 3145736 | tf_op jit(solution)/shard_map/ppermute | solution.py:558
  746.3 26.3 %collective-permute-start.42 = (bf16[256,2048]{1,0:T(8,128)(2,1)}, bf16[256,2048]{1,0:T(8,128)(2,1)S(1)}, u32[]{:S(2)}, u32[]{:S(2)}) collective-permute-start(bf16[256,2048]{1,0:T(8,128)(2,1)} %pad_maximum_fusion.24), channel_id=1, source_target_pairs={{0,2},{1,3},{2,0},{3,1},{4,6},{5,7},{6,4},{7,5},{8,10},{9,11},{10,... | collective-permute-start | bytes 3145736 | tf_op jit(solution)/shard_map/ppermute | solution.py:562
  760.9 45.9 %collective-permute-start.52 = (bf16[1024,2048]{1,0:T(8,128)(2,1)}, bf16[1024,2048]{1,0:T(8,128)(2,1)}, u32[]{:S(2)}, u32[]{:S(2)}) collective-permute-start(bf16[1024,2048]{1,0:T(8,128)(2,1)} %add_convert_fusion.1), channel_id=1, source_target_pairs={{0,1},{1,0},{2,3},{3,2},{4,5},{5,4},{6,7},{7,6},{8,9},{9,8},{10,11... | collective-permute-start | bytes 12582920 | tf_op jit(solution)/shard_map/ppermute | solution.py:566
  836.5 29.2 %collective-permute-start.45 = (bf16[512,2048]{1,0:T(8,128)(2,1)}, bf16[512,2048]{1,0:T(8,128)(2,1)}, u32[]{:S(2)}, u32[]{:S(2)}) collective-permute-start(bf16[512,2048]{1,0:T(8,128)(2,1)} %pad_maximum_fusion.11), channel_id=1, source_target_pairs={{0,1},{1,0},{2,3},{3,2},{4,5},{5,4},{6,7},{7,6},{8,9},{9,8},{10,11... | collective-permute-start | bytes 6291464 | tf_op jit(solution)/shard_map/ppermute | solution.py:566
  846.2 76.2 %collective-permute-start.66 = (bf16[1024,256]{1,0:T(8,128)(2,1)}, bf16[1024,256]{1,0:T(8,128)(2,1)}, u32[]{:S(2)}, u32[]{:S(2)}) collective-permute-start(bf16[1024,256]{1,0:T(8,128)(2,1)} %constant_dynamic-slice_fusion.2), channel_id=1, source_target_pairs={{0,4},{4,0},{8,12},{12,8},{16,20},{20,16},{24,28},{28,24},{1,5},{5... | collective-permute-start | bytes 1572872 | tf_op jit(solution)/shard_map/ppermute | solution.py:558
  848.7 43.2 %collective-permute-start.57 = (bf16[128,2048]{1,0:T(8,128)(2,1)}, bf16[128,2048]{1,0:T(8,128)(2,1)}, u32[]{:S(2)}, u32[]{:S(2)}) collective-permute-start(bf16[128,2048]{1,0:T(8,128)(2,1)} %slice.570), channel_id=1, source_target_pairs={{0,4},{4,0},{8,12},{12,8},{16,20},{20,16},{24,28},{28,24},{1,5},{5... | collective-permute-start | bytes 1572872 | tf_op jit(solution)/shard_map/ppermute | solution.py:558
  878.0 43.4 %collective-permute-start.55 = (bf16[128,2048]{1,0:T(8,128)(2,1)S(1)}, bf16[128,2048]{1,0:T(8,128)(2,1)S(1)}, u32[]{:S(2)}, u32[]{:S(2)}) collective-permute-start(bf16[128,2048]{1,0:T(8,128)(2,1)S(1)} %copy-done.52), channel_id=1, source_target_pairs={{0,2},{1,3},{2,0},{3,1},{4,6},{5,7},{6,4},{7,5},{8,10},{9,11},{10,... | collective-permute-start | bytes 1572872 | tf_op jit(solution)/shard_map/ppermute | solution.py:562
  921.7 30.6 %collective-permute-start.59 = (bf16[512,2048]{1,0:T(8,128)(2,1)S(1)}, bf16[512,2048]{1,0:T(8,128)(2,1)}, u32[]{:S(2)}, u32[]{:S(2)}) collective-permute-start(bf16[512,2048]{1,0:T(8,128)(2,1)S(1)} %pad_maximum_fusion.13), channel_id=1, source_target_pairs={{0,1},{1,0},{2,3},{3,2},{4,5},{5,4},{6,7},{7,6},{8,9},{9,8},{10,11... | collective-permute-start | bytes 6291464 | tf_op jit(solution)/shard_map/ppermute | solution.py:566
  (161 other events, 2890.2 us)
Sparse Core Ops, SparseCore 0:
  30.7 83.6 all-gather.3
  116.5 79.1 all-gather.5
  197.2 150.5 all-gather.7
  471.4 99.3 reduce-scatter.4
  599.4 57.5 reduce-scatter.6
  659.2 79.3 reduce-scatter.8
  835.2 83.4 reduce-scatter.10

commit v3 on v2

--- a/solution.py
+++ b/solution.py
@@ -334,9 +334,9 @@
     )(order, grad_gated, outputs, gate_pre, gain, ident)
 
 
-def backward_kernel(heads, order_ref, proj_ref, before_ref, edge_ref, taps_ref, ab_ref, par_ref, dout_ref,
+def backward_kernel(heads, order_ref, gate_ref, proj_ref, before_ref, edge_ref, taps_ref, ab_ref, par_ref, dout_ref,
                     inv_ref, state_ref, enter_ref, dfinal_ref,
-                    dproj_ref, dab_ref, dtaps_ref, dpar_ref, dhead_ref,
+                    dproj_ref, dtaps_ref, dpar_ref, dhead_ref,
                     xs_ref, gs_ref, ds_ref):
     step = pl.program_id(0)
     last = pl.num_programs(0) - 1
@@ -440,7 +440,7 @@
 
         dlog = mm_full((rows <= cols).astype(f32), drunning)
         dalpha = -dlog * par[0:1, :] * sigmoid(ab + par[1:2, :])
-        dab_ref[placed_rows(order_ref, s), :] = jnp.where(lane < heads, dalpha, dbeta).astype(bf16)
+        dproj_ref[placed_rows(order_ref, s), width + heads * VAL :] = jnp.where(lane < heads, dalpha, dbeta).astype(bf16)
         dpar_ref[0:8, :] += jnp.sum((dlog * log_decay).reshape(-1, 8, 128), axis=0)
         dpar_ref[8:16, :] += jnp.sum(dalpha.reshape(-1, 8, 128), axis=0)
 
@@ -457,12 +457,14 @@
         for s in range(2):
             dproj_ref[placed_rows(order_ref, s), lanes] = total[s * ROWS : (s + 1) * ROWS]
 
+    dproj_ref[:, width : width + heads * VAL] = gate_ref[...]
+
     @pl.when(step == last)
     def _():
         dhead_ref[...] = gs_ref[0:8, :]
 
 
-def delta_backward(order, proj, edge, taps, ab, par, dout, inverse, states, entering, dfinal):
+def delta_backward(order, dgate, proj, edge, taps, ab, par, dout, inverse, states, entering, dfinal):
     tokens, width = proj.shape
     heads = width // (2 * KEY + VAL)
     keys, vals = heads * KEY, heads * VAL
@@ -479,6 +481,7 @@
             num_scalar_prefetch=1,
             grid=(blocks,),
             in_specs=[
+                sent(vals),
                 rev(width),
                 pl.BlockSpec((HALO, width), lambda c, order: (jnp.maximum((blocks - 1 - c) * per - 1, 0), 0)),
                 whole(HALO, width),
@@ -492,8 +495,7 @@
                 whole(heads, KEY, VAL),
             ],
             out_specs=[
-                sent(width),
-                sent(128),
+                sent(width + vals + 128),
                 whole(32, width),
                 whole(16, 128),
                 whole(8, width),
@@ -505,8 +507,7 @@
             ],
         ),
         out_shape=[
-            jax.ShapeDtypeStruct((tokens, width), bf16),
-            jax.ShapeDtypeStruct((tokens, 128), bf16),
+            jax.ShapeDtypeStruct((tokens, width + vals + 128), bf16),
             jax.ShapeDtypeStruct((32, width), f32),
             jax.ShapeDtypeStruct((16, 128), f32),
             jax.ShapeDtypeStruct((8, width), f32),
@@ -514,7 +515,32 @@
         compiler_params=pltpu.CompilerParams(
             dimension_semantics=("arbitrary",), vmem_limit_bytes=56 * 2**20
         ),
-    )(order, proj, proj, edge, taps, ab, par, dout, inverse, states, entering, dfinal)
+    )(order, dgate, proj, proj, edge, taps, ab, par, dout, inverse, states, entering, dfinal)
+
+
+def assemble_kernel(parts, *refs):
+    out_ref, sems = refs[-2], refs[-1]
+    copies, at = [], 0
+    for i, (which, start, rows) in enumerate(parts):
+        copies.append(pltpu.make_async_copy(
+            refs[which].at[pl.ds(start, rows)], out_ref.at[pl.ds(at, rows)], sems.at[i]))
+        at += rows
+    for copy in copies:
+        copy.start()
+    for copy in copies:
+        copy.wait()
+
+
+def assembled(pieces, parts):
+    rows = sum(p[2] for p in parts)
+    return pl.pallas_call(
+        functools.partial(assemble_kernel, parts),
+        in_specs=[pl.BlockSpec(memory_space=pltpu.VMEM)] * len(pieces),
+        out_specs=pl.BlockSpec(memory_space=pl.ANY),
+        out_shape=jax.ShapeDtypeStruct((rows,) + pieces[0].shape[1:], pieces[0].dtype),
+        scratch_shapes=[pltpu.SemaphoreType.DMA((len(parts),))],
+        compiler_params=pltpu.CompilerParams(vmem_limit_bytes=32 * 2**20),
+    )(*pieces)
 
 
 def dot_rows(a, b):
@@ -599,42 +625,78 @@
 def chip_sum(away, near):
     if fold_of() == 1:
         return jnp.concatenate([near, away], axis=0).astype(bf16)
-    return plus(near, swap_core(away.astype(bf16)))
-
-
-def summed_rows(mine, beside=(), later=()):
-    if fold_of() == 1:
-        return [lax.psum(mine, "head")]
+    return plus(lax.optimization_barrier(near.astype(bf16)), swap_core(away.astype(bf16)))
+
+
+def together(*arrays):
+    return lax.optimization_barrier(arrays)
+
+
+def first_exchange(mine):
+    if fold_of() == 1:
+        return (mine,)
     n = mine.shape[0] // 8
     blocks = [mine[i * n : (i + 1) * n] for i in range(8)]
-    a = plus(mine[: 2 * n], swap_pair(mine[2 * n : 4 * n]))
     keep, give = (jnp.concatenate([blocks[4 + i], blocks[6 + i]], axis=0) for i in range(2))
-    b = plus(keep, swap_chip(give))
-    a, b = tie(a, *beside), tie(b, *beside)
-    a, b = plus(a[:n], swap_chip(a[n:])), plus(b[:n], swap_pair(b[n:]))
-    return [tie(a, *later), tie(b, *later)]
-
-
-def all_rows(pieces, beside=()):
-    if fold_of() == 1:
-        return pieces[0]
+    by_x, by_y = together(mine[2 * n : 4 * n], give)
+    return mine[: 2 * n], keep, swap_pair(by_x), swap_chip(by_y)
+
+
+def first_total(parts, *beside):
+    if fold_of() == 1:
+        return parts
+    a, b, far_a, far_b = together(*parts, *beside)[:4]
+    return together(plus(a, far_a), plus(b, far_b))
+
+
+def second_exchange(parts):
+    if fold_of() == 1:
+        return parts
+    a, b = parts
+    n = a.shape[0] // 2
+    return a[:n], b[:n], swap_chip(a[n:]), swap_pair(b[n:])
+
+
+def second_total(parts, *beside):
+    if fold_of() == 1:
+        return [lax.psum(parts[0], "head")]
+    a, b, far_a, far_b = together(*parts, *beside)[:4]
+    return list(together(plus(a, far_a), plus(b, far_b)))
+
+
+def all_rows(pieces, beside=(), work=None):
+    if fold_of() == 1:
+        return pieces[0], () if work is None else work(pieces[0])
+    a, b = together(*pieces)
+    far_a, far_b = together(swap_chip(a), swap_pair(b), *beside)[:2]
+    a, b = together(jnp.concatenate([a, far_a], axis=0), jnp.concatenate([b, far_b], axis=0))
+    done = () if work is None else work(a)
+    far_a, far_b, *done = together(swap_pair(a), swap_chip(b), *done)
+    n = far_b.shape[0] // 2
+    near = together(a, far_a, b, far_b)
+    far = together(*(swap_core(v) for v in near))
+    parts = []
+    for at in (0, 4):
+        parts += [(at, 0, 2 * n), (at + 1, 0, 2 * n)]
+        parts += [(at + 2, 0, n), (at + 3, 0, n), (at + 2, n, n), (at + 3, n, n)]
+    return assembled(near + far, tuple(parts)), tuple(done)
+
+
+def chip_rows(pieces):
+    if fold_of() == 1:
+        return pieces
     a, b = pieces
-    a = jnp.concatenate([a, swap_chip(a)], axis=0)
-    b = jnp.concatenate([b, swap_pair(b)], axis=0)
-    a, b = tie(a, *beside), tie(b, *beside)
-    far = swap_chip(b)
-    n = far.shape[0] // 2
-    b = jnp.concatenate([b[:n], far[:n], b[n:], far[n:]], axis=0)
-    near = [a, swap_pair(a), b]
-    return jnp.concatenate(near + [swap_core(v) for v in near], axis=0)
-
-
-def own_tokens(pieces, *beside):
-    if fold_of() == 1:
-        return pieces[0]
+    both_here = jnp.concatenate([a, b], axis=0)
+    return both_here, swap_chip(both_here)
+
+
+def own_tokens(parts, *beside):
+    if fold_of() == 1:
+        return parts[0]
     core, chip, _ = place_of()
-    near = jnp.concatenate([join(chip, v, swap_chip(v)) for v in pieces], axis=0)
-    near = tie(near, *beside)
+    here, far = together(*parts, *beside)[:2]
+    n = here.shape[0] // 2
+    near = jnp.concatenate([join(chip, here[:n], far[:n]), join(chip, here[n:], far[n:])], axis=0)
     return join(core, near, swap_core(near))
 
 
@@ -695,15 +757,19 @@
     return lax.all_gather(mine, "seq", axis=1, tiled=True, axis_index_groups=lines_of())
 
 
-def line_scatter(grad):
-    return lax.psum_scatter(grad, "seq", scatter_dimension=1, tiled=True, axis_index_groups=lines_of())
-
-
-def columns_of_sides(summed):
+def line_scatter(grad, axis=1):
+    return lax.psum_scatter(grad, "seq", scatter_dimension=axis, tiled=True, axis_index_groups=lines_of())
+
+
+def swapped_share(summed, axis=1):
+    return swap_pair(pick(summed, 1 - side_of(), axis)) if fold_of() == 2 else None
+
+
+def in_sides(summed, other, axis=1):
     if fold_of() == 1:
         return [summed.astype(f32)]
     at = side_of()
-    mine, other = pick(summed, at, 1), swap_pair(pick(summed, 1 - at, 1))
+    mine = pick(summed, at, axis)
     return [jnp.where(at == 0, mine, other).astype(f32), jnp.where(at == 0, other, mine).astype(f32)]
 
 
@@ -719,17 +785,21 @@
     for hop in range(count // fold - 1):
         sent = bias if hop == 0 else batched(move, state) + bias
         state = lax.ppermute(sent.astype(bf16), "seq", onward)
-    return state, move
-
-
-def states_back(local, move):
+    return state, jnp.swapaxes(move, 1, 2)
+
+
+def states_back(local, turned, works):
     fold, count = fold_of(), lax.axis_size("seq")
     onward = [(i + fold, i) for i in range(count - fold)]
-    state = jnp.zeros_like(local).astype(bf16)
+    sent, carried = local.astype(bf16), ()
     for hop in range(count // fold - 1):
-        sent = local if hop == 0 else batched_t(move, state) + local
-        state = lax.ppermute(sent.astype(bf16), "seq", onward)
-    return state.astype(f32)
+        if hop:
+            sent = (batched(turned, state) + local).astype(bf16)
+        state = lax.ppermute(sent, "seq", onward)
+        if hop < len(works):
+            carried = works[hop](sent, carried)
+        state, *carried = together(state, *carried)
+    return state.astype(f32), carried
 
 
 def on_device(
@@ -794,15 +864,20 @@
     places = jnp.stack(order[0] + order[1] + [order[2]])
     both_cot = pair_rows(tie(cotangent, proj), final)
     both_cot, turned_first = reordered(places, both_cot, normed_first)
+    mix_turned = mix_weight.T
+    side_weight = jnp.concatenate(
+        [tie(proj_weight, both_cot), tie(gate_weight, both_cot), tie(mix_turned, both_cot)], axis=0
+    )
     entering = tie(entering, both_cot)
     outputs, gated = gated_outputs(places, value_out, ident, entering, gate_pre, gain_out)
     half = row_count // 2
-    attention = summed_rows(chip_sum(dot_rows(gated[half:], out_weight), dot_rows(gated[:half], out_weight)))
+    mine = chip_sum(dot_rows(gated[half:], out_weight), dot_rows(gated[:half], out_weight))
+    attention = second_total(second_exchange(first_total(first_exchange(mine))))
     own_inputs = own_blocks(tokens)
     hidden_state = [x.astype(f32) + v.astype(f32) for x, v in zip(own_inputs, attention)]
     scale_second = [lax.rsqrt(jnp.mean(v * v, axis=1, keepdims=True) + eps_norm) for v in hidden_state]
     hat_second = [v * r for v, r in zip(hidden_state, scale_second)]
-    normed_second = all_rows([(v * gain_second).astype(bf16) for v in hat_second], (mlp_weight,) if fold == 2 else ())
+    normed_second, _ = all_rows([(v * gain_second).astype(bf16) for v in hat_second], (mlp_weight,))
     act = dot_right(mlp_in, normed_second)
     gate_act, up_act = act[:hidden], act[hidden:]
     sig = jax.nn.sigmoid(gate_act)
@@ -812,136 +887,166 @@
         [grad_mixed * up_act * sig * (1.0 + gate_act * (1.0 - sig)), grad_mixed * (gate_act * sig)], axis=0
     ).astype(bf16)
     mine = chip_sum(dot_left(grad_act[:, half:], mlp_in), dot_left(grad_act[:, :half], mlp_in))
-    in_grad = dot_rows(tie(grad_act, mine), normed_second).astype(bf16)
-    down_grad = dot_rows(tie(mixed, in_grad), both_cot).astype(bf16)
-    in_sum = line_scatter(in_grad)
-    down_sum = line_scatter(tie(down_grad, in_sum))
-    grad_normed_second = summed_rows(mine, *(((in_grad,), (down_grad,)) if fold == 2 else ()))
+    down_grad = dot_rows(tie(mixed, mine), both_cot).astype(bf16)
+    in_grad = dot_rows(tie(grad_act, down_grad), normed_second).astype(bf16)
+    down_sum = line_scatter(down_grad)
+    in_sum = line_scatter(tie(in_grad, down_sum))
+    grad_normed_second = first_total(first_exchange(mine), down_grad, in_grad)
+    grad_normed_second = second_total(second_exchange(grad_normed_second))
     grad_hidden = []
     for d, v, hat, r in zip(own_blocks(cotangent), grad_normed_second, hat_second, scale_second):
         g = v.astype(f32) * gain_second
         grad_hidden.append(d.astype(f32) + r * (g - hat * jnp.mean(g * hat, axis=1, keepdims=True)))
     attention_rounded = [v.astype(bf16) for v in grad_hidden]
-    grad_gain_second = jnp.sum(
-        mlp_in.astype(f32) * lax.optimization_barrier(in_grad).astype(f32), axis=0
-    ) / gain_second
-    near_rounded = own_tokens(attention_rounded)
-    attention_rounded = tie(all_rows(attention_rounded), in_sum)
+    gain_part = sum(
+        jnp.sum(v.astype(f32) * hat, axis=0) for v, hat in zip(grad_normed_second, hat_second)
+    )
+
+    if fold == 1:
+        gain_part = gain_part / lax.axis_size("head")
+
+    def branch_beside(after):
+        m = tie(mixed, after, down_sum)
+        return (chip_sum(dot_left(m[:, half:], mlp_down), dot_left(m[:, :half], mlp_down)),)
+
+    attention_rounded, (branch,) = all_rows(attention_rounded, (), branch_beside)
+    branch, attention_rounded = together(branch, attention_rounded)
+    branch = first_exchange(branch)
     grad_gated = dot_right(attention_rounded, out_weight)
-    mixed = tie(mixed, grad_gated)
-    branch = summed_rows(chip_sum(dot_left(mixed[:, half:], mlp_down), dot_left(mixed[:, :half], mlp_down)))
-    result = own_tokens([(v + w.astype(f32)).astype(bf16) for v, w in zip(hidden_state, branch)])
     grad_outputs, grad_gate, grad_gain_out, local_pull = gate_backward(
         places, grad_gated, outputs, gate_pre, gain_out, ident
     )
-    out_grad = dot_left(gated, attention_rounded).astype(bf16)
-    gate_grad = dot_left(grad_gate, turned_first).astype(bf16)
-    leaving = states_back(local_pull, move)
-    leaving = tie(leaving, out_grad, gate_grad, down_sum)
-    mid_sum = line_scatter(jnp.concatenate([out_grad, gate_grad], axis=0))
-    grad_proj, grad_mix, grad_taps, grad_par, grad_head = delta_backward(
-        places, proj, edge, taps, mix_pre, par, grad_outputs, inverse, states, entering, leaving
+
+    line_in = in_sum
+
+    def first_work(sent, carried):
+        parts = first_total(branch, sent)
+        return dot_left(gated, tie(attention_rounded, parts[0])).astype(bf16), *parts
+
+    def second_work(sent, carried):
+        parts = second_exchange(tuple(carried[1:]))
+        return carried[0], dot_left(tie(grad_gate, sent), turned_first).astype(bf16), *parts
+
+    def third_work(sent, carried):
+        parts = second_total(tuple(carried[2:]))
+        rows = [(v + w.astype(f32)).astype(bf16) for v, w in zip(hidden_state, parts)]
+        return jnp.concatenate(carried[:2], axis=0), line_in, *rows
+
+    leaving, (mid_grad, in_sum, *result) = states_back(local_pull, move, (first_work, second_work, third_work))
+    leaving, mid_grad, down_sum, *result = together(leaving, mid_grad, down_sum, *result)
+    result = chip_rows(result)
+    in_other, down_other = swapped_share(in_sum), swapped_share(down_sum)
+    mid_sum = line_scatter(tie(mid_grad, in_sum))
+    grad_side, grad_taps, grad_par, grad_head = delta_backward(
+        places, grad_gate, proj, edge, taps, mix_pre, par, grad_outputs, inverse, states, entering, leaving
     )
     following = lax.ppermute(grad_head, "seq", backward)
     fixes = []
     for s in range(3):
         fixes.append(sum(taps[3 - j] * following[s - 3 + j] for j in range(3 - s, 4)))
     at_end = order[1][-1] * UNIT + (1 ^ order[2]) * ROWS + ROWS - HALO
-    ending = lax.dynamic_slice_in_dim(grad_proj, at_end, HALO).astype(f32)
+    if fold == 2:
+        grad_side, in_other, down_other, *result = together(grad_side, in_other, down_other, *result)
+    ending = lax.dynamic_slice(grad_side, (at_end, 0), (HALO, width)).astype(f32)
     ending = (ending + jnp.pad(jnp.stack(fixes), ((HALO - 3, 0), (0, 0)))).astype(bf16)
-    grad_proj = lax.dynamic_update_slice_in_dim(grad_proj, ending, at_end, 0)
-    mix_turned = mix_weight.T
-    first = lambda lo, hi: (
-        dot_rows(grad_proj[lo:hi], proj_weight)
-        + dot_rows(grad_gate[lo:hi], gate_weight)
-        + dot_rows(grad_mix[lo:hi], mix_turned)
-    )
-    mine = chip_sum(first(half, row_count), first(0, half))
-    proj_grad = dot_left(tie(grad_proj, mine), turned_first).astype(bf16)
-    last_sum = line_scatter(tie(proj_grad, mid_sum))
-    grad_normed_first = summed_rows(mine, (proj_grad,) if fold == 2 else ())
-    grad_taps, grad_par, grad_mix, gate_grad = (
-        tie(v, grad_normed_first[0]) for v in (grad_taps, grad_par, grad_mix, gate_grad)
-    )
-    grad_normed_first = own_tokens(grad_normed_first, last_sum).astype(f32)
+    grad_side = lax.dynamic_update_slice(grad_side, ending, (at_end, 0))
+    proj_grad = dot_left(turned_first, grad_side[:, :width]).astype(bf16)
+    last_sum = line_scatter(proj_grad, 0)
+    away = dot_rows(tie(grad_side, proj_grad, mid_sum)[half:], side_weight).astype(bf16)
+    near = dot_rows(tie(grad_side, away)[:half], side_weight)
+    mine = chip_sum(away, near)
+    grad_normed_first = first_exchange(mine)
+    in_sum, down_sum, mid_sum, grad_taps, grad_par, grad_side, proj_grad = (
+        tie(v, mine) for v in (in_sum, down_sum, mid_sum, grad_taps, grad_par, grad_side, proj_grad)
+    )
     taps_sum = jnp.sum(grad_taps.reshape(4, 8, width), axis=1)
     par_sum = jnp.sum(grad_par.reshape(2, 8, 128), axis=1)
     every = jnp.zeros((2, shards * a_log.shape[0]), f32)
     every = lax.dynamic_update_slice(every, par_sum[:, :heads], (0, head_at))
-
-    def by_shard(lo, like):
-        block = taps_sum[:, lo : lo + like.shape[2] * shards * heads].reshape(4, heads, shards, like.shape[2])
-        return jnp.moveaxis(block, 2, 0).reshape(shards, -1)
-
-    few = jnp.concatenate(
-        [every[0].reshape(shards, -1), every[1].reshape(shards, -1), jnp.sum(grad_gain_out, axis=0).reshape(shards, -1)],
-        axis=1,
-    )
-    few = jnp.pad(few, ((0, 0), (0, share - few.shape[1]))).reshape(1, model)
-    of_taps = jnp.concatenate(
-        [by_shard(0, conv_query), by_shard(keys, conv_key), by_shard(2 * keys, conv_value)], axis=1
-    ).reshape(shards, heads, share)
-    of_taps = jnp.moveaxis(of_taps, 1, 0).reshape(heads, model)
-    mix_grad = dot_left(grad_mix, turned_first)
-    done_grad, done_gate = (tie(proj_grad, grad_mix), gate_grad)
-    products = (
-        jnp.sum(proj_weight.astype(f32) * done_grad.astype(f32), axis=0)
-        + jnp.sum(gate_weight.astype(f32) * done_gate.astype(f32), axis=0)
-        + jnp.sum(mix_turned.astype(f32) * mix_grad, axis=0)
-    )
-    extra = jnp.concatenate(
-        [mix_grad[: 2 * heads], of_taps, (products / gain_first)[None], grad_gain_second[None], few], axis=0
-    )
-    extra = line_total(extra)
-    extra_sides = columns_of_sides(lax.dynamic_slice_in_dim(extra, lax.axis_index("seq") // fold * fold * share, fold * share, 1))
-    grad_down, grad_mid, grad_last = columns_of_sides(down_sum), columns_of_sides(mid_sum), columns_of_sides(last_sum)
-    grad_in = columns_of_sides(in_sum)
-
-    small_at = 2 * heads
-    shared = sum(s[small_at + heads : small_at + heads + 3] for s in extra_sides)
+    mix_grad = dot_left(grad_side[:, width + vals :], turned_first)
+    few = jnp.concatenate([every.reshape(1, -1), jnp.sum(grad_gain_out, axis=0).reshape(1, -1)], axis=1)
+    fill = lambda v: jnp.pad(v, ((0, 0), (0, model - v.shape[1])))
+    extra = jnp.concatenate([gain_part[None], fill(few), mix_grad[: 2 * heads], fill(taps_sum)], axis=0)
+    extra = jnp.pad(extra, ((0, -extra.shape[0] % 8), (0, 0)))
+    grad_down, grad_in = in_sides(down_sum, down_other), in_sides(in_sum, in_other)
+    ready = (
+        both(grad_in, 0, hidden).T, both(grad_in, hidden, 2 * hidden).T, both(grad_down, 0, hidden),
+    )
+    step = lambda v, by: lax.ppermute(v, "seq", [(i, i ^ by) for i in range(shards)])
     if fold == 2:
+        far_a, far_b, extra, *ready = together(*grad_normed_first[2:], extra, *ready)
+        grad_normed_first = first_total((*grad_normed_first[:2], far_a, far_b))
+        far_extra = step(tie(extra, grad_normed_first[0]), 2)
+        own_result = own_tokens([tie(v, grad_normed_first[0]) for v in result])
+        grad_normed_first = second_total(second_exchange(grad_normed_first), far_extra, own_result)
+        extra = extra + tie(far_extra, grad_normed_first[0])
+    else:
+        own_result = own_tokens(result)
+        grad_normed_first, extra = second_total(grad_normed_first), line_total(extra)
+    after = grad_normed_first[0]
+    grad_tokens, gain_row = [], 0.0
+    for x, d, v in zip(own_inputs, grad_hidden, grad_normed_first):
+        x, v = x.astype(f32), v.astype(f32)
+        r = lax.rsqrt(jnp.mean(x * x, axis=1, keepdims=True) + eps_norm)
+        hat = x * r
+        g = v * gain_first
+        gain_row = gain_row + jnp.sum(v * hat, axis=0, keepdims=True)
+        grad_tokens.append((d + r * (g - hat * jnp.mean(g * hat, axis=1, keepdims=True))).astype(bf16))
+    grad_tokens = chip_rows(grad_tokens)
+    mid_other = swapped_share(tie(mid_sum, after))
+    if fold == 2:
+        far_extra, far_row = step(extra, 4), step(gain_row, 2)
+        *grad_tokens, far_extra, far_row, last_sum = together(*grad_tokens, far_extra, far_row, last_sum)
+        extra, gain_row = extra + far_extra, gain_row + far_row
+        last_other, other, far_row = swap_pair(pick(last_sum, 1 - side, 0)), swap_pair(extra), step(gain_row, 4)
+        grad_tokens = own_tokens(grad_tokens).astype(f32)
+        gain_row = gain_row + far_row
+        gain_row = gain_row + swap_pair(gain_row)
+        sides = [jnp.where(side == 0, extra, other), jnp.where(side == 0, other, extra)]
+        shared = jnp.concatenate([gain_row, extra[:2] + other[:2]], axis=0)
         shared = shared + swap_core(shared)
         shared = shared + swap_chip(shared)
     else:
-        shared = lax.psum(shared, "head")
-    few = shared[2]
-    n_rate, n_gain = a_log.shape[0], out_gain.shape[0]
+        last_other, sides = None, [extra]
+        grad_tokens = own_tokens(grad_tokens).astype(f32)
+        gain_row = line_total(gain_row) / lax.axis_size("head")
+        shared = lax.psum(jnp.concatenate([gain_row, extra[:2]], axis=0), "head")
+    result = own_result
+    me = lax.axis_index("seq")
+    take = lambda v, at, n: lax.dynamic_slice_in_dim(v, at, n, v.ndim - 1)
+    grad_alpha = jnp.concatenate([take(v[2 : 2 + heads], me * share, share) for v in sides], axis=0).T
+    grad_beta = jnp.concatenate([take(v[2 + heads : 2 + 2 * heads], me * share, share) for v in sides], axis=0).T
     filters = []
-    for like, lo in ((conv_query, 0), (conv_key, 1), (conv_value, 2)):
-        n = 4 * heads * like.shape[2]
-        start = (0, 4 * heads * conv_query.shape[2], 8 * heads * conv_query.shape[2])[lo]
-        filters.append(jnp.concatenate(
-            [s[small_at : small_at + heads].reshape(-1)[start : start + n].reshape(4, heads, -1) for s in extra_sides],
+    for like, lo, size in ((conv_query, 0, KEY), (conv_key, keys, KEY), (conv_value, 2 * keys, VAL)):
+        n = like.shape[2]
+        filters.append(jnp.stack(
+            [take(v[2 + 2 * heads : 6 + 2 * heads], lo + h * size + me * n, n) for v in sides for h in range(heads)],
             axis=1,
         ))
-    own_inputs = tokens.astype(f32)
-    own_scale = lax.rsqrt(jnp.mean(own_inputs * own_inputs, axis=1, keepdims=True) + eps_norm)
-    own_hat = own_inputs * own_scale
-    g = grad_normed_first * gain_first
-    grad_tokens = near_rounded.astype(f32) + own_scale * (
-        g - own_hat * jnp.mean(g * own_hat, axis=1, keepdims=True)
-    )
+    n_rate, n_gain = a_log.shape[0], out_gain.shape[0]
+    few = shared[2]
+    grad_mid, grad_last = in_sides(mid_sum, mid_other), in_sides(last_sum, last_other, 0)
+    channels = lambda lo, hi: jnp.concatenate([v[:, lo:hi] for v in grad_last], axis=1)
+
     return (
         result,
         grad_tokens,
-        shared[0],
-        both(grad_last, 0, keys).T,
-        both(grad_last, keys, 2 * keys).T,
-        both(grad_last, 2 * keys, width).T,
+        take(shared[0], me * share, share),
+        channels(0, keys),
+        channels(keys, 2 * keys),
+        channels(2 * keys, width),
         both(grad_mid, vals, 2 * vals).T,
-        both(extra_sides, 0, heads).T,
-        both(extra_sides, heads, 2 * heads).T,
+        grad_alpha,
+        grad_beta,
         filters[0],
         filters[1],
         filters[2],
-        few[:n_rate],
-        few[n_rate : 2 * n_rate],
-        few[2 * n_rate : 2 * n_rate + n_gain],
+        take(few, me * n_rate, n_rate),
+        take(few, (shards + me) * n_rate, n_rate),
+        take(few, 2 * shards * n_rate + me * n_gain, n_gain),
         both(grad_mid, 0, vals),
-        shared[1],
-        both(grad_in, 0, hidden).T,
-        both(grad_in, hidden, 2 * hidden).T,
-        both(grad_down, 0, hidden),
+        take(shared[1], me * share, share),
+        *ready,
     )
 
 

time: 982 us -> 876 us (0.89)
  local copies, waits for them, and re-layouts: 86.8 us -> 49.8 us
  other arithmetic: 163 us -> 128 us
  waiting for transfers between devices: 310 us -> 289 us
  matrix products: 203 us -> 189 us
    ppermute x18 -> x15, waiting for transfers between devices: 84 us -> 54.1 us  [swap_chip(): return lax.ppermute(v, 'head', [(i, i ^ 2) for i in range(4)])]
    reduce_sum x7 -> x3, other arithmetic: 17.4 us -> 2.4 us  [the longest x1 1.6 us: on_device(): r = lax.rsqrt(jnp.mean(x * x, axis=1, keepdims=True) + eps_norm)]
    unnamed x268 -> x219, local copies, waits for them, and re-layouts: 41.4 us -> 26.6 us
    all_gather x3, waiting for transfers between devices: 18.3 us -> 31.9 us  [gathered(): lax.all_gather(mine, 'seq', axis=1, tiled=True, axis_index_groups=lines_o...]
    dot_general x11 -> x7, matrix products: 68.2 us -> 59 us  [dot_rows(): lax.dot_general(a, b, (((1,), (0,)), ((), ())), preferred_element_type=f32)]
    select_n x16 -> x11, other arithmetic: 27.5 us -> 19.4 us  [join(): jnp.where(at == 0, mine, other)]
    ppermute x5 -> x7, waiting for transfers between devices: 23.7 us -> 17 us  [the longest x3 8.7 us: states_back(): state = lax.ppermute(sent, 'seq', onward)]
    ppermute x22 -> x23, waiting for transfers between devices: 140 us -> 135 us  [swap_pair(): lax.ppermute(v, 'seq', [(i, i ^ 1) for i in range(lax.axis_size('seq'))])]
  transfers between devices with their start and end apart: 76 -> 77, of which waited for: 34 -> 46; matrix products, arithmetic and copies ran while one was open for 36% -> 31% of each run, Pallas kernels for 12% -> 13%
where the time goes in v3:
time: 876 us; the launch traced here: 870 us
  waiting for transfers between devices  289 us (33%)
  matrix products  189 us (22%)
  other arithmetic  128 us (15%)
  Pallas kernels  118 us (13%)
  starting transfers between devices  79.3 us (9%)
  local copies, waits for them, and re-layouts  49.8 us (6%)
  between operations  16.8 us (2%)
    ppermute x23, waiting for transfers between devices, swap_pair(): lax.ppermute(v, 'seq', [(i, i ^ 1) for i in range(lax.axis_size('seq'))])  135 us
    dot_general x8, matrix products, dot_left(): lax.dot_general(a, b, (((0,), (0,)), ((), ())), preferred_element_type=f32)  64 us
    dot_general x5, matrix products, dot_right(): lax.dot_general(a, b, (((1,), (1,)), ((), ())), preferred_element_type=f32)  62.2 us
    dot_general x7, matrix products, dot_rows(): lax.dot_general(a, b, (((1,), (0,)), ((), ())), preferred_element_type=f32)  59 us
    ppermute x15, waiting for transfers between devices, swap_chip(): return lax.ppermute(v, 'head', [(i, i ^ 2) for i in range(4)])  54.1 us
    pallas_call x1, Pallas kernels, delta_backward(): pl.pallas_call(functools.partial(backward_kernel, heads), grid_spec=pltpu...  52.6 us
    pallas_call x1, Pallas kernels, delta_forward(): pl.pallas_call(functools.partial(forward_kernel, heads), grid=(blocks,),...  35 us
    all_gather x3, waiting for transfers between devices, gathered(): lax.all_gather(mine, 'seq', axis=1, tiled=True, axis_index_groups=lines_o...  31.9 us
  transfers between devices with their start and end apart: 77, of which 46 were waited for; matrix products, arithmetic and copies ran while one was open for 31% of the time, Pallas kernels for 13%

profile of v3, /device:TPU:0, one launch (start us, length us, event | category | flops | bytes accessed | tf_op | source)
XLA Modules:
  0.0 869.8 jit_solution(18192370521621527161)
XLA Ops:
  14.2 11.9 %collective-permute-done = bf16[1024,256]{1,0:T(8,128)(2,1)S(1)} collective-permute-done((bf16[1024,256]{1,0:T(8,128)(2,1)S(1)}, bf16[1024,256]{1,0:T(8,128)(2,1)S(1)}, u32[]{:S(2)}, u32[]{:S(2)}) %collective-permute-start) | collective-permute-done | bytes 524320 | tf_op jit(solution)/shard_map/ppermute | solution.py:584
  52.0 36.0 %collective-permute-done.1 = bf16[512,2048]{1,0:T(8,128)(2,1)S(1)} collective-permute-done((bf16[512,2048]{1,0:T(8,128)(2,1)S(1)}, bf16[512,2048]{1,0:T(8,128)(2,1)S(1)}, u32[]{:S(2)}, u32[]{:S(2)}) %collective-permute-start.1) | collective-permute-done | bytes 2097184 | tf_op jit(solution)/shard_map/ppermute | solution.py:584
  105.5 11.7 %fusion.2.refs_1_ = bf16[2048,2048]{1,0:T(8,128)(2,1)} fusion(f32[2048]{0:T(1024)S(1)} %bitcast.154, f32[2048]{0:T(1024)S(1)} %add_rsqrt_fusion, bf16[1024,2048]{1,0:T(8,128)(2,1)S(1)} %get-tuple-element.440, bf16[1024,2048]{1,0:T(8,128)(2,1)S(1)} %get-tuple-element.439), kind=kLoop, calls=%fused_computation.4 | loop fusion | flops 29360128 | bytes 16793600 | tf_op jit(solution)/shard_map/convert_element_type | solution.py:854
  117.2 14.7 %convolution_convert_fusion.7.proj_ref.before_ref = bf16[2048,1024]{1,0:T(8,128)(2,1)} fusion(bf16[2048,2048]{1,0:T(8,128)(2,1)} %fusion.2.refs_1_, bf16[1024,2048]{1,0:T(8,128)(2,1)} %all-gather.4.cloned.1.call-done), kind=kOutput, calls=%fused_computation.48 | convolution fusion | flops 8592031744 | bytes 16777216 | tf_op jit(solution)/shard_map/dot_general | solution.py:555
  145.5 35.0 %shard_map.347 = (f32[2048,512]{1,0:T(8,128)}, bf16[2048,256]{1,0:T(8,128)(2,1)S(1)}, bf16[2048,256]{1,0:T(8,128)(2,1)S(1)}, bf16[16,2,128,384]{3,2,1,0:T(8,128)(2,1)}, f32[2,128,384]{2,1,0:T(8,128)S(1)}) custom-call(bf16[2048,1024]{1,0:T(8,128)(2,1)} %convolution_convert_fusion.7.proj_ref.before_ref, bf16[16,1024]{1,0:T(8,128)(2,1)S(1)} %collective-permute-done.6.edge_ref, ...), custom_call_target="tpu_custom_call" | custom-call | tf_op jit(solution)/shard_map/pallas_call | solution.py:169
  198.9 11.4 %fusion.116.gate_ref = f32[2048,512]{1,0:T(8,128)} fusion(bf16[2048,2048]{1,0:T(8,128)(2,1)} %fusion.2.refs_1_, bf16[1024,2048]{1,0:T(8,128)(2,1)} %all-gather.6.cloned.1.call-done), kind=kOutput, calls=%fused_computation.360 | convolution fusion | flops 4294967296 | bytes 14680064 | tf_op jit(solution)/shard_map/dot_general | solution.py:555
  221.3 8.5 pad_maximum_fusion.1.refs_0_
  229.9 8.4 shard_map.348
  245.1 9.0 %shard_map.349 = (f32[2048,512]{1,0:T(8,128)}, bf16[2048,512]{1,0:T(8,128)(2,1)S(1)}) custom-call(s32[17]{0:T(128)S(1)} %stack.131.order_ref, f32[2048,512]{1,0:T(8,128)} %get-tuple-element.197.value_ref, bf16[2048,256]{1,0:T(8,128)(2,1)S(1)} %get-tuple-element.198.ident_ref, bf16[2,128,256]{2,1,0:T(8,128)(2,1)S(1)} %collective-permute-done.9.state_ref.enter_ref, ...), custom_call_target="tpu_custom_call" | custom-call | tf_op jit(solution)/shard_map/pallas_call | solution.py:251
  269.5 21.9 %collective-permute-done.14 = bf16[256,2048]{1,0:T(8,128)(2,1)S(1)} collective-permute-done((bf16[256,2048]{1,0:T(8,128)(2,1)S(1)}, bf16[256,2048]{1,0:T(8,128)(2,1)S(1)}, u32[]{:S(2)}, u32[]{:S(2)}) %collective-permute-start.14) | collective-permute-done | bytes 1048608 | tf_op jit(solution)/shard_map/ppermute | solution.py:584
  296.1 10.7 %collective-permute-done.16 = bf16[128,2048]{1,0:T(8,128)(2,1)S(1)} collective-permute-done((bf16[128,2048]{1,0:T(8,128)(2,1)S(1)}, bf16[128,2048]{1,0:T(8,128)(2,1)S(1)}, u32[]{:S(2)}, u32[]{:S(2)}) %collective-permute-start.16) | collective-permute-done | bytes 524320 | tf_op jit(solution)/shard_map/ppermute | solution.py:588
  313.3 31.9 %all-gather.8.cloned.1.call-done = bf16[2064,2048]{1,0:T(8,128)(2,1)} async-done(((bf16[2064,512]{1,0:T(8,128)(2,1)}), bf16[2064,2048]{1,0:T(8,128)(2,1)}) %all-gather.8.cloned.1.call-update) | async-done | bytes 8454160 | tf_op jit(solution)/shard_map/all_gather | solution.py:757
  348.4 22.2 %collective-permute-done.21.refs_1_ = bf16[256,2048]{1,0:T(8,128)(2,1)S(1)} collective-permute-done((bf16[256,2048]{1,0:T(8,128)(2,1)S(1)}, bf16[256,2048]{1,0:T(8,128)(2,1)S(1)}, u32[]{:S(2)}, u32[]{:S(2)}) %collective-permute-start.21) | collective-permute-done | bytes 1048608 | tf_op jit(solution)/shard_map/ppermute | solution.py:584
  383.0 16.1 %fusion.8 = f32[1376,2048]{1,0:T(8,128)} fusion(bf16[2048,2048]{1,0:T(8,128)(2,1)S(1)} %shard_map.350, bf16[2064,2048]{1,0:T(8,128)(2,1)} %all-gather.8.cloned.1.call-done), kind=kOutput, calls=%fused_computation.26 | convolution fusion | flops 11542724608 | bytes 25296896 | tf_op jit(solution)/shard_map/dot_general | solution.py:555
  399.1 13.8 %multiply_convert_fusion.1 = (bf16[688,2048]{1,0:T(8,128)(2,1)}, bf16[688,2048]{1,0:T(8,128)(2,1)}, bf16[688,2048]{1,0:T(8,128)(2,1)}) fusion(f32[1376,2048]{1,0:T(8,128)} %fusion.8, bf16[2048,2048]{1,0:T(8,128)(2,1)S(1)} %bitcast.141, bf16[2064,2048]{1,0:T(8,128)(2,1)} %all-gather.8.cloned.1.call-done), kind=kOutput, calls=%fused_computation.18 | convolution fusion | flops 5792497664 | bytes 30932992 | tf_op jit(solution)/shard_map/dot_general | solution.py:555
  412.9 11.1 %fusion.18 = bf16[1024,2048]{1,0:T(8,128)(2,1)} fusion(bf16[2064,2048]{1,0:T(8,128)(2,1)} %all-gather.8.cloned.1.call-done, bf16[688,2048]{1,0:T(8,128)(2,1)} %get-tuple-element.433, bf16[688,2048]{1,0:T(8,128)(2,1)} %get-tuple-element.432), kind=kOutput, calls=%fused_computation.43 | convolution fusion | flops 5779095552 | bytes 15466496 | tf_op jit(solution)/shard_map/dot_general | solution.py:551
  424.2 9.4 %fusion.15 = bf16[1024,2048]{1,0:T(8,128)(2,1)S(1)} fusion(bf16[2064,2048]{1,0:T(8,128)(2,1)} %all-gather.8.cloned.1.call-done, bf16[688,2048]{1,0:T(8,128)(2,1)S(1)} %copy-done.39, bf16[688,2048]{1,0:T(8,128)(2,1)S(1)} %copy-done.38), kind=kOutput, calls=%fused_computation.42 | convolution fusion | flops 5779095552 | bytes 15466496 | tf_op jit(solution)/shard_map/dot_general | solution.py:551
  447.4 7.4 convolution_convert_fusion.8
  454.9 17.8 %convolution_convert_fusion = bf16[1376,2048]{1,0:T(8,128)(2,1)} fusion(bf16[1376,2048]{1,0:T(8,128)(2,1)} %pad_maximum_fusion.2, bf16[2048,2048]{1,0:T(8,128)(2,1)} %copy-done.1), kind=kOutput, calls=%fused_computation.11 | convolution fusion | flops 11545542656 | bytes 19660800 | tf_op jit(solution)/shard_map/dot_general | solution.py:547
  478.6 11.4 %collective-permute-done.30 = bf16[128,2048]{1,0:T(8,128)(2,1)S(1)} collective-permute-done((bf16[128,2048]{1,0:T(8,128)(2,1)S(1)}, bf16[128,2048]{1,0:T(8,128)(2,1)S(1)}, u32[]{:S(2)}, u32[]{:S(2)}) %collective-permute-start.30) | collective-permute-done | bytes 524320 | tf_op jit(solution)/shard_map/ppermute | solution.py:588
  497.7 9.6 %collective-permute-done.32 = bf16[128,2048]{1,0:T(8,128)(2,1)S(1)} collective-permute-done((bf16[128,2048]{1,0:T(8,128)(2,1)S(1)}, bf16[128,2048]{1,0:T(8,128)(2,1)S(1)}, u32[]{:S(2)}, u32[]{:S(2)}) %collective-permute-start.32) | collective-permute-done | bytes 524320 | tf_op jit(solution)/shard_map/ppermute | solution.py:588
  510.1 7.9 convolution_convert_fusion.3
  533.3 10.3 %collective-permute-done.34.refs_1_ = bf16[256,2048]{1,0:T(8,128)(2,1)S(1)} collective-permute-done((bf16[256,2048]{1,0:T(8,128)(2,1)S(1)}, bf16[256,2048]{1,0:T(8,128)(2,1)S(1)}, u32[]{:S(2)}, u32[]{:S(2)}) %collective-permute-start.34) | collective-permute-done | bytes 1048608 | tf_op jit(solution)/shard_map/ppermute | solution.py:584
  564.8 9.8 %shard_map.352 = (bf16[2048,512]{1,0:T(8,128)(2,1)S(1)}, bf16[2048,512]{1,0:T(8,128)(2,1)S(1)}, f32[8,256]{1,0:T(8,128)S(1)}, f32[2,128,256]{2,1,0:T(8,128)S(1)}) custom-call(s32[17]{0:T(128)S(1)} %copy-done.15, f32[2048,512]{1,0:T(8,128)} %fusion.31.grad_ref, f32[2048,512]{1,0:T(8,128)} %get-tuple-element.270.out_ref, f32[2048,512]{1,0:T(8,128)} %fusion.116.gate_ref, ...), custom_call_target="tpu_custom_call" | custom-call | tf_op jit(solution)/shard_map/pallas_call | solution.py:306
  619.3 15.2 %reduce-scatter.7.cloned.1.call-done = bf16[1376,512]{1,0:T(8,128)(2,1)} async-done(((bf16[1376,2048]{1,0:T(8,128)(2,1)}), bf16[1376,512]{1,0:T(8,128)(2,1)}) %reduce-scatter.7.cloned.1.call-update) | async-done | bytes 1409040 | tf_op jit(solution)/shard_map/reduce_scatter | solution.py:761
  645.2 52.6 %shard_map.353 = (bf16[2048,1664]{1,0:T(8,128)(2,1)}, f32[32,1024]{1,0:T(8,128)}, f32[16,128]{1,0:T(8,128)}, f32[8,1024]{1,0:T(8,128)}) custom-call(s32[17]{0:T(128)} %copy-done.14, bf16[2048,512]{1,0:T(8,128)(2,1)} %copy-done.6, bf16[2048,1024]{1,0:T(8,128)(2,1)} %convolution_convert_fusion.7.proj_ref.before_ref, ...), custom_call_target="tpu_custom_call" | custom-call | tf_op jit(solution)/shard_map/pallas_call | solution.py:478
  699.9 7.5 collective-permute-done.51
  710.2 14.2 %fusion.12 = bf16[2048,1024]{1,0:T(8,128)(2,1)} fusion(bf16[2048,2048]{1,0:T(8,128)(2,1)} %copy-done, bf16[2048,1664]{1,0:T(8,128)(2,1)} %fusion.88), kind=kOutput, calls=%fused_computation.41 | convolution fusion | flops 8592031744 | bytes 16777216 | tf_op jit(solution)/shard_map/dot_general | solution.py:551
  724.4 12.3 %convolution_convert_fusion.2 = bf16[1024,2048]{1,0:T(8,128)(2,1)} fusion(bf16[1664,2048]{1,0:T(8,128)(2,1)} %constant_dynamic-update-slice_fusion.5, bf16[2048,1664]{1,0:T(8,128)(2,1)} %fusion.88), kind=kOutput, calls=%fused_computation.40 | convolution fusion | flops 6981419008 | bytes 14417920 | tf_op jit(solution)/shard_map/dot_general | solution.py:547
  736.7 11.2 %convolution_convert_fusion.1 = bf16[1024,2048]{1,0:T(8,128)(2,1)S(1)} fusion(bf16[1664,2048]{1,0:T(8,128)(2,1)} %constant_dynamic-update-slice_fusion.5, bf16[2048,1664]{1,0:T(8,128)(2,1)} %fusion.88), kind=kOutput, calls=%fused_computation.39 | convolution fusion | flops 6981419008 | bytes 14417920 | tf_op jit(solution)/shard_map/dot_general | solution.py:547
  766.9 13.3 %collective-permute-done.53 = bf16[256,2048]{1,0:T(8,128)(2,1)} collective-permute-done((bf16[256,2048]{1,0:T(8,128)(2,1)}, bf16[256,2048]{1,0:T(8,128)(2,1)}, u32[]{:S(2)}, u32[]{:S(2)}) %collective-permute-start.53) | collective-permute-done | bytes 1048608 | tf_op jit(solution)/shard_map/ppermute | solution.py:584
  822.0 13.4 %collective-permute-done.59 = bf16[256,2048]{1,0:T(8,128)(2,1)S(1)} collective-permute-done((bf16[256,2048]{1,0:T(8,128)(2,1)S(1)}, bf16[256,2048]{1,0:T(8,128)(2,1)S(1)}, u32[]{:S(2)}, u32[]{:S(2)}) %collective-permute-start.59) | collective-permute-done | bytes 1048608 | tf_op jit(solution)/shard_map/ppermute | solution.py:588
  (613 shorter events, 355.4 us)
Async XLA Ops:
  7.2 110.0 %all-gather.4.cloned.1.call-start = ((), (), s32[]{:S(2)}) async-start(), calls=%async_computation.4 | async-start | bytes 5242880 | tf_op jit(solution)/shard_map/all_gather | solution.py:757
  27.5 171.4 %all-gather.6.cloned.1.call-start = ((), (), s32[]{:S(2)}) async-start(), calls=%async_computation.5 | async-start | bytes 5242880 | tf_op jit(solution)/shard_map/all_gather | solution.py:757
  29.4 65.3 %collective-permute-start.12 = (bf16[1024,256]{1,0:T(8,128)(2,1)}, bf16[1024,256]{1,0:T(8,128)(2,1)}, u32[]{:S(2)}, u32[]{:S(2)}) collective-permute-start(bf16[1024,256]{1,0:T(8,128)(2,1)} %pad_maximum_fusion.32), channel_id=1, source_target_pairs={{0,4},{4,0},{8,12},{12,8},{16,20},{20,16},{24,28},{28,24},{1,5},{5... | collective-permute-start | bytes 1572872 | tf_op jit(solution)/shard_map/ppermute | solution.py:584
  34.5 53.6 %collective-permute-start.1 = (bf16[512,2048]{1,0:T(8,128)(2,1)S(1)}, bf16[512,2048]{1,0:T(8,128)(2,1)S(1)}, u32[]{:S(2)}, u32[]{:S(2)}) collective-permute-start(bf16[512,2048]{1,0:T(8,128)(2,1)S(1)} %constant_dynamic-slice_fusion.40), channel_id=1, source_target_pairs={{0,4},{4,0},{8,12},{12,8},{16,20},{20,16},{24,28},{28,24},{1,5},{5... | collective-permute-start | bytes 6291464 | tf_op jit(solution)/shard_map/ppermute | solution.py:584
  49.1 41.5 %collective-permute-start.5 = (bf16[4,4096]{1,0:T(4,128)(2,1)S(1)}, bf16[4,4096]{1,0:T(4,128)(2,1)S(1)}, u32[]{:S(2)}, u32[]{:S(2)}) collective-permute-start(bf16[4,4096]{1,0:T(4,128)(2,1)S(1)} %pad_maximum_fusion.36), channel_id=1, source_target_pairs={{0,16},{4,20},{8,24},{12,28},{16,0},{20,4},{24,8},{28,12},{1,17},{... | collective-permute-start | bytes 98312 | tf_op jit(solution)/shard_map/ppermute | solution.py:724
  89.1 92.3 %collective-permute-start.18 = (bf16[2064,256]{1,0:T(8,128)(2,1)}, bf16[2064,256]{1,0:T(8,128)(2,1)}, u32[]{:S(2)}, u32[]{:S(2)}) collective-permute-start(bf16[2064,256]{1,0:T(8,128)(2,1)} %pad_maximum_fusion.11), channel_id=1, source_target_pairs={{0,4},{4,0},{8,12},{12,8},{16,20},{20,16},{24,28},{28,24},{1,5},{5... | collective-permute-start | bytes 3170312 | tf_op jit(solution)/shard_map/ppermute | solution.py:584
  97.2 248.0 %all-gather.8.cloned.1.call-start = ((), (), s32[]{:S(2)}) async-start(), calls=%async_computation.6 | async-start | bytes 10567680 | tf_op jit(solution)/shard_map/all_gather | solution.py:757
  133.3 48.1 %collective-permute-start.10 = (bf16[512,2048]{1,0:T(8,128)(2,1)}, bf16[512,2048]{1,0:T(8,128)(2,1)}, u32[]{:S(2)}, u32[]{:S(2)}) collective-permute-start(bf16[512,2048]{1,0:T(8,128)(2,1)} %constant_dynamic-slice_fusion.26), channel_id=1, source_target_pairs={{0,4},{4,0},{8,12},{12,8},{16,20},{20,16},{24,28},{28,24},{1,5},{5... | collective-permute-start | bytes 6291464 | tf_op jit(solution)/shard_map/ppermute | solution.py:584
  181.4 33.1 %collective-permute-start.11 = (bf16[512,2048]{1,0:T(8,128)(2,1)}, bf16[512,2048]{1,0:T(8,128)(2,1)S(1)}, u32[]{:S(2)}, u32[]{:S(2)}) collective-permute-start(bf16[512,2048]{1,0:T(8,128)(2,1)} %collective-permute-done.10), channel_id=1, source_target_pairs={{0,1},{1,0},{2,3},{3,2},{4,5},{5,4},{6,7},{7,6},{8,9},{9,8},{10,11... | collective-permute-start | bytes 6291464 | tf_op jit(solution)/shard_map/ppermute | solution.py:592
  189.6 320.5 %reduce-scatter.5.cloned.1.call-start = ((), (), s32[]{:S(2)}) async-start(), calls=%async_computation.7 | async-start | bytes 3522560 | tf_op jit(solution)/shard_map/reduce_scatter | solution.py:761
  212.1 33.0 %collective-permute-start.9 = (bf16[2,128,256]{2,1,0:T(8,128)(2,1)}, bf16[2,128,256]{2,1,0:T(8,128)(2,1)S(1)}, u32[]{:S(2)}, u32[]{:S(2)}) collective-permute-start(bf16[2,128,256]{2,1,0:T(8,128)(2,1)} %fusion.50), channel_id=1, source_target_pairs={{0,8},{4,12},{8,16},{12,20},{16,24},{20,28},{1,9},{5,13},{9,17},{1... | collective-permute-start | bytes 393224 | tf_op jit(solution)/shard_map/ppermute | solution.py:787
  266.1 25.4 %collective-permute-start.14 = (bf16[256,2048]{1,0:T(8,128)(2,1)S(1)}, bf16[256,2048]{1,0:T(8,128)(2,1)S(1)}, u32[]{:S(2)}, u32[]{:S(2)}) collective-permute-start(bf16[256,2048]{1,0:T(8,128)(2,1)S(1)} %get-tuple-element.205), channel_id=1, source_target_pairs={{0,4},{4,0},{8,12},{12,8},{16,20},{20,16},{24,28},{28,24},{1,5},{5... | collective-permute-start | bytes 3145736 | tf_op jit(solution)/shard_map/ppermute | solution.py:584
  268.0 24.9 %collective-permute-start.15 = (bf16[256,2048]{1,0:T(8,128)(2,1)S(1)}, bf16[256,2048]{1,0:T(8,128)(2,1)S(1)}, u32[]{:S(2)}, u32[]{:S(2)}) collective-permute-start(bf16[256,2048]{1,0:T(8,128)(2,1)S(1)} %pad_maximum_fusion.15), channel_id=1, source_target_pairs={{0,2},{1,3},{2,0},{3,1},{4,6},{5,7},{6,4},{7,5},{8,10},{9,11},{10,... | collective-permute-start | bytes 3145736 | tf_op jit(solution)/shard_map/ppermute | solution.py:588
  312.1 33.1 %collective-permute-start.19 = (bf16[128,2048]{1,0:T(8,128)(2,1)S(1)}, bf16[128,2048]{1,0:T(8,128)(2,1)S(1)}, u32[]{:S(2)}, u32[]{:S(2)}) collective-permute-start(bf16[128,2048]{1,0:T(8,128)(2,1)S(1)} %get-tuple-element.219), channel_id=1, source_target_pairs={{0,2},{1,3},{2,0},{3,1},{4,6},{5,7},{6,4},{7,5},{8,10},{9,11},{10,... | collective-permute-start | bytes 1572872 | tf_op jit(solution)/shard_map/ppermute | solution.py:588
  312.7 32.5 %collective-permute-start.20 = (bf16[128,2048]{1,0:T(8,128)(2,1)S(1)}, bf16[128,2048]{1,0:T(8,128)(2,1)S(1)}, u32[]{:S(2)}, u32[]{:S(2)}) collective-permute-start(bf16[128,2048]{1,0:T(8,128)(2,1)S(1)} %get-tuple-element.220), channel_id=1, source_target_pairs={{0,4},{4,0},{8,12},{12,8},{16,20},{20,16},{24,28},{28,24},{1,5},{5... | collective-permute-start | bytes 1572872 | tf_op jit(solution)/shard_map/ppermute | solution.py:584
  345.4 25.2 %collective-permute-start.21 = (bf16[256,2048]{1,0:T(8,128)(2,1)S(1)}, bf16[256,2048]{1,0:T(8,128)(2,1)S(1)}, u32[]{:S(2)}, u32[]{:S(2)}) collective-permute-start(bf16[256,2048]{1,0:T(8,128)(2,1)S(1)} %pad_maximum_fusion.16.refs_0_), channel_id=1, source_target_pairs={{0,4},{4,0},{8,12},{12,8},{16,20},{20,16},{24,28},{28,24},{1,5},{5... | collective-permute-start | bytes 3145736 | tf_op jit(solution)/shard_map/ppermute | solution.py:584
  346.9 24.8 %collective-permute-start.22 = (bf16[256,2048]{1,0:T(8,128)(2,1)S(1)}, bf16[256,2048]{1,0:T(8,128)(2,1)S(1)}, u32[]{:S(2)}, u32[]{:S(2)}) collective-permute-start(bf16[256,2048]{1,0:T(8,128)(2,1)S(1)} %pad_maximum_fusion.17.refs_2_), channel_id=1, source_target_pairs={{0,2},{1,3},{2,0},{3,1},{4,6},{5,7},{6,4},{7,5},{8,10},{9,11},{10,... | collective-permute-start | bytes 3145736 | tf_op jit(solution)/shard_map/ppermute | solution.py:588
  445.4 27.5 %collective-permute-start.28 = (bf16[256,2048]{1,0:T(8,128)(2,1)}, bf16[256,2048]{1,0:T(8,128)(2,1)}, u32[]{:S(2)}, u32[]{:S(2)}) collective-permute-start(bf16[256,2048]{1,0:T(8,128)(2,1)} %get-tuple-element.235), channel_id=1, source_target_pairs={{0,4},{4,0},{8,12},{12,8},{16,20},{20,16},{24,28},{28,24},{1,5},{5... | collective-permute-start | bytes 3145736 | tf_op jit(solution)/shard_map/ppermute | solution.py:584
  446.0 27.0 %collective-permute-start.29 = (bf16[256,2048]{1,0:T(8,128)(2,1)}, bf16[256,2048]{1,0:T(8,128)(2,1)}, u32[]{:S(2)}, u32[]{:S(2)}) collective-permute-start(bf16[256,2048]{1,0:T(8,128)(2,1)} %pad_maximum_fusion.19), channel_id=1, source_target_pairs={{0,2},{1,3},{2,0},{3,1},{4,6},{5,7},{6,4},{7,5},{8,10},{9,11},{10,... | collective-permute-start | bytes 3145736 | tf_op jit(solution)/shard_map/ppermute | solution.py:588
  454.9 179.6 %reduce-scatter.7.cloned.1.call-start = ((), (), s32[]{:S(2)}) async-start(), calls=%async_computation.8 | async-start | bytes 7045120 | tf_op jit(solution)/shard_map/reduce_scatter | solution.py:761
  518.0 25.6 %collective-permute-start.34 = (bf16[256,2048]{1,0:T(8,128)(2,1)S(1)}, bf16[256,2048]{1,0:T(8,128)(2,1)S(1)}, u32[]{:S(2)}, u32[]{:S(2)}) collective-permute-start(bf16[256,2048]{1,0:T(8,128)(2,1)S(1)} %pad_maximum_fusion.20.refs_0_), channel_id=1, source_target_pairs={{0,4},{4,0},{8,12},{12,8},{16,20},{20,16},{24,28},{28,24},{1,5},{5... | collective-permute-start | bytes 3145736 | tf_op jit(solution)/shard_map/ppermute | solution.py:584
  519.5 25.4 %collective-permute-start.35 = (bf16[256,2048]{1,0:T(8,128)(2,1)S(1)}, bf16[256,2048]{1,0:T(8,128)(2,1)}, u32[]{:S(2)}, u32[]{:S(2)}) collective-permute-start(bf16[256,2048]{1,0:T(8,128)(2,1)S(1)} %pad_maximum_fusion.21.refs_2_), channel_id=1, source_target_pairs={{0,2},{1,3},{2,0},{3,1},{4,6},{5,7},{6,4},{7,5},{8,10},{9,11},{10,... | collective-permute-start | bytes 3145736 | tf_op jit(solution)/shard_map/ppermute | solution.py:588
  527.8 196.6 %reduce-scatter.9.cloned.1.call-start = ((), (), s32[]{:S(2)}) async-start(), calls=%async_computation.9 | async-start | bytes 5242880 | tf_op jit(solution)/shard_map/reduce_scatter | solution.py:761
  556.5 25.5 %collective-permute-start.42 = (bf16[256,2048]{1,0:T(8,128)(2,1)}, bf16[256,2048]{1,0:T(8,128)(2,1)}, u32[]{:S(2)}, u32[]{:S(2)}) collective-permute-start(bf16[256,2048]{1,0:T(8,128)(2,1)} %get-tuple-element.277), channel_id=1, source_target_pairs={{0,4},{4,0},{8,12},{12,8},{16,20},{20,16},{24,28},{28,24},{1,5},{5... | collective-permute-start | bytes 3145736 | tf_op jit(solution)/shard_map/ppermute | solution.py:584
  557.1 25.2 %collective-permute-start.43 = (bf16[256,2048]{1,0:T(8,128)(2,1)}, bf16[256,2048]{1,0:T(8,128)(2,1)}, u32[]{:S(2)}, u32[]{:S(2)}) collective-permute-start(bf16[256,2048]{1,0:T(8,128)(2,1)} %pad_maximum_fusion.23), channel_id=1, source_target_pairs={{0,2},{1,3},{2,0},{3,1},{4,6},{5,7},{6,4},{7,5},{8,10},{9,11},{10,... | collective-permute-start | bytes 3145736 | tf_op jit(solution)/shard_map/ppermute | solution.py:588
  635.3 186.7 %reduce-scatter.11.cloned.1.call-start = ((), (), s32[]{:S(2)}) async-start(), calls=%async_computation.10 | async-start | bytes 5242880 | tf_op jit(solution)/shard_map/reduce_scatter | solution.py:761
  638.2 69.3 %collective-permute-start.50 = (bf16[256,2048]{1,0:T(8,128)(2,1)S(1)}, bf16[256,2048]{1,0:T(8,128)(2,1)S(1)}, u32[]{:S(2)}, u32[]{:S(2)}) collective-permute-start(bf16[256,2048]{1,0:T(8,128)(2,1)S(1)} %constant_dynamic-update-slice_fusion.3), channel_id=1, source_target_pairs={{0,2},{1,3},{2,0},{3,1},{4,6},{5,7},{6,4},{7,5},{8,10},{9,11},{10,... | collective-permute-start | bytes 3145736 | tf_op jit(solution)/shard_map/ppermute | solution.py:588
  639.8 67.6 %collective-permute-start.48 = (bf16[1376,256]{1,0:T(8,128)(2,1)S(1)}, bf16[1376,256]{1,0:T(8,128)(2,1)S(1)}, u32[]{:S(2)}, u32[]{:S(2)}) collective-permute-start(bf16[1376,256]{1,0:T(8,128)(2,1)S(1)} %constant_dynamic-slice_fusion.24), channel_id=1, source_target_pairs={{0,4},{4,0},{8,12},{12,8},{16,20},{20,16},{24,28},{28,24},{1,5},{5... | collective-permute-start | bytes 2113544 | tf_op jit(solution)/shard_map/ppermute | solution.py:584
  644.7 62.8 %collective-permute-start.49 = (bf16[688,256]{1,0:T(8,128)(2,1)S(1)}, bf16[688,256]{1,0:T(8,128)(2,1)S(1)}, u32[]{:S(2)}, u32[]{:S(2)}) collective-permute-start(bf16[688,256]{1,0:T(8,128)(2,1)S(1)} %constant_dynamic-slice_fusion.23), channel_id=1, source_target_pairs={{0,4},{4,0},{8,12},{12,8},{16,20},{20,16},{24,28},{28,24},{1,5},{5... | collective-permute-start | bytes 1056776 | tf_op jit(solution)/shard_map/ppermute | solution.py:584
  754.3 25.9 %collective-permute-start.53 = (bf16[256,2048]{1,0:T(8,128)(2,1)}, bf16[256,2048]{1,0:T(8,128)(2,1)}, u32[]{:S(2)}, u32[]{:S(2)}) collective-permute-start(bf16[256,2048]{1,0:T(8,128)(2,1)} %get-tuple-element.326), channel_id=1, source_target_pairs={{0,4},{4,0},{8,12},{12,8},{16,20},{20,16},{24,28},{28,24},{1,5},{5... | collective-permute-start | bytes 3145736 | tf_op jit(solution)/shard_map/ppermute | solution.py:584
  755.9 25.7 %collective-permute-start.54 = (bf16[256,2048]{1,0:T(8,128)(2,1)}, bf16[256,2048]{1,0:T(8,128)(2,1)}, u32[]{:S(2)}, u32[]{:S(2)}) collective-permute-start(bf16[256,2048]{1,0:T(8,128)(2,1)} %pad_maximum_fusion.25), channel_id=1, source_target_pairs={{0,2},{1,3},{2,0},{3,1},{4,6},{5,7},{6,4},{7,5},{8,10},{9,11},{10,... | collective-permute-start | bytes 3145736 | tf_op jit(solution)/shard_map/ppermute | solution.py:588
  811.0 24.4 %collective-permute-start.59 = (bf16[256,2048]{1,0:T(8,128)(2,1)S(1)}, bf16[256,2048]{1,0:T(8,128)(2,1)S(1)}, u32[]{:S(2)}, u32[]{:S(2)}) collective-permute-start(bf16[256,2048]{1,0:T(8,128)(2,1)S(1)} %pad_maximum_fusion.26), channel_id=1, source_target_pairs={{0,2},{1,3},{2,0},{3,1},{4,6},{5,7},{6,4},{7,5},{8,10},{9,11},{10,... | collective-permute-start | bytes 3145736 | tf_op jit(solution)/shard_map/ppermute | solution.py:588
  (145 other events, 2218.1 us)
Sparse Core Ops, SparseCore 0:
  27.6 83.6 all-gather.3
  113.4 79.1 all-gather.5
  194.2 151.0 all-gather.7
  455.0 55.0 reduce-scatter.4
  527.9 106.5 reduce-scatter.6
  636.8 77.8 reduce-scatter.8
  736.8 77.8 reduce-scatter.10

commit v4 on v3

--- a/solution.py
+++ b/solution.py
@@ -821,10 +821,8 @@
     proj_weight = gathered(proj_parts)
     mid_weight = gathered(side_parts([w_gate_out.T, w_out]))
     gate_weight, out_weight = mid_weight[:vals], mid_weight[vals:]
-    mlp_parts = side_parts([w_gate.T, w_up.T, w_down])
-    mlp_weight = gathered(mlp_parts)
-    mlp_gate, mlp_up, mlp_down = (mlp_weight[i * hidden : (i + 1) * hidden] for i in range(3))
-    mlp_in = mlp_weight[: 2 * hidden]
+    mlp_in = gathered(side_parts([w_gate.T, w_up.T]))
+    mlp_down = gathered(side_parts([w_down]))
 
     small = [norm1_gain, norm2_gain, w_alpha, w_beta, conv_query, conv_key, conv_value, a_log, dt_bias, out_gain]
     flat = jnp.concatenate([s.astype(bf16).reshape(-1) for s in small])
@@ -872,12 +870,14 @@
     outputs, gated = gated_outputs(places, value_out, ident, entering, gate_pre, gain_out)
     half = row_count // 2
     mine = chip_sum(dot_rows(gated[half:], out_weight), dot_rows(gated[:half], out_weight))
-    attention = second_total(second_exchange(first_total(first_exchange(mine))))
+    attention = second_total(second_exchange(first_total(first_exchange(mine), mlp_in)))
     own_inputs = own_blocks(tokens)
     hidden_state = [x.astype(f32) + v.astype(f32) for x, v in zip(own_inputs, attention)]
     scale_second = [lax.rsqrt(jnp.mean(v * v, axis=1, keepdims=True) + eps_norm) for v in hidden_state]
     hat_second = [v * r for v, r in zip(hidden_state, scale_second)]
-    normed_second, _ = all_rows([(v * gain_second).astype(bf16) for v in hat_second], (mlp_weight,))
+    normed_second, (mlp_down,) = all_rows(
+        [(v * gain_second).astype(bf16) for v in hat_second], (), lambda after: (mlp_down,)
+    )
     act = dot_right(mlp_in, normed_second)
     gate_act, up_act = act[:hidden], act[hidden:]
     sig = jax.nn.sigmoid(gate_act)

time: 876 us -> 868 us (level)
  waiting for transfers between devices: 289 us -> 277 us
    ppermute x23 -> x24, waiting for transfers between devices: 135 us -> 92.1 us  [swap_pair(): lax.ppermute(v, 'seq', [(i, i ^ 1) for i in range(lax.axis_size('seq'))])]
    all_gather x3 -> x4, waiting for transfers between devices: 31.9 us -> 55.5 us  [gathered(): lax.all_gather(mine, 'seq', axis=1, tiled=True, axis_index_groups=lines_o...]
    ppermute x23 -> x24, starting transfers between devices: 28.4 us -> 29.6 us  [swap_pair(): lax.ppermute(v, 'seq', [(i, i ^ 1) for i in range(lax.axis_size('seq'))])]
    select_n x11 -> x12, other arithmetic: 19.4 us -> 20.5 us  [join(): jnp.where(at == 0, mine, other)]
    unnamed x219 -> x195, local copies, waits for them, and re-layouts: 26.6 us -> 26.5 us
  transfers between devices with their start and end apart: 77 -> 79, of which waited for: 46 -> 42; matrix products, arithmetic and copies ran while one was open for 31% -> 32% of each run, Pallas kernels for 13% -> 14%
where the time goes in v4:
time: 868 us; the launch traced here: 862 us
  waiting for transfers between devices  277 us (32%)
  matrix products  187 us (22%)
  other arithmetic  131 us (15%)
  Pallas kernels  119 us (14%)
  starting transfers between devices  81.2 us (9%)
  local copies, waits for them, and re-layouts  50 us (6%)
  between operations  16.7 us (2%)
    ppermute x24, waiting for transfers between devices, swap_pair(): lax.ppermute(v, 'seq', [(i, i ^ 1) for i in range(lax.axis_size('seq'))])  92.1 us
    dot_general x8, matrix products, dot_left(): lax.dot_general(a, b, (((0,), (0,)), ((), ())), preferred_element_type=f32)  63.6 us
    dot_general x5, matrix products, dot_right(): lax.dot_general(a, b, (((1,), (1,)), ((), ())), preferred_element_type=f32)  60.2 us
    dot_general x7, matrix products, dot_rows(): lax.dot_general(a, b, (((1,), (0,)), ((), ())), preferred_element_type=f32)  59.4 us
    ppermute x15, waiting for transfers between devices, swap_chip(): return lax.ppermute(v, 'head', [(i, i ^ 2) for i in range(4)])  59.4 us
    all_gather x4, waiting for transfers between devices, gathered(): lax.all_gather(mine, 'seq', axis=1, tiled=True, axis_index_groups=lines_o...  55.5 us
    pallas_call x1, Pallas kernels, delta_backward(): pl.pallas_call(functools.partial(backward_kernel, heads), grid_spec=pltpu...  52.6 us
    pallas_call x1, Pallas kernels, delta_forward(): pl.pallas_call(functools.partial(forward_kernel, heads), grid=(blocks,),...  35 us
  transfers between devices with their start and end apart: 79, of which 42 were waited for; matrix products, arithmetic and copies ran while one was open for 32% of the time, Pallas kernels for 14%

profile of v4, /device:TPU:0, one launch (start us, length us, event | category | flops | bytes accessed | tf_op | source)
XLA Modules:
  0.0 862.4 jit_solution(33010587312703386)
XLA Ops:
  14.2 11.9 %collective-permute-done = bf16[1024,256]{1,0:T(8,128)(2,1)S(1)} collective-permute-done((bf16[1024,256]{1,0:T(8,128)(2,1)S(1)}, bf16[1024,256]{1,0:T(8,128)(2,1)S(1)}, u32[]{:S(2)}, u32[]{:S(2)}) %collective-permute-start) | collective-permute-done | bytes 524320 | tf_op jit(solution)/shard_map/ppermute | solution.py:584
  52.1 36.0 %collective-permute-done.1 = bf16[512,2048]{1,0:T(8,128)(2,1)S(1)} collective-permute-done((bf16[512,2048]{1,0:T(8,128)(2,1)S(1)}, bf16[512,2048]{1,0:T(8,128)(2,1)S(1)}, u32[]{:S(2)}, u32[]{:S(2)}) %collective-permute-start.1) | collective-permute-done | bytes 2097184 | tf_op jit(solution)/shard_map/ppermute | solution.py:584
  102.5 11.7 %fusion.2.refs_1_ = bf16[2048,2048]{1,0:T(8,128)(2,1)} fusion(f32[2048]{0:T(1024)S(1)} %bitcast.160, f32[2048]{0:T(1024)S(1)} %add_rsqrt_fusion, bf16[1024,2048]{1,0:T(8,128)(2,1)S(1)} %get-tuple-element.442, bf16[1024,2048]{1,0:T(8,128)(2,1)S(1)} %get-tuple-element.441), kind=kLoop, calls=%fused_computation.4 | loop fusion | flops 29360128 | bytes 16793600 | tf_op jit(solution)/shard_map/convert_element_type | solution.py:852
  114.1 14.0 %convolution_convert_fusion.9.proj_ref.before_ref = bf16[2048,1024]{1,0:T(8,128)(2,1)} fusion(bf16[2048,2048]{1,0:T(8,128)(2,1)} %fusion.2.refs_1_, bf16[1024,2048]{1,0:T(8,128)(2,1)} %all-gather.5.cloned.1.call-done), kind=kOutput, calls=%fused_computation.42 | convolution fusion | flops 8592031744 | bytes 16777216 | tf_op jit(solution)/shard_map/dot_general | solution.py:555
  144.5 35.0 %shard_map.347 = (f32[2048,512]{1,0:T(8,128)}, bf16[2048,256]{1,0:T(8,128)(2,1)S(1)}, bf16[2048,256]{1,0:T(8,128)(2,1)S(1)}, bf16[16,2,128,384]{3,2,1,0:T(8,128)(2,1)}, f32[2,128,384]{2,1,0:T(8,128)S(1)}) custom-call(bf16[2048,1024]{1,0:T(8,128)(2,1)} %convolution_convert_fusion.9.proj_ref.before_ref, bf16[16,1024]{1,0:T(8,128)(2,1)S(1)} %collective-permute-done.6.edge_ref, ...), custom_call_target="tpu_custom_call" | custom-call | tf_op jit(solution)/shard_map/pallas_call | solution.py:169
  198.9 10.6 %fusion.100.gate_ref = f32[2048,512]{1,0:T(8,128)} fusion(bf16[2048,2048]{1,0:T(8,128)(2,1)} %fusion.2.refs_1_, bf16[1024,2048]{1,0:T(8,128)(2,1)} %all-gather.7.cloned.1.call-done), kind=kOutput, calls=%fused_computation.353 | convolution fusion | flops 4294967296 | bytes 14680064 | tf_op jit(solution)/shard_map/dot_general | solution.py:555
  221.2 8.5 pad_maximum_fusion.1.refs_0_
  229.7 8.4 shard_map.348
  244.8 8.9 %shard_map.349 = (f32[2048,512]{1,0:T(8,128)}, bf16[2048,512]{1,0:T(8,128)(2,1)S(1)}) custom-call(s32[17]{0:T(128)S(1)} %stack.131.order_ref, f32[2048,512]{1,0:T(8,128)} %get-tuple-element.198.value_ref, bf16[2048,256]{1,0:T(8,128)(2,1)S(1)} %get-tuple-element.199.ident_ref, bf16[2,128,256]{2,1,0:T(8,128)(2,1)S(1)} %collective-permute-done.9.state_ref.enter_ref, ...), custom_call_target="tpu_custom_call" | custom-call | tf_op jit(solution)/shard_map/pallas_call | solution.py:251
  272.3 28.6 %all-gather.9.cloned.1.call-done = bf16[1376,2048]{1,0:T(8,128)(2,1)} async-done(((bf16[1376,512]{1,0:T(8,128)(2,1)}), bf16[1376,2048]{1,0:T(8,128)(2,1)}) %all-gather.9.cloned.1.call-update) | async-done | bytes 5636112 | tf_op jit(solution)/shard_map/all_gather | solution.py:757
  310.3 8.7 %collective-permute-done.17 = bf16[128,2048]{1,0:T(8,128)(2,1)S(1)} collective-permute-done((bf16[128,2048]{1,0:T(8,128)(2,1)S(1)}, bf16[128,2048]{1,0:T(8,128)(2,1)S(1)}, u32[]{:S(2)}, u32[]{:S(2)}) %collective-permute-start.17) | collective-permute-done | bytes 524320 | tf_op jit(solution)/shard_map/ppermute | solution.py:588
  326.4 10.7 %collective-permute-done.19 = bf16[128,2048]{1,0:T(8,128)(2,1)S(1)} collective-permute-done((bf16[128,2048]{1,0:T(8,128)(2,1)S(1)}, bf16[128,2048]{1,0:T(8,128)(2,1)S(1)}, u32[]{:S(2)}, u32[]{:S(2)}) %collective-permute-start.19) | collective-permute-done | bytes 524320 | tf_op jit(solution)/shard_map/ppermute | solution.py:588
  340.5 26.9 %all-gather.11.cloned.1.call-done = bf16[688,2048]{1,0:T(8,128)(2,1)} async-done(((bf16[688,512]{1,0:T(8,128)(2,1)}), bf16[688,2048]{1,0:T(8,128)(2,1)}) %all-gather.11.cloned.1.call-update) | async-done | bytes 2818064 | tf_op jit(solution)/shard_map/all_gather | solution.py:757
  379.9 16.0 %fusion.136 = f32[1376,2048]{1,0:T(8,128)} fusion(bf16[1376,2048]{1,0:T(8,128)(2,1)} %all-gather.9.cloned.1.call-done, bf16[2048,2048]{1,0:T(8,128)(2,1)S(1)} %shard_map.350), kind=kOutput, calls=%fused_computation.389 | convolution fusion | flops 11542724608 | bytes 25296896 | tf_op jit(solution)/shard_map/dot_general | solution.py:555
  396.0 13.4 %multiply_convert_fusion.1 = (bf16[688,2048]{1,0:T(8,128)(2,1)S(1)}, bf16[688,2048]{1,0:T(8,128)(2,1)}, bf16[688,2048]{1,0:T(8,128)(2,1)}) fusion(f32[1376,2048]{1,0:T(8,128)} %fusion.136, bf16[688,2048]{1,0:T(8,128)(2,1)} %all-gather.11.cloned.1.call-done, bf16[2048,2048]{1,0:T(8,128)(2,1)S(1)} %bitcast.147), kind=kOutput, calls=%fused_computation.18 | convolution fusion | flops 5792497664 | bytes 30932992 | tf_op jit(solution)/shard_map/dot_general | solution.py:555
  409.4 12.2 %convolution_convert_fusion.5 = bf16[1024,2048]{1,0:T(8,128)(2,1)} fusion(bf16[1376,2048]{1,0:T(8,128)(2,1)} %all-gather.9.cloned.1.call-done, bf16[688,2048]{1,0:T(8,128)(2,1)} %get-tuple-element.435, bf16[688,2048]{1,0:T(8,128)(2,1)S(1)} %get-tuple-element.434), kind=kOutput, calls=%fused_computation.38 | convolution fusion | flops 5779095552 | bytes 15466496 | tf_op jit(solution)/shard_map/dot_general | solution.py:551
  421.7 9.6 %convolution_convert_fusion.6 = bf16[1024,2048]{1,0:T(8,128)(2,1)S(1)} fusion(bf16[1376,2048]{1,0:T(8,128)(2,1)} %all-gather.9.cloned.1.call-done, bf16[688,2048]{1,0:T(8,128)(2,1)S(1)} %copy-done.40, bf16[688,2048]{1,0:T(8,128)(2,1)} %copy-done.39), kind=kOutput, calls=%fused_computation.39 | convolution fusion | flops 5779095552 | bytes 15466496 | tf_op jit(solution)/shard_map/dot_general | solution.py:551
  444.8 7.4 convolution_convert_fusion.10
  452.3 18.2 %convolution_convert_fusion = bf16[1376,2048]{1,0:T(8,128)(2,1)} fusion(bf16[1376,2048]{1,0:T(8,128)(2,1)} %pad_maximum_fusion.2, bf16[2048,2048]{1,0:T(8,128)(2,1)} %copy-done.1), kind=kOutput, calls=%fused_computation.11 | convolution fusion | flops 11545542656 | bytes 19660800 | tf_op jit(solution)/shard_map/dot_general | solution.py:547
  473.7 12.6 %collective-permute-done.31 = bf16[128,2048]{1,0:T(8,128)(2,1)S(1)} collective-permute-done((bf16[128,2048]{1,0:T(8,128)(2,1)S(1)}, bf16[128,2048]{1,0:T(8,128)(2,1)S(1)}, u32[]{:S(2)}, u32[]{:S(2)}) %collective-permute-start.31) | collective-permute-done | bytes 524320 | tf_op jit(solution)/shard_map/ppermute | solution.py:588
  492.3 10.5 %collective-permute-done.33 = bf16[128,2048]{1,0:T(8,128)(2,1)S(1)} collective-permute-done((bf16[128,2048]{1,0:T(8,128)(2,1)S(1)}, bf16[128,2048]{1,0:T(8,128)(2,1)S(1)}, u32[]{:S(2)}, u32[]{:S(2)}) %collective-permute-start.33) | collective-permute-done | bytes 524320 | tf_op jit(solution)/shard_map/ppermute | solution.py:588
  504.5 7.9 convolution_convert_fusion.3
  525.9 12.0 %collective-permute-done.35.refs_1_ = bf16[256,2048]{1,0:T(8,128)(2,1)S(1)} collective-permute-done((bf16[256,2048]{1,0:T(8,128)(2,1)S(1)}, bf16[256,2048]{1,0:T(8,128)(2,1)S(1)}, u32[]{:S(2)}, u32[]{:S(2)}) %collective-permute-start.35) | collective-permute-done | bytes 1048608 | tf_op jit(solution)/shard_map/ppermute | solution.py:584
  559.2 9.8 %shard_map.352 = (bf16[2048,512]{1,0:T(8,128)(2,1)S(1)}, bf16[2048,512]{1,0:T(8,128)(2,1)S(1)}, f32[8,256]{1,0:T(8,128)S(1)}, f32[2,128,256]{2,1,0:T(8,128)S(1)}) custom-call(s32[17]{0:T(128)S(1)} %copy-done.15, f32[2048,512]{1,0:T(8,128)} %fusion.15.grad_ref, f32[2048,512]{1,0:T(8,128)} %get-tuple-element.272.out_ref, f32[2048,512]{1,0:T(8,128)} %fusion.100.gate_ref, ...), custom_call_target="tpu_custom_call" | custom-call | tf_op jit(solution)/shard_map/pallas_call | solution.py:306
  613.1 14.1 %reduce-scatter.7.cloned.1.call-done = bf16[1376,512]{1,0:T(8,128)(2,1)} async-done(((bf16[1376,2048]{1,0:T(8,128)(2,1)}), bf16[1376,512]{1,0:T(8,128)(2,1)}) %reduce-scatter.7.cloned.1.call-update) | async-done | bytes 1409040 | tf_op jit(solution)/shard_map/reduce_scatter | solution.py:761
  637.8 52.6 %shard_map.353 = (bf16[2048,1664]{1,0:T(8,128)(2,1)}, f32[32,1024]{1,0:T(8,128)}, f32[16,128]{1,0:T(8,128)}, f32[8,1024]{1,0:T(8,128)}) custom-call(s32[17]{0:T(128)} %copy-done.14, bf16[2048,512]{1,0:T(8,128)(2,1)} %copy-done.6, bf16[2048,1024]{1,0:T(8,128)(2,1)} %convolution_convert_fusion.9.proj_ref.before_ref, ...), custom_call_target="tpu_custom_call" | custom-call | tf_op jit(solution)/shard_map/pallas_call | solution.py:478
  692.5 7.4 collective-permute-done.52
  702.6 14.2 %fusion.6 = bf16[2048,1024]{1,0:T(8,128)(2,1)} fusion(bf16[2048,2048]{1,0:T(8,128)(2,1)} %copy-done, bf16[2048,1664]{1,0:T(8,128)(2,1)} %fusion.72), kind=kOutput, calls=%fused_computation.35 | convolution fusion | flops 8592031744 | bytes 16777216 | tf_op jit(solution)/shard_map/dot_general | solution.py:551
  716.8 12.2 %convolution_convert_fusion.2 = bf16[1024,2048]{1,0:T(8,128)(2,1)} fusion(bf16[1664,2048]{1,0:T(8,128)(2,1)} %constant_dynamic-update-slice_fusion.5, bf16[2048,1664]{1,0:T(8,128)(2,1)} %fusion.72), kind=kOutput, calls=%fused_computation.34 | convolution fusion | flops 6981419008 | bytes 14417920 | tf_op jit(solution)/shard_map/dot_general | solution.py:547
  729.1 11.2 %convolution_convert_fusion.1 = bf16[1024,2048]{1,0:T(8,128)(2,1)S(1)} fusion(bf16[1664,2048]{1,0:T(8,128)(2,1)} %constant_dynamic-update-slice_fusion.5, bf16[2048,1664]{1,0:T(8,128)(2,1)} %fusion.72), kind=kOutput, calls=%fused_computation.33 | convolution fusion | flops 6981419008 | bytes 14417920 | tf_op jit(solution)/shard_map/dot_general | solution.py:547
  759.6 13.2 %collective-permute-done.54 = bf16[256,2048]{1,0:T(8,128)(2,1)} collective-permute-done((bf16[256,2048]{1,0:T(8,128)(2,1)}, bf16[256,2048]{1,0:T(8,128)(2,1)}, u32[]{:S(2)}, u32[]{:S(2)}) %collective-permute-start.54) | collective-permute-done | bytes 1048608 | tf_op jit(solution)/shard_map/ppermute | solution.py:584
  814.6 13.2 %collective-permute-done.60 = bf16[256,2048]{1,0:T(8,128)(2,1)S(1)} collective-permute-done((bf16[256,2048]{1,0:T(8,128)(2,1)S(1)}, bf16[256,2048]{1,0:T(8,128)(2,1)S(1)}, u32[]{:S(2)}, u32[]{:S(2)}) %collective-permute-start.60) | collective-permute-done | bytes 1048608 | tf_op jit(solution)/shard_map/ppermute | solution.py:588
  (596 shorter events, 358.1 us)
Async XLA Ops:
  7.2 106.9 %all-gather.5.cloned.1.call-start = ((), (), s32[]{:S(2)}) async-start(), calls=%async_computation.4 | async-start | bytes 5242880 | tf_op jit(solution)/shard_map/all_gather | solution.py:757
  27.5 171.4 %all-gather.7.cloned.1.call-start = ((), (), s32[]{:S(2)}) async-start(), calls=%async_computation.5 | async-start | bytes 5242880 | tf_op jit(solution)/shard_map/all_gather | solution.py:757
  29.5 62.3 %collective-permute-start.12 = (bf16[1024,256]{1,0:T(8,128)(2,1)}, bf16[1024,256]{1,0:T(8,128)(2,1)}, u32[]{:S(2)}, u32[]{:S(2)}) collective-permute-start(bf16[1024,256]{1,0:T(8,128)(2,1)} %pad_maximum_fusion.33), channel_id=1, source_target_pairs={{0,4},{4,0},{8,12},{12,8},{16,20},{20,16},{24,28},{28,24},{1,5},{5... | collective-permute-start | bytes 1572872 | tf_op jit(solution)/shard_map/ppermute | solution.py:584
  35.7 52.4 %collective-permute-start.1 = (bf16[512,2048]{1,0:T(8,128)(2,1)S(1)}, bf16[512,2048]{1,0:T(8,128)(2,1)S(1)}, u32[]{:S(2)}, u32[]{:S(2)}) collective-permute-start(bf16[512,2048]{1,0:T(8,128)(2,1)S(1)} %constant_dynamic-slice_fusion.40), channel_id=1, source_target_pairs={{0,4},{4,0},{8,12},{12,8},{16,20},{20,16},{24,28},{28,24},{1,5},{5... | collective-permute-start | bytes 6291464 | tf_op jit(solution)/shard_map/ppermute | solution.py:584
  49.2 41.4 %collective-permute-start.5 = (bf16[4,4096]{1,0:T(4,128)(2,1)S(1)}, bf16[4,4096]{1,0:T(4,128)(2,1)S(1)}, u32[]{:S(2)}, u32[]{:S(2)}) collective-permute-start(bf16[4,4096]{1,0:T(4,128)(2,1)S(1)} %pad_maximum_fusion.37), channel_id=1, source_target_pairs={{0,16},{4,20},{8,24},{12,28},{16,0},{20,4},{24,8},{28,12},{1,17},{... | collective-permute-start | bytes 98312 | tf_op jit(solution)/shard_map/ppermute | solution.py:724
  89.0 90.6 %collective-permute-start.16 = (bf16[1376,256]{1,0:T(8,128)(2,1)}, bf16[1376,256]{1,0:T(8,128)(2,1)}, u32[]{:S(2)}, u32[]{:S(2)}) collective-permute-start(bf16[1376,256]{1,0:T(8,128)(2,1)} %pad_maximum_fusion.28), channel_id=1, source_target_pairs={{0,4},{4,0},{8,12},{12,8},{16,20},{20,16},{24,28},{28,24},{1,5},{5... | collective-permute-start | bytes 2113544 | tf_op jit(solution)/shard_map/ppermute | solution.py:584
  94.2 206.7 %all-gather.9.cloned.1.call-start = ((), (), s32[]{:S(2)}) async-start(), calls=%async_computation.6 | async-start | bytes 7045120 | tf_op jit(solution)/shard_map/all_gather | solution.py:757
  129.6 49.9 %collective-permute-start.10 = (bf16[512,2048]{1,0:T(8,128)(2,1)}, bf16[512,2048]{1,0:T(8,128)(2,1)}, u32[]{:S(2)}, u32[]{:S(2)}) collective-permute-start(bf16[512,2048]{1,0:T(8,128)(2,1)} %constant_dynamic-slice_fusion.26), channel_id=1, source_target_pairs={{0,4},{4,0},{8,12},{12,8},{16,20},{20,16},{24,28},{28,24},{1,5},{5... | collective-permute-start | bytes 6291464 | tf_op jit(solution)/shard_map/ppermute | solution.py:584
  179.5 35.0 %collective-permute-start.11 = (bf16[512,2048]{1,0:T(8,128)(2,1)}, bf16[512,2048]{1,0:T(8,128)(2,1)S(1)}, u32[]{:S(2)}, u32[]{:S(2)}) collective-permute-start(bf16[512,2048]{1,0:T(8,128)(2,1)} %collective-permute-done.10), channel_id=1, source_target_pairs={{0,1},{1,0},{2,3},{3,2},{4,5},{5,4},{6,7},{7,6},{8,9},{9,8},{10,11... | collective-permute-start | bytes 6291464 | tf_op jit(solution)/shard_map/ppermute | solution.py:592
  187.7 179.7 %all-gather.11.cloned.1.call-start = ((), (), s32[]{:S(2)}) async-start(), calls=%async_computation.7 | async-start | bytes 3522560 | tf_op jit(solution)/shard_map/all_gather | solution.py:757
  211.2 33.6 %collective-permute-start.9 = (bf16[2,128,256]{2,1,0:T(8,128)(2,1)}, bf16[2,128,256]{2,1,0:T(8,128)(2,1)S(1)}, u32[]{:S(2)}, u32[]{:S(2)}) collective-permute-start(bf16[2,128,256]{2,1,0:T(8,128)(2,1)} %fusion.34), channel_id=1, source_target_pairs={{0,8},{4,12},{8,16},{12,20},{16,24},{20,28},{1,9},{5,13},{9,17},{1... | collective-permute-start | bytes 393224 | tf_op jit(solution)/shard_map/ppermute | solution.py:787
  267.7 33.3 %collective-permute-start.14 = (bf16[256,2048]{1,0:T(8,128)(2,1)}, bf16[256,2048]{1,0:T(8,128)(2,1)}, u32[]{:S(2)}, u32[]{:S(2)}) collective-permute-start(bf16[256,2048]{1,0:T(8,128)(2,1)} %get-tuple-element.206), channel_id=1, source_target_pairs={{0,4},{4,0},{8,12},{12,8},{16,20},{20,16},{24,28},{28,24},{1,5},{5... | collective-permute-start | bytes 3145736 | tf_op jit(solution)/shard_map/ppermute | solution.py:584
  269.4 31.6 %collective-permute-start.15 = (bf16[256,2048]{1,0:T(8,128)(2,1)}, bf16[256,2048]{1,0:T(8,128)(2,1)}, u32[]{:S(2)}, u32[]{:S(2)}) collective-permute-start(bf16[256,2048]{1,0:T(8,128)(2,1)} %pad_maximum_fusion.13), channel_id=1, source_target_pairs={{0,2},{1,3},{2,0},{3,1},{4,6},{5,7},{6,4},{7,5},{8,10},{9,11},{10,... | collective-permute-start | bytes 3145736 | tf_op jit(solution)/shard_map/ppermute | solution.py:588
  271.7 36.4 %collective-permute-start.23 = (bf16[688,256]{1,0:T(8,128)(2,1)}, bf16[688,256]{1,0:T(8,128)(2,1)}, u32[]{:S(2)}, u32[]{:S(2)}) collective-permute-start(bf16[688,256]{1,0:T(8,128)(2,1)} %broadcast_select_fusion.30), channel_id=1, source_target_pairs={{0,4},{4,0},{8,12},{12,8},{16,20},{20,16},{24,28},{28,24},{1,5},{5... | collective-permute-start | bytes 1056776 | tf_op jit(solution)/shard_map/ppermute | solution.py:584
  310.1 194.4 %reduce-scatter.5.cloned.1.call-start = ((), (), s32[]{:S(2)}) async-start(), calls=%async_computation.8 | async-start | bytes 3522560 | tf_op jit(solution)/shard_map/reduce_scatter | solution.py:761
  337.5 29.9 %collective-permute-start.21 = (bf16[256,2048]{1,0:T(8,128)(2,1)S(1)}, bf16[256,2048]{1,0:T(8,128)(2,1)S(1)}, u32[]{:S(2)}, u32[]{:S(2)}) collective-permute-start(bf16[256,2048]{1,0:T(8,128)(2,1)S(1)} %pad_maximum_fusion.14.refs_0_), channel_id=1, source_target_pairs={{0,4},{4,0},{8,12},{12,8},{16,20},{20,16},{24,28},{28,24},{1,5},{5... | collective-permute-start | bytes 3145736 | tf_op jit(solution)/shard_map/ppermute | solution.py:584
  339.0 28.3 %collective-permute-start.22 = (bf16[256,2048]{1,0:T(8,128)(2,1)S(1)}, bf16[256,2048]{1,0:T(8,128)(2,1)}, u32[]{:S(2)}, u32[]{:S(2)}) collective-permute-start(bf16[256,2048]{1,0:T(8,128)(2,1)S(1)} %pad_maximum_fusion.15.refs_2_), channel_id=1, source_target_pairs={{0,2},{1,3},{2,0},{3,1},{4,6},{5,7},{6,4},{7,5},{8,10},{9,11},{10,... | collective-permute-start | bytes 3145736 | tf_op jit(solution)/shard_map/ppermute | solution.py:588
  441.9 28.8 %collective-permute-start.29 = (bf16[256,2048]{1,0:T(8,128)(2,1)}, bf16[256,2048]{1,0:T(8,128)(2,1)S(1)}, u32[]{:S(2)}, u32[]{:S(2)}) collective-permute-start(bf16[256,2048]{1,0:T(8,128)(2,1)} %get-tuple-element.237), channel_id=1, source_target_pairs={{0,4},{4,0},{8,12},{12,8},{16,20},{20,16},{24,28},{28,24},{1,5},{5... | collective-permute-start | bytes 3145736 | tf_op jit(solution)/shard_map/ppermute | solution.py:584
  443.4 27.3 %collective-permute-start.30 = (bf16[256,2048]{1,0:T(8,128)(2,1)}, bf16[256,2048]{1,0:T(8,128)(2,1)}, u32[]{:S(2)}, u32[]{:S(2)}) collective-permute-start(bf16[256,2048]{1,0:T(8,128)(2,1)} %pad_maximum_fusion.17), channel_id=1, source_target_pairs={{0,2},{1,3},{2,0},{3,1},{4,6},{5,7},{6,4},{7,5},{8,10},{9,11},{10,... | collective-permute-start | bytes 3145736 | tf_op jit(solution)/shard_map/ppermute | solution.py:588
  452.3 174.9 %reduce-scatter.7.cloned.1.call-start = ((), (), s32[]{:S(2)}) async-start(), calls=%async_computation.9 | async-start | bytes 7045120 | tf_op jit(solution)/shard_map/reduce_scatter | solution.py:761
  512.4 25.6 %collective-permute-start.35 = (bf16[256,2048]{1,0:T(8,128)(2,1)S(1)}, bf16[256,2048]{1,0:T(8,128)(2,1)S(1)}, u32[]{:S(2)}, u32[]{:S(2)}) collective-permute-start(bf16[256,2048]{1,0:T(8,128)(2,1)S(1)} %pad_maximum_fusion.18.refs_0_), channel_id=1, source_target_pairs={{0,4},{4,0},{8,12},{12,8},{16,20},{20,16},{24,28},{28,24},{1,5},{5... | collective-permute-start | bytes 3145736 | tf_op jit(solution)/shard_map/ppermute | solution.py:584
  513.9 25.4 %collective-permute-start.36 = (bf16[256,2048]{1,0:T(8,128)(2,1)S(1)}, bf16[256,2048]{1,0:T(8,128)(2,1)}, u32[]{:S(2)}, u32[]{:S(2)}) collective-permute-start(bf16[256,2048]{1,0:T(8,128)(2,1)S(1)} %pad_maximum_fusion.19.refs_2_), channel_id=1, source_target_pairs={{0,2},{1,3},{2,0},{3,1},{4,6},{5,7},{6,4},{7,5},{8,10},{9,11},{10,... | collective-permute-start | bytes 3145736 | tf_op jit(solution)/shard_map/ppermute | solution.py:588
  520.4 196.4 %reduce-scatter.9.cloned.1.call-start = ((), (), s32[]{:S(2)}) async-start(), calls=%async_computation.10 | async-start | bytes 5242880 | tf_op jit(solution)/shard_map/reduce_scatter | solution.py:761
  550.9 25.5 %collective-permute-start.43 = (bf16[256,2048]{1,0:T(8,128)(2,1)}, bf16[256,2048]{1,0:T(8,128)(2,1)}, u32[]{:S(2)}, u32[]{:S(2)}) collective-permute-start(bf16[256,2048]{1,0:T(8,128)(2,1)} %get-tuple-element.279), channel_id=1, source_target_pairs={{0,4},{4,0},{8,12},{12,8},{16,20},{20,16},{24,28},{28,24},{1,5},{5... | collective-permute-start | bytes 3145736 | tf_op jit(solution)/shard_map/ppermute | solution.py:584
  551.5 25.2 %collective-permute-start.44 = (bf16[256,2048]{1,0:T(8,128)(2,1)}, bf16[256,2048]{1,0:T(8,128)(2,1)}, u32[]{:S(2)}, u32[]{:S(2)}) collective-permute-start(bf16[256,2048]{1,0:T(8,128)(2,1)} %pad_maximum_fusion.21), channel_id=1, source_target_pairs={{0,2},{1,3},{2,0},{3,1},{4,6},{5,7},{6,4},{7,5},{8,10},{9,11},{10,... | collective-permute-start | bytes 3145736 | tf_op jit(solution)/shard_map/ppermute | solution.py:588
  627.9 186.7 %reduce-scatter.11.cloned.1.call-start = ((), (), s32[]{:S(2)}) async-start(), calls=%async_computation.11 | async-start | bytes 5242880 | tf_op jit(solution)/shard_map/reduce_scatter | solution.py:761
  630.9 69.1 %collective-permute-start.51 = (bf16[256,2048]{1,0:T(8,128)(2,1)S(1)}, bf16[256,2048]{1,0:T(8,128)(2,1)S(1)}, u32[]{:S(2)}, u32[]{:S(2)}) collective-permute-start(bf16[256,2048]{1,0:T(8,128)(2,1)S(1)} %constant_dynamic-update-slice_fusion.3), channel_id=1, source_target_pairs={{0,2},{1,3},{2,0},{3,1},{4,6},{5,7},{6,4},{7,5},{8,10},{9,11},{10,... | collective-permute-start | bytes 3145736 | tf_op jit(solution)/shard_map/ppermute | solution.py:588
  632.5 67.5 %collective-permute-start.49 = (bf16[1376,256]{1,0:T(8,128)(2,1)S(1)}, bf16[1376,256]{1,0:T(8,128)(2,1)S(1)}, u32[]{:S(2)}, u32[]{:S(2)}) collective-permute-start(bf16[1376,256]{1,0:T(8,128)(2,1)S(1)} %constant_dynamic-slice_fusion.24), channel_id=1, source_target_pairs={{0,4},{4,0},{8,12},{12,8},{16,20},{20,16},{24,28},{28,24},{1,5},{5... | collective-permute-start | bytes 2113544 | tf_op jit(solution)/shard_map/ppermute | solution.py:584
  637.3 62.6 %collective-permute-start.50 = (bf16[688,256]{1,0:T(8,128)(2,1)S(1)}, bf16[688,256]{1,0:T(8,128)(2,1)S(1)}, u32[]{:S(2)}, u32[]{:S(2)}) collective-permute-start(bf16[688,256]{1,0:T(8,128)(2,1)S(1)} %constant_dynamic-slice_fusion.23), channel_id=1, source_target_pairs={{0,4},{4,0},{8,12},{12,8},{16,20},{20,16},{24,28},{28,24},{1,5},{5... | collective-permute-start | bytes 1056776 | tf_op jit(solution)/shard_map/ppermute | solution.py:584
  746.7 26.0 %collective-permute-start.54 = (bf16[256,2048]{1,0:T(8,128)(2,1)}, bf16[256,2048]{1,0:T(8,128)(2,1)}, u32[]{:S(2)}, u32[]{:S(2)}) collective-permute-start(bf16[256,2048]{1,0:T(8,128)(2,1)} %get-tuple-element.328), channel_id=1, source_target_pairs={{0,4},{4,0},{8,12},{12,8},{16,20},{20,16},{24,28},{28,24},{1,5},{5... | collective-permute-start | bytes 3145736 | tf_op jit(solution)/shard_map/ppermute | solution.py:584
  748.6 25.7 %collective-permute-start.55 = (bf16[256,2048]{1,0:T(8,128)(2,1)}, bf16[256,2048]{1,0:T(8,128)(2,1)}, u32[]{:S(2)}, u32[]{:S(2)}) collective-permute-start(bf16[256,2048]{1,0:T(8,128)(2,1)} %pad_maximum_fusion.23), channel_id=1, source_target_pairs={{0,2},{1,3},{2,0},{3,1},{4,6},{5,7},{6,4},{7,5},{8,10},{9,11},{10,... | collective-permute-start | bytes 3145736 | tf_op jit(solution)/shard_map/ppermute | solution.py:588
  803.5 24.4 %collective-permute-start.60 = (bf16[256,2048]{1,0:T(8,128)(2,1)S(1)}, bf16[256,2048]{1,0:T(8,128)(2,1)S(1)}, u32[]{:S(2)}, u32[]{:S(2)}) collective-permute-start(bf16[256,2048]{1,0:T(8,128)(2,1)S(1)} %pad_maximum_fusion.24), channel_id=1, source_target_pairs={{0,2},{1,3},{2,0},{3,1},{4,6},{5,7},{6,4},{7,5},{8,10},{9,11},{10,... | collective-permute-start | bytes 3145736 | tf_op jit(solution)/shard_map/ppermute | solution.py:588
  (135 other events, 1859.1 us)
Sparse Core Ops, SparseCore 0:
  27.6 83.6 all-gather.4
  113.4 79.1 all-gather.6
  194.7 106.2 all-gather.8
  310.2 57.1 all-gather.10
  452.4 52.0 reduce-scatter.4
  520.6 106.5 reduce-scatter.6
  629.5 77.8 reduce-scatter.8
  729.2 77.9 reduce-scatter.10

commit v5 on v4

--- a/solution.py
+++ b/solution.py
@@ -368,76 +368,103 @@
     par = par_ref[...]
     lane = lax.broadcasted_iota(jnp.int32, (ROWS, 128), 1)
     row_at = lax.broadcasted_iota(jnp.int32, (ROWS, 1), 0)
+    terms, found = {}, {}
+    for s in range(span // ROWS):
+        terms[s] = decay_terms(heads, ab_ref[s * ROWS : (s + 1) * ROWS, :], par)
+
+    def tokens_of(s, h):
+        at = slice(s * ROWS, (s + 1) * ROWS)
+        log_decay, running, running_rows, strength = terms[s]
+        qs, ks, vs = h * KEY, keys + h * KEY, 2 * keys + h * VAL
+        u = conv_at(xs_ref, taps_ref, HALO + s * ROWS, qs, KEY)
+        su = sigmoid(u)
+        wu = u * su
+        ru = lax.rsqrt(jnp.sum(wu * wu, axis=1, keepdims=True) + eps_norm)
+        q = wu * (ru * KEY**-0.5)
+        y = conv_at(xs_ref, taps_ref, HALO + s * ROWS, ks, KEY)
+        sy = sigmoid(y)
+        wy = y * sy
+        ry = lax.rsqrt(jnp.sum(wy * wy, axis=1, keepdims=True) + eps_norm)
+        k = wy * ry
+        x = conv_at(xs_ref, taps_ref, HALO + s * ROWS, vs, VAL)
+        sx = sigmoid(x)
+        v = x * sx
+        yield
+        qb, kb = q.astype(bf16), k.astype(bf16)
+        beta = strength[:, heads + h : heads + h + 1]
+        passed = running[:, h : h + 1]
+        grow = jnp.exp(passed)
+        end = running[ROWS - 1 : ROWS, h : h + 1]
+        tail = jnp.exp(end - passed)
+        ratio = ratio_of(running, running_rows, h, rows, cols)
+        p = ratio * mm_nt(qb, kb)
+        t = inv_ref[at, h * KEY : (h + 1) * KEY]
+        dout = dout_ref[at, h * VAL : (h + 1) * VAL]
+        state = state_ref[s, h, :, :VAL].astype(f32) + mm(state_ref[s, h, :, VAL:], enter_ref[h])
+        state_b = state.astype(bf16)
+        yield
+        held = mm(kb, state_b)
+        yield
+        err = mm(t, beta * (v - grow * held))
+        err_b = err.astype(bf16)
+        yield
+        dp = mm_nt(dout, err_b) * ratio
+        dp_b = dp.astype(bf16)
+        from_out = mm_tn(p, dout)
+        dq = grow * mm_nt(dout, state_b) + mm(dp_b, kb)
+        yield
+        dstate = ds_ref[h]
+        dstate_b = dstate.astype(bf16)
+        derr = from_out + mm(tail * k, dstate_b)
+        yield
+        dright = mm_tn(t, derr)
+        yield
+        dright_b = dright.astype(bf16)
+        da = jnp.where(rows > cols, mm_nt(dright_b, err_b) * ratio, 0.0) * (-beta)
+        da_b = da.astype(bf16)
+        back = (beta * grow) * dright
+        back_b = back.astype(bf16)
+        ds_ref[h] = jnp.exp(end) * dstate + mm_tn(grow * q, dout) - mm_tn(kb, back_b)
+        yield
+        dk_read = mm(da_b, kb) - mm_nt(back_b, state_b)
+        dk_tail = tail * mm_nt(err_b, dstate_b)
+        dk_write = mm_tn(dp_b, qb) + mm_tn(da_b, kb) + dk_tail
+        dk = dk_read + dk_write
+        dv = beta * dright
+        to_beta = (1.0 - beta) * jnp.sum(dright * err, axis=1, keepdims=True)
+        to_decay = jnp.sum(q * dq + k * (dk_read - dk_write), axis=1, keepdims=True)
+        at_end = jnp.exp(end) * jnp.sum(
+            jnp.sum(state * dstate, axis=1, keepdims=True), axis=0, keepdims=True
+        ) + jnp.sum(jnp.sum(k * dk_tail, axis=1, keepdims=True), axis=0, keepdims=True)
+        to_decay = to_decay + jnp.where(row_at == ROWS - 1, at_end, 0.0)
+        found[s, h] = (to_decay, to_beta)
+        yield
+        along = jnp.sum(wu * dq, axis=1, keepdims=True)
+        du = (KEY**-0.5) * (ru * dq - wu * (ru * ru * ru * along))
+        gs_ref[at, qs : qs + KEY] = du * (su * (1.0 + u * (1.0 - su)))
+        along = jnp.sum(wy * dk, axis=1, keepdims=True)
+        dy = ry * dk - wy * (ry * ry * ry * along)
+        gs_ref[at, ks : ks + KEY] = dy * (sy * (1.0 + y * (1.0 - sy)))
+        gs_ref[at, vs : vs + VAL] = dv * (sx * (1.0 + x * (1.0 - sx)))
+
+    def in_step(steps, count=None):
+        while steps and count != 0:
+            steps = [one for one in steps if next(one, steps) is not steps]
+            count = None if count is None else count - 1
+        return steps
+
+    every = [tokens_of(s, h) for s in reversed(range(span // ROWS)) for h in range(heads)]
+    every = in_step(every, 5)
+    started = {s: every[i * heads : (i + 1) * heads] for i, s in enumerate(reversed(range(span // ROWS)))}
     for s in reversed(range(span // ROWS)):
         at = slice(s * ROWS, (s + 1) * ROWS)
-        ab = ab_ref[at, :]
-        log_decay, running, running_rows, strength = decay_terms(heads, ab, par)
+        ab, log_decay = ab_ref[at, :], terms[s][0]
         drunning = jnp.zeros((ROWS, 128), f32)
         dbeta = jnp.zeros((ROWS, 128), f32)
-
+        in_step(started[s])
         for h in range(heads):
-            qs, ks, vs = h * KEY, keys + h * KEY, 2 * keys + h * VAL
-            u = conv_at(xs_ref, taps_ref, HALO + s * ROWS, qs, KEY)
-            su = sigmoid(u)
-            wu = u * su
-            ru = lax.rsqrt(jnp.sum(wu * wu, axis=1, keepdims=True) + eps_norm)
-            q = wu * (ru * KEY**-0.5)
-            y = conv_at(xs_ref, taps_ref, HALO + s * ROWS, ks, KEY)
-            sy = sigmoid(y)
-            wy = y * sy
-            ry = lax.rsqrt(jnp.sum(wy * wy, axis=1, keepdims=True) + eps_norm)
-            k = wy * ry
-            x = conv_at(xs_ref, taps_ref, HALO + s * ROWS, vs, VAL)
-            sx = sigmoid(x)
-            v = x * sx
-            qb, kb = q.astype(bf16), k.astype(bf16)
-            beta = strength[:, heads + h : heads + h + 1]
-            passed = running[:, h : h + 1]
-            grow = jnp.exp(passed)
-            end = running[ROWS - 1 : ROWS, h : h + 1]
-            tail = jnp.exp(end - passed)
-            ratio = ratio_of(running, running_rows, h, rows, cols)
-            p = ratio * mm_nt(qb, kb)
-            t = inv_ref[at, h * KEY : (h + 1) * KEY]
-            dout = dout_ref[at, h * VAL : (h + 1) * VAL]
-            state = state_ref[s, h, :, :VAL].astype(f32) + mm(state_ref[s, h, :, VAL:], enter_ref[h])
-            state_b = state.astype(bf16)
-            dstate = ds_ref[h]
-            dstate_b = dstate.astype(bf16)
-            err = mm(t, beta * (v - grow * mm(kb, state_b)))
-            err_b = err.astype(bf16)
-            derr = mm_tn(p, dout) + mm(tail * k, dstate_b)
-            dright = mm_tn(t, derr)
-            dright_b = dright.astype(bf16)
-            dp = mm_nt(dout, err_b) * ratio
-            dp_b = dp.astype(bf16)
-            da = jnp.where(rows > cols, mm_nt(dright_b, err_b) * ratio, 0.0) * (-beta)
-            da_b = da.astype(bf16)
-            back = (beta * grow) * dright
-            back_b = back.astype(bf16)
-            dq = grow * mm_nt(dout, state_b) + mm(dp_b, kb)
-            dk_read = mm(da_b, kb) - mm_nt(back_b, state_b)
-            dk_tail = tail * mm_nt(err_b, dstate_b)
-            dk_write = mm_tn(dp_b, qb) + mm_tn(da_b, kb) + dk_tail
-            dk = dk_read + dk_write
-            dv = beta * dright
-            to_beta = (1.0 - beta) * jnp.sum(dright * err, axis=1, keepdims=True)
-            to_decay = jnp.sum(q * dq + k * (dk_read - dk_write), axis=1, keepdims=True)
-            at_end = jnp.exp(end) * jnp.sum(
-                jnp.sum(state * dstate, axis=1, keepdims=True), axis=0, keepdims=True
-            ) + jnp.sum(jnp.sum(k * dk_tail, axis=1, keepdims=True), axis=0, keepdims=True)
-            to_decay = to_decay + jnp.where(row_at == ROWS - 1, at_end, 0.0)
-            drunning = jnp.where(lane == h, to_decay, drunning)
-            dbeta = jnp.where(lane == heads + h, to_beta, dbeta)
-            ds_ref[h] = jnp.exp(end) * dstate + mm_tn(grow * q, dout) - mm_tn(kb, back_b)
-            along = jnp.sum(wu * dq, axis=1, keepdims=True)
-            du = (KEY**-0.5) * (ru * dq - wu * (ru * ru * ru * along))
-            gs_ref[at, qs : qs + KEY] = du * (su * (1.0 + u * (1.0 - su)))
-            along = jnp.sum(wy * dk, axis=1, keepdims=True)
-            dy = ry * dk - wy * (ry * ry * ry * along)
-            gs_ref[at, ks : ks + KEY] = dy * (sy * (1.0 + y * (1.0 - sy)))
-            gs_ref[at, vs : vs + VAL] = dv * (sx * (1.0 + x * (1.0 - sx)))
-
+            drunning = jnp.where(lane == h, found[s, h][0], drunning)
+            dbeta = jnp.where(lane == heads + h, found[s, h][1], dbeta)
         dlog = mm_full((rows <= cols).astype(f32), drunning)
         dalpha = -dlog * par[0:1, :] * sigmoid(ab + par[1:2, :])
         dproj_ref[placed_rows(order_ref, s), width + heads * VAL :] = jnp.where(lane < heads, dalpha, dbeta).astype(bf16)
@@ -446,16 +473,22 @@
 
     for lo in range(0, width, 256):
         lanes = slice(lo, lo + 256)
-        grad = gs_ref[0:span, lanes]
-        total = taps_ref[3:4, lanes] * grad
+        here = xs_ref[HALO : HALO + span, lanes]
+        total = jnp.zeros((span, 256), f32)
         for i in range(4):
-            moved = xs_ref[HALO - 3 + i : HALO - 3 + i + span, lanes] * grad
-            dtaps_ref[8 * i : 8 * i + 8, lanes] += jnp.sum(moved.reshape(-1, 8, 256), axis=0)
-            if i < 3:
-                total = total + taps_ref[i : i + 1, lanes] * gs_ref[3 - i : 3 - i + span, lanes]
+            grad = gs_ref[3 - i : 3 - i + span, lanes]
+            dtaps_ref[8 * i : 8 * i + 8, lanes] += jnp.sum((here * grad).reshape(-1, 8, 256), axis=0)
+            total = total + taps_ref[i : i + 1, lanes] * grad
         total = total.astype(bf16)
         for s in range(2):
             dproj_ref[placed_rows(order_ref, s), lanes] = total[s * ROWS : (s + 1) * ROWS]
+
+    @pl.when(step == last)
+    def _():
+        head_row = lax.broadcasted_iota(jnp.int32, (8, width), 0)
+        for i in range(3):
+            moved = gs_ref[0:8, :] * xs_ref[HALO - 3 + i : HALO + 5 + i, :]
+            dtaps_ref[8 * i : 8 * i + 8, :] += jnp.where(head_row < 3 - i, moved, 0.0)
 
     dproj_ref[:, width : width + heads * VAL] = gate_ref[...]
 

time: 868 us -> 863 us (level)
  transfers between devices with their start and end apart: 79 -> 79, of which waited for: 42 -> 42; matrix products, arithmetic and copies ran while one was open for 32% -> 32% of each run, Pallas kernels for 14% -> 13%
where the time goes in v5:
time: 863 us; the launch traced here: 858 us
  waiting for transfers between devices  277 us (32%)
  matrix products  187 us (22%)
  other arithmetic  131 us (15%)
  Pallas kernels  115 us (13%)
  starting transfers between devices  80.5 us (9%)
  local copies, waits for them, and re-layouts  50 us (6%)
  between operations  16.7 us (2%)
    ppermute x24, waiting for transfers between devices, swap_pair(): lax.ppermute(v, 'seq', [(i, i ^ 1) for i in range(lax.axis_size('seq'))])  92.2 us
    dot_general x8, matrix products, dot_left(): lax.dot_general(a, b, (((0,), (0,)), ((), ())), preferred_element_type=f32)  63.4 us
    dot_general x5, matrix products, dot_right(): lax.dot_general(a, b, (((1,), (1,)), ((), ())), preferred_element_type=f32)  60.2 us
    ppermute x15, waiting for transfers between devices, swap_chip(): return lax.ppermute(v, 'head', [(i, i ^ 2) for i in range(4)])  59.5 us
    dot_general x7, matrix products, dot_rows(): lax.dot_general(a, b, (((1,), (0,)), ((), ())), preferred_element_type=f32)  59.5 us
    all_gather x4, waiting for transfers between devices, gathered(): lax.all_gather(mine, 'seq', axis=1, tiled=True, axis_index_groups=lines_o...  55.5 us
    pallas_call x1, Pallas kernels, delta_backward(): pl.pallas_call(functools.partial(backward_kernel, heads), grid_spec=pltpu...  48.4 us
    pallas_call x1, Pallas kernels, delta_forward(): pl.pallas_call(functools.partial(forward_kernel, heads), grid=(blocks,),...  35 us
  transfers between devices with their start and end apart: 79, of which 42 were waited for; matrix products, arithmetic and copies ran while one was open for 32% of the time, Pallas kernels for 13%

profile of v5, /device:TPU:0, one launch (start us, length us, event | category | flops | bytes accessed | tf_op | source)
XLA Modules:
  0.0 857.8 jit_solution(10029045028074599533)
XLA Ops:
  14.2 11.9 %collective-permute-done = bf16[1024,256]{1,0:T(8,128)(2,1)S(1)} collective-permute-done((bf16[1024,256]{1,0:T(8,128)(2,1)S(1)}, bf16[1024,256]{1,0:T(8,128)(2,1)S(1)}, u32[]{:S(2)}, u32[]{:S(2)}) %collective-permute-start) | collective-permute-done | bytes 524320 | tf_op jit(solution)/shard_map/ppermute | solution.py:617
  52.1 36.0 %collective-permute-done.1 = bf16[512,2048]{1,0:T(8,128)(2,1)S(1)} collective-permute-done((bf16[512,2048]{1,0:T(8,128)(2,1)S(1)}, bf16[512,2048]{1,0:T(8,128)(2,1)S(1)}, u32[]{:S(2)}, u32[]{:S(2)}) %collective-permute-start.1) | collective-permute-done | bytes 2097184 | tf_op jit(solution)/shard_map/ppermute | solution.py:617
  102.5 11.7 %fusion.2.refs_1_ = bf16[2048,2048]{1,0:T(8,128)(2,1)} fusion(f32[2048]{0:T(1024)S(1)} %bitcast.160, f32[2048]{0:T(1024)S(1)} %add_rsqrt_fusion, bf16[1024,2048]{1,0:T(8,128)(2,1)S(1)} %get-tuple-element.442, bf16[1024,2048]{1,0:T(8,128)(2,1)S(1)} %get-tuple-element.441), kind=kLoop, calls=%fused_computation.4 | loop fusion | flops 29360128 | bytes 16793600 | tf_op jit(solution)/shard_map/convert_element_type | solution.py:885
  114.1 14.0 %convolution_convert_fusion.9.proj_ref.before_ref = bf16[2048,1024]{1,0:T(8,128)(2,1)} fusion(bf16[2048,2048]{1,0:T(8,128)(2,1)} %fusion.2.refs_1_, bf16[1024,2048]{1,0:T(8,128)(2,1)} %all-gather.5.cloned.1.call-done), kind=kOutput, calls=%fused_computation.42 | convolution fusion | flops 8592031744 | bytes 16777216 | tf_op jit(solution)/shard_map/dot_general | solution.py:588
  144.5 35.0 %shard_map.347 = (f32[2048,512]{1,0:T(8,128)}, bf16[2048,256]{1,0:T(8,128)(2,1)S(1)}, bf16[2048,256]{1,0:T(8,128)(2,1)S(1)}, bf16[16,2,128,384]{3,2,1,0:T(8,128)(2,1)}, f32[2,128,384]{2,1,0:T(8,128)S(1)}) custom-call(bf16[2048,1024]{1,0:T(8,128)(2,1)} %convolution_convert_fusion.9.proj_ref.before_ref, bf16[16,1024]{1,0:T(8,128)(2,1)S(1)} %collective-permute-done.6.edge_ref, ...), custom_call_target="tpu_custom_call" | custom-call | tf_op jit(solution)/shard_map/pallas_call | solution.py:169
  198.9 10.6 %fusion.100.gate_ref = f32[2048,512]{1,0:T(8,128)} fusion(bf16[2048,2048]{1,0:T(8,128)(2,1)} %fusion.2.refs_1_, bf16[1024,2048]{1,0:T(8,128)(2,1)} %all-gather.7.cloned.1.call-done), kind=kOutput, calls=%fused_computation.353 | convolution fusion | flops 4294967296 | bytes 14680064 | tf_op jit(solution)/shard_map/dot_general | solution.py:588
  221.2 8.5 pad_maximum_fusion.1.refs_0_
  229.7 8.4 shard_map.348
  244.8 8.9 %shard_map.349 = (f32[2048,512]{1,0:T(8,128)}, bf16[2048,512]{1,0:T(8,128)(2,1)S(1)}) custom-call(s32[17]{0:T(128)S(1)} %stack.131.order_ref, f32[2048,512]{1,0:T(8,128)} %get-tuple-element.198.value_ref, bf16[2048,256]{1,0:T(8,128)(2,1)S(1)} %get-tuple-element.199.ident_ref, bf16[2,128,256]{2,1,0:T(8,128)(2,1)S(1)} %collective-permute-done.9.state_ref.enter_ref, ...), custom_call_target="tpu_custom_call" | custom-call | tf_op jit(solution)/shard_map/pallas_call | solution.py:251
  272.3 28.6 %all-gather.9.cloned.1.call-done = bf16[1376,2048]{1,0:T(8,128)(2,1)} async-done(((bf16[1376,512]{1,0:T(8,128)(2,1)}), bf16[1376,2048]{1,0:T(8,128)(2,1)}) %all-gather.9.cloned.1.call-update) | async-done | bytes 5636112 | tf_op jit(solution)/shard_map/all_gather | solution.py:790
  310.3 8.7 %collective-permute-done.17 = bf16[128,2048]{1,0:T(8,128)(2,1)S(1)} collective-permute-done((bf16[128,2048]{1,0:T(8,128)(2,1)S(1)}, bf16[128,2048]{1,0:T(8,128)(2,1)S(1)}, u32[]{:S(2)}, u32[]{:S(2)}) %collective-permute-start.17) | collective-permute-done | bytes 524320 | tf_op jit(solution)/shard_map/ppermute | solution.py:621
  326.4 10.7 %collective-permute-done.19 = bf16[128,2048]{1,0:T(8,128)(2,1)S(1)} collective-permute-done((bf16[128,2048]{1,0:T(8,128)(2,1)S(1)}, bf16[128,2048]{1,0:T(8,128)(2,1)S(1)}, u32[]{:S(2)}, u32[]{:S(2)}) %collective-permute-start.19) | collective-permute-done | bytes 524320 | tf_op jit(solution)/shard_map/ppermute | solution.py:621
  340.5 26.9 %all-gather.11.cloned.1.call-done = bf16[688,2048]{1,0:T(8,128)(2,1)} async-done(((bf16[688,512]{1,0:T(8,128)(2,1)}), bf16[688,2048]{1,0:T(8,128)(2,1)}) %all-gather.11.cloned.1.call-update) | async-done | bytes 2818064 | tf_op jit(solution)/shard_map/all_gather | solution.py:790
  379.9 16.0 %fusion.136 = f32[1376,2048]{1,0:T(8,128)} fusion(bf16[1376,2048]{1,0:T(8,128)(2,1)} %all-gather.9.cloned.1.call-done, bf16[2048,2048]{1,0:T(8,128)(2,1)S(1)} %shard_map.350), kind=kOutput, calls=%fused_computation.389 | convolution fusion | flops 11542724608 | bytes 25296896 | tf_op jit(solution)/shard_map/dot_general | solution.py:588
  396.0 13.4 %multiply_convert_fusion.1 = (bf16[688,2048]{1,0:T(8,128)(2,1)S(1)}, bf16[688,2048]{1,0:T(8,128)(2,1)}, bf16[688,2048]{1,0:T(8,128)(2,1)}) fusion(f32[1376,2048]{1,0:T(8,128)} %fusion.136, bf16[688,2048]{1,0:T(8,128)(2,1)} %all-gather.11.cloned.1.call-done, bf16[2048,2048]{1,0:T(8,128)(2,1)S(1)} %bitcast.147), kind=kOutput, calls=%fused_computation.18 | convolution fusion | flops 5792497664 | bytes 30932992 | tf_op jit(solution)/shard_map/dot_general | solution.py:588
  409.4 12.2 %convolution_convert_fusion.5 = bf16[1024,2048]{1,0:T(8,128)(2,1)} fusion(bf16[1376,2048]{1,0:T(8,128)(2,1)} %all-gather.9.cloned.1.call-done, bf16[688,2048]{1,0:T(8,128)(2,1)} %get-tuple-element.435, bf16[688,2048]{1,0:T(8,128)(2,1)S(1)} %get-tuple-element.434), kind=kOutput, calls=%fused_computation.38 | convolution fusion | flops 5779095552 | bytes 15466496 | tf_op jit(solution)/shard_map/dot_general | solution.py:584
  421.7 9.6 %convolution_convert_fusion.6 = bf16[1024,2048]{1,0:T(8,128)(2,1)S(1)} fusion(bf16[1376,2048]{1,0:T(8,128)(2,1)} %all-gather.9.cloned.1.call-done, bf16[688,2048]{1,0:T(8,128)(2,1)S(1)} %copy-done.40, bf16[688,2048]{1,0:T(8,128)(2,1)} %copy-done.39), kind=kOutput, calls=%fused_computation.39 | convolution fusion | flops 5779095552 | bytes 15466496 | tf_op jit(solution)/shard_map/dot_general | solution.py:584
  444.8 7.4 convolution_convert_fusion.10
  452.3 18.2 %convolution_convert_fusion = bf16[1376,2048]{1,0:T(8,128)(2,1)} fusion(bf16[1376,2048]{1,0:T(8,128)(2,1)} %pad_maximum_fusion.2, bf16[2048,2048]{1,0:T(8,128)(2,1)} %copy-done.1), kind=kOutput, calls=%fused_computation.11 | convolution fusion | flops 11545542656 | bytes 19660800 | tf_op jit(solution)/shard_map/dot_general | solution.py:580
  473.7 12.6 %collective-permute-done.31 = bf16[128,2048]{1,0:T(8,128)(2,1)S(1)} collective-permute-done((bf16[128,2048]{1,0:T(8,128)(2,1)S(1)}, bf16[128,2048]{1,0:T(8,128)(2,1)S(1)}, u32[]{:S(2)}, u32[]{:S(2)}) %collective-permute-start.31) | collective-permute-done | bytes 524320 | tf_op jit(solution)/shard_map/ppermute | solution.py:621
  492.3 10.5 %collective-permute-done.33 = bf16[128,2048]{1,0:T(8,128)(2,1)S(1)} collective-permute-done((bf16[128,2048]{1,0:T(8,128)(2,1)S(1)}, bf16[128,2048]{1,0:T(8,128)(2,1)S(1)}, u32[]{:S(2)}, u32[]{:S(2)}) %collective-permute-start.33) | collective-permute-done | bytes 524320 | tf_op jit(solution)/shard_map/ppermute | solution.py:621
  504.5 7.9 convolution_convert_fusion.3
  525.9 12.0 %collective-permute-done.35.refs_1_ = bf16[256,2048]{1,0:T(8,128)(2,1)S(1)} collective-permute-done((bf16[256,2048]{1,0:T(8,128)(2,1)S(1)}, bf16[256,2048]{1,0:T(8,128)(2,1)S(1)}, u32[]{:S(2)}, u32[]{:S(2)}) %collective-permute-start.35) | collective-permute-done | bytes 1048608 | tf_op jit(solution)/shard_map/ppermute | solution.py:617
  559.3 9.8 %shard_map.352 = (bf16[2048,512]{1,0:T(8,128)(2,1)S(1)}, bf16[2048,512]{1,0:T(8,128)(2,1)S(1)}, f32[8,256]{1,0:T(8,128)S(1)}, f32[2,128,256]{2,1,0:T(8,128)S(1)}) custom-call(s32[17]{0:T(128)S(1)} %copy-done.15, f32[2048,512]{1,0:T(8,128)} %fusion.15.grad_ref, f32[2048,512]{1,0:T(8,128)} %get-tuple-element.272.out_ref, f32[2048,512]{1,0:T(8,128)} %fusion.100.gate_ref, ...), custom_call_target="tpu_custom_call" | custom-call | tf_op jit(solution)/shard_map/pallas_call | solution.py:306
  613.6 13.5 %reduce-scatter.7.cloned.1.call-done = bf16[1376,512]{1,0:T(8,128)(2,1)} async-done(((bf16[1376,2048]{1,0:T(8,128)(2,1)}), bf16[1376,512]{1,0:T(8,128)(2,1)}) %reduce-scatter.7.cloned.1.call-update) | async-done | bytes 1409040 | tf_op jit(solution)/shard_map/reduce_scatter | solution.py:794
  637.8 48.4 %shard_map.353 = (bf16[2048,1664]{1,0:T(8,128)(2,1)}, f32[32,1024]{1,0:T(8,128)}, f32[16,128]{1,0:T(8,128)}, f32[8,1024]{1,0:T(8,128)}) custom-call(s32[17]{0:T(128)} %copy-done.14, bf16[2048,512]{1,0:T(8,128)(2,1)} %copy-done.6, bf16[2048,1024]{1,0:T(8,128)(2,1)} %convolution_convert_fusion.9.proj_ref.before_ref, ...), custom_call_target="tpu_custom_call" | custom-call | tf_op jit(solution)/shard_map/pallas_call | solution.py:511
  688.4 6.5 collective-permute-done.52
  697.6 14.0 %fusion.6 = bf16[2048,1024]{1,0:T(8,128)(2,1)} fusion(bf16[2048,2048]{1,0:T(8,128)(2,1)} %copy-done, bf16[2048,1664]{1,0:T(8,128)(2,1)} %fusion.72), kind=kOutput, calls=%fused_computation.35 | convolution fusion | flops 8592031744 | bytes 16777216 | tf_op jit(solution)/shard_map/dot_general | solution.py:584
  711.6 12.2 %convolution_convert_fusion.2 = bf16[1024,2048]{1,0:T(8,128)(2,1)} fusion(bf16[1664,2048]{1,0:T(8,128)(2,1)} %constant_dynamic-update-slice_fusion.5, bf16[2048,1664]{1,0:T(8,128)(2,1)} %fusion.72), kind=kOutput, calls=%fused_computation.34 | convolution fusion | flops 6981419008 | bytes 14417920 | tf_op jit(solution)/shard_map/dot_general | solution.py:580
  723.9 11.2 %convolution_convert_fusion.1 = bf16[1024,2048]{1,0:T(8,128)(2,1)S(1)} fusion(bf16[1664,2048]{1,0:T(8,128)(2,1)} %constant_dynamic-update-slice_fusion.5, bf16[2048,1664]{1,0:T(8,128)(2,1)} %fusion.72), kind=kOutput, calls=%fused_computation.33 | convolution fusion | flops 6981419008 | bytes 14417920 | tf_op jit(solution)/shard_map/dot_general | solution.py:580
  755.4 12.1 %collective-permute-done.54 = bf16[256,2048]{1,0:T(8,128)(2,1)} collective-permute-done((bf16[256,2048]{1,0:T(8,128)(2,1)}, bf16[256,2048]{1,0:T(8,128)(2,1)}, u32[]{:S(2)}, u32[]{:S(2)}) %collective-permute-start.54) | collective-permute-done | bytes 1048608 | tf_op jit(solution)/shard_map/ppermute | solution.py:617
  810.2 13.4 %collective-permute-done.60 = bf16[256,2048]{1,0:T(8,128)(2,1)S(1)} collective-permute-done((bf16[256,2048]{1,0:T(8,128)(2,1)S(1)}, bf16[256,2048]{1,0:T(8,128)(2,1)S(1)}, u32[]{:S(2)}, u32[]{:S(2)}) %collective-permute-start.60) | collective-permute-done | bytes 1048608 | tf_op jit(solution)/shard_map/ppermute | solution.py:621
  (596 shorter events, 360.1 us)
Async XLA Ops:
  7.2 106.9 %all-gather.5.cloned.1.call-start = ((), (), s32[]{:S(2)}) async-start(), calls=%async_computation.4 | async-start | bytes 5242880 | tf_op jit(solution)/shard_map/all_gather | solution.py:790
  27.5 171.4 %all-gather.7.cloned.1.call-start = ((), (), s32[]{:S(2)}) async-start(), calls=%async_computation.5 | async-start | bytes 5242880 | tf_op jit(solution)/shard_map/all_gather | solution.py:790
  29.5 62.3 %collective-permute-start.12 = (bf16[1024,256]{1,0:T(8,128)(2,1)}, bf16[1024,256]{1,0:T(8,128)(2,1)}, u32[]{:S(2)}, u32[]{:S(2)}) collective-permute-start(bf16[1024,256]{1,0:T(8,128)(2,1)} %pad_maximum_fusion.33), channel_id=1, source_target_pairs={{0,4},{4,0},{8,12},{12,8},{16,20},{20,16},{24,28},{28,24},{1,5},{5... | collective-permute-start | bytes 1572872 | tf_op jit(solution)/shard_map/ppermute | solution.py:617
  35.7 52.4 %collective-permute-start.1 = (bf16[512,2048]{1,0:T(8,128)(2,1)S(1)}, bf16[512,2048]{1,0:T(8,128)(2,1)S(1)}, u32[]{:S(2)}, u32[]{:S(2)}) collective-permute-start(bf16[512,2048]{1,0:T(8,128)(2,1)S(1)} %constant_dynamic-slice_fusion.40), channel_id=1, source_target_pairs={{0,4},{4,0},{8,12},{12,8},{16,20},{20,16},{24,28},{28,24},{1,5},{5... | collective-permute-start | bytes 6291464 | tf_op jit(solution)/shard_map/ppermute | solution.py:617
  49.2 41.4 %collective-permute-start.5 = (bf16[4,4096]{1,0:T(4,128)(2,1)S(1)}, bf16[4,4096]{1,0:T(4,128)(2,1)S(1)}, u32[]{:S(2)}, u32[]{:S(2)}) collective-permute-start(bf16[4,4096]{1,0:T(4,128)(2,1)S(1)} %pad_maximum_fusion.37), channel_id=1, source_target_pairs={{0,16},{4,20},{8,24},{12,28},{16,0},{20,4},{24,8},{28,12},{1,17},{... | collective-permute-start | bytes 98312 | tf_op jit(solution)/shard_map/ppermute | solution.py:757
  89.0 90.6 %collective-permute-start.16 = (bf16[1376,256]{1,0:T(8,128)(2,1)}, bf16[1376,256]{1,0:T(8,128)(2,1)}, u32[]{:S(2)}, u32[]{:S(2)}) collective-permute-start(bf16[1376,256]{1,0:T(8,128)(2,1)} %pad_maximum_fusion.28), channel_id=1, source_target_pairs={{0,4},{4,0},{8,12},{12,8},{16,20},{20,16},{24,28},{28,24},{1,5},{5... | collective-permute-start | bytes 2113544 | tf_op jit(solution)/shard_map/ppermute | solution.py:617
  94.2 206.7 %all-gather.9.cloned.1.call-start = ((), (), s32[]{:S(2)}) async-start(), calls=%async_computation.6 | async-start | bytes 7045120 | tf_op jit(solution)/shard_map/all_gather | solution.py:790
  129.6 49.9 %collective-permute-start.10 = (bf16[512,2048]{1,0:T(8,128)(2,1)}, bf16[512,2048]{1,0:T(8,128)(2,1)}, u32[]{:S(2)}, u32[]{:S(2)}) collective-permute-start(bf16[512,2048]{1,0:T(8,128)(2,1)} %constant_dynamic-slice_fusion.26), channel_id=1, source_target_pairs={{0,4},{4,0},{8,12},{12,8},{16,20},{20,16},{24,28},{28,24},{1,5},{5... | collective-permute-start | bytes 6291464 | tf_op jit(solution)/shard_map/ppermute | solution.py:617
  179.5 35.0 %collective-permute-start.11 = (bf16[512,2048]{1,0:T(8,128)(2,1)}, bf16[512,2048]{1,0:T(8,128)(2,1)S(1)}, u32[]{:S(2)}, u32[]{:S(2)}) collective-permute-start(bf16[512,2048]{1,0:T(8,128)(2,1)} %collective-permute-done.10), channel_id=1, source_target_pairs={{0,1},{1,0},{2,3},{3,2},{4,5},{5,4},{6,7},{7,6},{8,9},{9,8},{10,11... | collective-permute-start | bytes 6291464 | tf_op jit(solution)/shard_map/ppermute | solution.py:625
  187.7 179.7 %all-gather.11.cloned.1.call-start = ((), (), s32[]{:S(2)}) async-start(), calls=%async_computation.7 | async-start | bytes 3522560 | tf_op jit(solution)/shard_map/all_gather | solution.py:790
  211.2 33.6 %collective-permute-start.9 = (bf16[2,128,256]{2,1,0:T(8,128)(2,1)}, bf16[2,128,256]{2,1,0:T(8,128)(2,1)S(1)}, u32[]{:S(2)}, u32[]{:S(2)}) collective-permute-start(bf16[2,128,256]{2,1,0:T(8,128)(2,1)} %fusion.34), channel_id=1, source_target_pairs={{0,8},{4,12},{8,16},{12,20},{16,24},{20,28},{1,9},{5,13},{9,17},{1... | collective-permute-start | bytes 393224 | tf_op jit(solution)/shard_map/ppermute | solution.py:820
  267.7 33.3 %collective-permute-start.14 = (bf16[256,2048]{1,0:T(8,128)(2,1)}, bf16[256,2048]{1,0:T(8,128)(2,1)}, u32[]{:S(2)}, u32[]{:S(2)}) collective-permute-start(bf16[256,2048]{1,0:T(8,128)(2,1)} %get-tuple-element.206), channel_id=1, source_target_pairs={{0,4},{4,0},{8,12},{12,8},{16,20},{20,16},{24,28},{28,24},{1,5},{5... | collective-permute-start | bytes 3145736 | tf_op jit(solution)/shard_map/ppermute | solution.py:617
  269.4 31.6 %collective-permute-start.15 = (bf16[256,2048]{1,0:T(8,128)(2,1)}, bf16[256,2048]{1,0:T(8,128)(2,1)}, u32[]{:S(2)}, u32[]{:S(2)}) collective-permute-start(bf16[256,2048]{1,0:T(8,128)(2,1)} %pad_maximum_fusion.13), channel_id=1, source_target_pairs={{0,2},{1,3},{2,0},{3,1},{4,6},{5,7},{6,4},{7,5},{8,10},{9,11},{10,... | collective-permute-start | bytes 3145736 | tf_op jit(solution)/shard_map/ppermute | solution.py:621
  271.7 36.4 %collective-permute-start.23 = (bf16[688,256]{1,0:T(8,128)(2,1)}, bf16[688,256]{1,0:T(8,128)(2,1)}, u32[]{:S(2)}, u32[]{:S(2)}) collective-permute-start(bf16[688,256]{1,0:T(8,128)(2,1)} %broadcast_select_fusion.30), channel_id=1, source_target_pairs={{0,4},{4,0},{8,12},{12,8},{16,20},{20,16},{24,28},{28,24},{1,5},{5... | collective-permute-start | bytes 1056776 | tf_op jit(solution)/shard_map/ppermute | solution.py:617
  310.1 194.4 %reduce-scatter.5.cloned.1.call-start = ((), (), s32[]{:S(2)}) async-start(), calls=%async_computation.8 | async-start | bytes 3522560 | tf_op jit(solution)/shard_map/reduce_scatter | solution.py:794
  337.5 29.9 %collective-permute-start.21 = (bf16[256,2048]{1,0:T(8,128)(2,1)S(1)}, bf16[256,2048]{1,0:T(8,128)(2,1)S(1)}, u32[]{:S(2)}, u32[]{:S(2)}) collective-permute-start(bf16[256,2048]{1,0:T(8,128)(2,1)S(1)} %pad_maximum_fusion.14.refs_0_), channel_id=1, source_target_pairs={{0,4},{4,0},{8,12},{12,8},{16,20},{20,16},{24,28},{28,24},{1,5},{5... | collective-permute-start | bytes 3145736 | tf_op jit(solution)/shard_map/ppermute | solution.py:617
  339.0 28.3 %collective-permute-start.22 = (bf16[256,2048]{1,0:T(8,128)(2,1)S(1)}, bf16[256,2048]{1,0:T(8,128)(2,1)}, u32[]{:S(2)}, u32[]{:S(2)}) collective-permute-start(bf16[256,2048]{1,0:T(8,128)(2,1)S(1)} %pad_maximum_fusion.15.refs_2_), channel_id=1, source_target_pairs={{0,2},{1,3},{2,0},{3,1},{4,6},{5,7},{6,4},{7,5},{8,10},{9,11},{10,... | collective-permute-start | bytes 3145736 | tf_op jit(solution)/shard_map/ppermute | solution.py:621
  441.9 28.8 %collective-permute-start.29 = (bf16[256,2048]{1,0:T(8,128)(2,1)}, bf16[256,2048]{1,0:T(8,128)(2,1)S(1)}, u32[]{:S(2)}, u32[]{:S(2)}) collective-permute-start(bf16[256,2048]{1,0:T(8,128)(2,1)} %get-tuple-element.237), channel_id=1, source_target_pairs={{0,4},{4,0},{8,12},{12,8},{16,20},{20,16},{24,28},{28,24},{1,5},{5... | collective-permute-start | bytes 3145736 | tf_op jit(solution)/shard_map/ppermute | solution.py:617
  443.4 27.3 %collective-permute-start.30 = (bf16[256,2048]{1,0:T(8,128)(2,1)}, bf16[256,2048]{1,0:T(8,128)(2,1)}, u32[]{:S(2)}, u32[]{:S(2)}) collective-permute-start(bf16[256,2048]{1,0:T(8,128)(2,1)} %pad_maximum_fusion.17), channel_id=1, source_target_pairs={{0,2},{1,3},{2,0},{3,1},{4,6},{5,7},{6,4},{7,5},{8,10},{9,11},{10,... | collective-permute-start | bytes 3145736 | tf_op jit(solution)/shard_map/ppermute | solution.py:621
  452.3 174.9 %reduce-scatter.7.cloned.1.call-start = ((), (), s32[]{:S(2)}) async-start(), calls=%async_computation.9 | async-start | bytes 7045120 | tf_op jit(solution)/shard_map/reduce_scatter | solution.py:794
  512.4 25.6 %collective-permute-start.35 = (bf16[256,2048]{1,0:T(8,128)(2,1)S(1)}, bf16[256,2048]{1,0:T(8,128)(2,1)S(1)}, u32[]{:S(2)}, u32[]{:S(2)}) collective-permute-start(bf16[256,2048]{1,0:T(8,128)(2,1)S(1)} %pad_maximum_fusion.18.refs_0_), channel_id=1, source_target_pairs={{0,4},{4,0},{8,12},{12,8},{16,20},{20,16},{24,28},{28,24},{1,5},{5... | collective-permute-start | bytes 3145736 | tf_op jit(solution)/shard_map/ppermute | solution.py:617
  513.9 25.4 %collective-permute-start.36 = (bf16[256,2048]{1,0:T(8,128)(2,1)S(1)}, bf16[256,2048]{1,0:T(8,128)(2,1)}, u32[]{:S(2)}, u32[]{:S(2)}) collective-permute-start(bf16[256,2048]{1,0:T(8,128)(2,1)S(1)} %pad_maximum_fusion.19.refs_2_), channel_id=1, source_target_pairs={{0,2},{1,3},{2,0},{3,1},{4,6},{5,7},{6,4},{7,5},{8,10},{9,11},{10,... | collective-permute-start | bytes 3145736 | tf_op jit(solution)/shard_map/ppermute | solution.py:621
  520.4 191.2 %reduce-scatter.9.cloned.1.call-start = ((), (), s32[]{:S(2)}) async-start(), calls=%async_computation.10 | async-start | bytes 5242880 | tf_op jit(solution)/shard_map/reduce_scatter | solution.py:794
  551.1 25.5 %collective-permute-start.43 = (bf16[256,2048]{1,0:T(8,128)(2,1)}, bf16[256,2048]{1,0:T(8,128)(2,1)}, u32[]{:S(2)}, u32[]{:S(2)}) collective-permute-start(bf16[256,2048]{1,0:T(8,128)(2,1)} %get-tuple-element.279), channel_id=1, source_target_pairs={{0,4},{4,0},{8,12},{12,8},{16,20},{20,16},{24,28},{28,24},{1,5},{5... | collective-permute-start | bytes 3145736 | tf_op jit(solution)/shard_map/ppermute | solution.py:617
  551.7 25.2 %collective-permute-start.44 = (bf16[256,2048]{1,0:T(8,128)(2,1)}, bf16[256,2048]{1,0:T(8,128)(2,1)}, u32[]{:S(2)}, u32[]{:S(2)}) collective-permute-start(bf16[256,2048]{1,0:T(8,128)(2,1)} %pad_maximum_fusion.21), channel_id=1, source_target_pairs={{0,2},{1,3},{2,0},{3,1},{4,6},{5,7},{6,4},{7,5},{8,10},{9,11},{10,... | collective-permute-start | bytes 3145736 | tf_op jit(solution)/shard_map/ppermute | solution.py:621
  627.9 182.3 %reduce-scatter.11.cloned.1.call-start = ((), (), s32[]{:S(2)}) async-start(), calls=%async_computation.11 | async-start | bytes 5242880 | tf_op jit(solution)/shard_map/reduce_scatter | solution.py:794
  630.9 64.1 %collective-permute-start.51 = (bf16[256,2048]{1,0:T(8,128)(2,1)S(1)}, bf16[256,2048]{1,0:T(8,128)(2,1)S(1)}, u32[]{:S(2)}, u32[]{:S(2)}) collective-permute-start(bf16[256,2048]{1,0:T(8,128)(2,1)S(1)} %constant_dynamic-update-slice_fusion.3), channel_id=1, source_target_pairs={{0,2},{1,3},{2,0},{3,1},{4,6},{5,7},{6,4},{7,5},{8,10},{9,11},{10,... | collective-permute-start | bytes 3145736 | tf_op jit(solution)/shard_map/ppermute | solution.py:621
  632.5 62.5 %collective-permute-start.49 = (bf16[1376,256]{1,0:T(8,128)(2,1)S(1)}, bf16[1376,256]{1,0:T(8,128)(2,1)S(1)}, u32[]{:S(2)}, u32[]{:S(2)}) collective-permute-start(bf16[1376,256]{1,0:T(8,128)(2,1)S(1)} %constant_dynamic-slice_fusion.24), channel_id=1, source_target_pairs={{0,4},{4,0},{8,12},{12,8},{16,20},{20,16},{24,28},{28,24},{1,5},{5... | collective-permute-start | bytes 2113544 | tf_op jit(solution)/shard_map/ppermute | solution.py:617
  637.3 57.6 %collective-permute-start.50 = (bf16[688,256]{1,0:T(8,128)(2,1)S(1)}, bf16[688,256]{1,0:T(8,128)(2,1)S(1)}, u32[]{:S(2)}, u32[]{:S(2)}) collective-permute-start(bf16[688,256]{1,0:T(8,128)(2,1)S(1)} %constant_dynamic-slice_fusion.23), channel_id=1, source_target_pairs={{0,4},{4,0},{8,12},{12,8},{16,20},{20,16},{24,28},{28,24},{1,5},{5... | collective-permute-start | bytes 1056776 | tf_op jit(solution)/shard_map/ppermute | solution.py:617
  741.6 25.9 %collective-permute-start.54 = (bf16[256,2048]{1,0:T(8,128)(2,1)}, bf16[256,2048]{1,0:T(8,128)(2,1)}, u32[]{:S(2)}, u32[]{:S(2)}) collective-permute-start(bf16[256,2048]{1,0:T(8,128)(2,1)} %get-tuple-element.328), channel_id=1, source_target_pairs={{0,4},{4,0},{8,12},{12,8},{16,20},{20,16},{24,28},{28,24},{1,5},{5... | collective-permute-start | bytes 3145736 | tf_op jit(solution)/shard_map/ppermute | solution.py:617
  743.0 25.6 %collective-permute-start.55 = (bf16[256,2048]{1,0:T(8,128)(2,1)}, bf16[256,2048]{1,0:T(8,128)(2,1)}, u32[]{:S(2)}, u32[]{:S(2)}) collective-permute-start(bf16[256,2048]{1,0:T(8,128)(2,1)} %pad_maximum_fusion.23), channel_id=1, source_target_pairs={{0,2},{1,3},{2,0},{3,1},{4,6},{5,7},{6,4},{7,5},{8,10},{9,11},{10,... | collective-permute-start | bytes 3145736 | tf_op jit(solution)/shard_map/ppermute | solution.py:621
  799.3 24.3 %collective-permute-start.60 = (bf16[256,2048]{1,0:T(8,128)(2,1)S(1)}, bf16[256,2048]{1,0:T(8,128)(2,1)S(1)}, u32[]{:S(2)}, u32[]{:S(2)}) collective-permute-start(bf16[256,2048]{1,0:T(8,128)(2,1)S(1)} %pad_maximum_fusion.24), channel_id=1, source_target_pairs={{0,2},{1,3},{2,0},{3,1},{4,6},{5,7},{6,4},{7,5},{8,10},{9,11},{10,... | collective-permute-start | bytes 3145736 | tf_op jit(solution)/shard_map/ppermute | solution.py:621
  (135 other events, 1852.4 us)
Sparse Core Ops, SparseCore 0:
  27.6 83.6 all-gather.4
  113.4 79.1 all-gather.6
  194.7 106.2 all-gather.8
  310.2 57.1 all-gather.10
  452.4 52.0 reduce-scatter.4
  520.6 106.5 reduce-scatter.6
  629.5 77.8 reduce-scatter.8
  724.1 77.9 reduce-scatter.10

commit v6 on v5

--- a/solution.py
+++ b/solution.py
@@ -282,7 +282,7 @@
     gain = gain_ref[0:1, :]
     for h in range(heads):
         span = slice(h * VAL, (h + 1) * VAL)
-        grad = jnp.concatenate([grad_ref[placed_rows(order_ref, sub), span] for sub in range(2)], axis=0)
+        grad = jnp.concatenate([grad_ref[placed_rows(order_ref, sub), span] for sub in range(2)], axis=0).astype(f32)
         out, gate = out_ref[:, span], gate_ref[:, span]
         scale = lax.rsqrt(jnp.mean(out * out, axis=1, keepdims=True) + eps_norm)
         unit = out * scale
@@ -945,7 +945,7 @@
     attention_rounded, (branch,) = all_rows(attention_rounded, (), branch_beside)
     branch, attention_rounded = together(branch, attention_rounded)
     branch = first_exchange(branch)
-    grad_gated = dot_right(attention_rounded, out_weight)
+    grad_gated = dot_right(attention_rounded, out_weight).astype(bf16)
     grad_outputs, grad_gate, grad_gain_out, local_pull = gate_backward(
         places, grad_gated, outputs, gate_pre, gain_out, ident
     )

time: 863 us -> 863 us (level)
  no operation moved by 1% of the time
where the time goes in v6:
time: 863 us; the launch traced here: 858 us
  waiting for transfers between devices  278 us (32%)
  matrix products  187 us (22%)
  other arithmetic  131 us (15%)
  Pallas kernels  115 us (13%)
  starting transfers between devices  80.5 us (9%)
  local copies, waits for them, and re-layouts  50 us (6%)
  between operations  16.7 us (2%)
    ppermute x24, waiting for transfers between devices, swap_pair(): lax.ppermute(v, 'seq', [(i, i ^ 1) for i in range(lax.axis_size('seq'))])  92.9 us
    dot_general x8, matrix products, dot_left(): lax.dot_general(a, b, (((0,), (0,)), ((), ())), preferred_element_type=f32)  63.4 us
    dot_general x5, matrix products, dot_right(): lax.dot_general(a, b, (((1,), (1,)), ((), ())), preferred_element_type=f32)  59.7 us
    ppermute x15, waiting for transfers between devices, swap_chip(): return lax.ppermute(v, 'head', [(i, i ^ 2) for i in range(4)])  59.5 us
    dot_general x7, matrix products, dot_rows(): lax.dot_general(a, b, (((1,), (0,)), ((), ())), preferred_element_type=f32)  59.5 us
    all_gather x4, waiting for transfers between devices, gathered(): lax.all_gather(mine, 'seq', axis=1, tiled=True, axis_index_groups=lines_o...  55.5 us
    pallas_call x1, Pallas kernels, delta_backward(): pl.pallas_call(functools.partial(backward_kernel, heads), grid_spec=pltpu...  48.4 us
    pallas_call x1, Pallas kernels, delta_forward(): pl.pallas_call(functools.partial(forward_kernel, heads), grid=(blocks,),...  35 us
  transfers between devices with their start and end apart: 79, of which 42 were waited for; matrix products, arithmetic and copies ran while one was open for 32% of the time, Pallas kernels for 13%

profile of v6, /device:TPU:0, one launch (start us, length us, event | category | flops | bytes accessed | tf_op | source)
XLA Modules:
  0.0 857.7 jit_solution(16789646352976301861)
XLA Ops:
  14.2 11.9 %collective-permute-done = bf16[1024,256]{1,0:T(8,128)(2,1)S(1)} collective-permute-done((bf16[1024,256]{1,0:T(8,128)(2,1)S(1)}, bf16[1024,256]{1,0:T(8,128)(2,1)S(1)}, u32[]{:S(2)}, u32[]{:S(2)}) %collective-permute-start) | collective-permute-done | bytes 524320 | tf_op jit(solution)/shard_map/ppermute | solution.py:617
  52.1 36.0 %collective-permute-done.1 = bf16[512,2048]{1,0:T(8,128)(2,1)S(1)} collective-permute-done((bf16[512,2048]{1,0:T(8,128)(2,1)S(1)}, bf16[512,2048]{1,0:T(8,128)(2,1)S(1)}, u32[]{:S(2)}, u32[]{:S(2)}) %collective-permute-start.1) | collective-permute-done | bytes 2097184 | tf_op jit(solution)/shard_map/ppermute | solution.py:617
  102.5 11.7 %fusion.2.refs_1_ = bf16[2048,2048]{1,0:T(8,128)(2,1)} fusion(f32[2048]{0:T(1024)S(1)} %bitcast.160, f32[2048]{0:T(1024)S(1)} %add_rsqrt_fusion, bf16[1024,2048]{1,0:T(8,128)(2,1)S(1)} %get-tuple-element.442, bf16[1024,2048]{1,0:T(8,128)(2,1)S(1)} %get-tuple-element.441), kind=kLoop, calls=%fused_computation.4 | loop fusion | flops 29360128 | bytes 16793600 | tf_op jit(solution)/shard_map/convert_element_type | solution.py:885
  114.1 14.0 %convolution_convert_fusion.9.proj_ref.before_ref = bf16[2048,1024]{1,0:T(8,128)(2,1)} fusion(bf16[2048,2048]{1,0:T(8,128)(2,1)} %fusion.2.refs_1_, bf16[1024,2048]{1,0:T(8,128)(2,1)} %all-gather.5.cloned.1.call-done), kind=kOutput, calls=%fused_computation.42 | convolution fusion | flops 8592031744 | bytes 16777216 | tf_op jit(solution)/shard_map/dot_general | solution.py:588
  144.5 35.0 %shard_map.347 = (f32[2048,512]{1,0:T(8,128)}, bf16[2048,256]{1,0:T(8,128)(2,1)S(1)}, bf16[2048,256]{1,0:T(8,128)(2,1)S(1)}, bf16[16,2,128,384]{3,2,1,0:T(8,128)(2,1)}, f32[2,128,384]{2,1,0:T(8,128)S(1)}) custom-call(bf16[2048,1024]{1,0:T(8,128)(2,1)} %convolution_convert_fusion.9.proj_ref.before_ref, bf16[16,1024]{1,0:T(8,128)(2,1)S(1)} %collective-permute-done.6.edge_ref, ...), custom_call_target="tpu_custom_call" | custom-call | tf_op jit(solution)/shard_map/pallas_call | solution.py:169
  198.9 10.6 %fusion.99.gate_ref = f32[2048,512]{1,0:T(8,128)} fusion(bf16[2048,2048]{1,0:T(8,128)(2,1)} %fusion.2.refs_1_, bf16[1024,2048]{1,0:T(8,128)(2,1)} %all-gather.7.cloned.1.call-done), kind=kOutput, calls=%fused_computation.353 | convolution fusion | flops 4294967296 | bytes 14680064 | tf_op jit(solution)/shard_map/dot_general | solution.py:588
  221.2 8.5 pad_maximum_fusion.1.refs_0_
  229.7 8.4 shard_map.348
  244.8 8.9 %shard_map.349 = (f32[2048,512]{1,0:T(8,128)}, bf16[2048,512]{1,0:T(8,128)(2,1)S(1)}) custom-call(s32[17]{0:T(128)S(1)} %stack.131.order_ref, f32[2048,512]{1,0:T(8,128)} %get-tuple-element.198.value_ref, bf16[2048,256]{1,0:T(8,128)(2,1)S(1)} %get-tuple-element.199.ident_ref, bf16[2,128,256]{2,1,0:T(8,128)(2,1)S(1)} %collective-permute-done.9.state_ref.enter_ref, ...), custom_call_target="tpu_custom_call" | custom-call | tf_op jit(solution)/shard_map/pallas_call | solution.py:251
  272.3 28.6 %all-gather.9.cloned.1.call-done = bf16[1376,2048]{1,0:T(8,128)(2,1)} async-done(((bf16[1376,512]{1,0:T(8,128)(2,1)}), bf16[1376,2048]{1,0:T(8,128)(2,1)}) %all-gather.9.cloned.1.call-update) | async-done | bytes 5636112 | tf_op jit(solution)/shard_map/all_gather | solution.py:790
  310.3 8.7 %collective-permute-done.17 = bf16[128,2048]{1,0:T(8,128)(2,1)S(1)} collective-permute-done((bf16[128,2048]{1,0:T(8,128)(2,1)S(1)}, bf16[128,2048]{1,0:T(8,128)(2,1)S(1)}, u32[]{:S(2)}, u32[]{:S(2)}) %collective-permute-start.17) | collective-permute-done | bytes 524320 | tf_op jit(solution)/shard_map/ppermute | solution.py:621
  326.4 10.7 %collective-permute-done.19 = bf16[128,2048]{1,0:T(8,128)(2,1)S(1)} collective-permute-done((bf16[128,2048]{1,0:T(8,128)(2,1)S(1)}, bf16[128,2048]{1,0:T(8,128)(2,1)S(1)}, u32[]{:S(2)}, u32[]{:S(2)}) %collective-permute-start.19) | collective-permute-done | bytes 524320 | tf_op jit(solution)/shard_map/ppermute | solution.py:621
  340.5 26.9 %all-gather.11.cloned.1.call-done = bf16[688,2048]{1,0:T(8,128)(2,1)} async-done(((bf16[688,512]{1,0:T(8,128)(2,1)}), bf16[688,2048]{1,0:T(8,128)(2,1)}) %all-gather.11.cloned.1.call-update) | async-done | bytes 2818064 | tf_op jit(solution)/shard_map/all_gather | solution.py:790
  379.9 16.0 %fusion.135 = f32[1376,2048]{1,0:T(8,128)} fusion(bf16[1376,2048]{1,0:T(8,128)(2,1)} %all-gather.9.cloned.1.call-done, bf16[2048,2048]{1,0:T(8,128)(2,1)S(1)} %shard_map.350), kind=kOutput, calls=%fused_computation.389 | convolution fusion | flops 11542724608 | bytes 25296896 | tf_op jit(solution)/shard_map/dot_general | solution.py:588
  396.0 13.4 %multiply_convert_fusion.1 = (bf16[688,2048]{1,0:T(8,128)(2,1)S(1)}, bf16[688,2048]{1,0:T(8,128)(2,1)}, bf16[688,2048]{1,0:T(8,128)(2,1)}) fusion(f32[1376,2048]{1,0:T(8,128)} %fusion.135, bf16[688,2048]{1,0:T(8,128)(2,1)} %all-gather.11.cloned.1.call-done, bf16[2048,2048]{1,0:T(8,128)(2,1)S(1)} %bitcast.147), kind=kOutput, calls=%fused_computation.18 | convolution fusion | flops 5792497664 | bytes 30932992 | tf_op jit(solution)/shard_map/dot_general | solution.py:588
  409.4 12.2 %convolution_convert_fusion.5 = bf16[1024,2048]{1,0:T(8,128)(2,1)} fusion(bf16[1376,2048]{1,0:T(8,128)(2,1)} %all-gather.9.cloned.1.call-done, bf16[688,2048]{1,0:T(8,128)(2,1)} %get-tuple-element.435, bf16[688,2048]{1,0:T(8,128)(2,1)S(1)} %get-tuple-element.434), kind=kOutput, calls=%fused_computation.38 | convolution fusion | flops 5779095552 | bytes 15466496 | tf_op jit(solution)/shard_map/dot_general | solution.py:584
  421.7 9.6 %convolution_convert_fusion.6 = bf16[1024,2048]{1,0:T(8,128)(2,1)S(1)} fusion(bf16[1376,2048]{1,0:T(8,128)(2,1)} %all-gather.9.cloned.1.call-done, bf16[688,2048]{1,0:T(8,128)(2,1)S(1)} %copy-done.40, bf16[688,2048]{1,0:T(8,128)(2,1)} %copy-done.39), kind=kOutput, calls=%fused_computation.39 | convolution fusion | flops 5779095552 | bytes 15466496 | tf_op jit(solution)/shard_map/dot_general | solution.py:584
  444.8 7.4 convolution_convert_fusion.10
  452.3 18.2 %convolution_convert_fusion = bf16[1376,2048]{1,0:T(8,128)(2,1)} fusion(bf16[1376,2048]{1,0:T(8,128)(2,1)} %pad_maximum_fusion.2, bf16[2048,2048]{1,0:T(8,128)(2,1)} %copy-done.1), kind=kOutput, calls=%fused_computation.11 | convolution fusion | flops 11545542656 | bytes 19660800 | tf_op jit(solution)/shard_map/dot_general | solution.py:580
  473.7 12.6 %collective-permute-done.31 = bf16[128,2048]{1,0:T(8,128)(2,1)S(1)} collective-permute-done((bf16[128,2048]{1,0:T(8,128)(2,1)S(1)}, bf16[128,2048]{1,0:T(8,128)(2,1)S(1)}, u32[]{:S(2)}, u32[]{:S(2)}) %collective-permute-start.31) | collective-permute-done | bytes 524320 | tf_op jit(solution)/shard_map/ppermute | solution.py:621
  492.3 10.5 %collective-permute-done.33 = bf16[128,2048]{1,0:T(8,128)(2,1)S(1)} collective-permute-done((bf16[128,2048]{1,0:T(8,128)(2,1)S(1)}, bf16[128,2048]{1,0:T(8,128)(2,1)S(1)}, u32[]{:S(2)}, u32[]{:S(2)}) %collective-permute-start.33) | collective-permute-done | bytes 524320 | tf_op jit(solution)/shard_map/ppermute | solution.py:621
  504.5 7.9 convolution_convert_fusion.3
  525.9 12.0 %collective-permute-done.35.refs_1_ = bf16[256,2048]{1,0:T(8,128)(2,1)S(1)} collective-permute-done((bf16[256,2048]{1,0:T(8,128)(2,1)S(1)}, bf16[256,2048]{1,0:T(8,128)(2,1)S(1)}, u32[]{:S(2)}, u32[]{:S(2)}) %collective-permute-start.35) | collective-permute-done | bytes 1048608 | tf_op jit(solution)/shard_map/ppermute | solution.py:617
  558.9 9.6 %shard_map.352 = (bf16[2048,512]{1,0:T(8,128)(2,1)S(1)}, bf16[2048,512]{1,0:T(8,128)(2,1)S(1)}, f32[8,256]{1,0:T(8,128)S(1)}, f32[2,128,256]{2,1,0:T(8,128)S(1)}) custom-call(s32[17]{0:T(128)S(1)} %copy-done.15, bf16[2048,512]{1,0:T(8,128)(2,1)} %convolution_convert_fusion.13.grad_ref, f32[2048,512]{1,0:T(8,128)} %get-tuple-element.272.out_ref, ...), custom_call_target="tpu_custom_call" | custom-call | tf_op jit(solution)/shard_map/pallas_call | solution.py:306
  569.9 6.7 collective-permute-done.43
  613.7 13.5 %reduce-scatter.7.cloned.1.call-done = bf16[1376,512]{1,0:T(8,128)(2,1)} async-done(((bf16[1376,2048]{1,0:T(8,128)(2,1)}), bf16[1376,512]{1,0:T(8,128)(2,1)}) %reduce-scatter.7.cloned.1.call-update) | async-done | bytes 1409040 | tf_op jit(solution)/shard_map/reduce_scatter | solution.py:794
  637.8 48.4 %shard_map.353 = (bf16[2048,1664]{1,0:T(8,128)(2,1)}, f32[32,1024]{1,0:T(8,128)}, f32[16,128]{1,0:T(8,128)}, f32[8,1024]{1,0:T(8,128)}) custom-call(s32[17]{0:T(128)} %copy-done.14, bf16[2048,512]{1,0:T(8,128)(2,1)} %copy-done.6, bf16[2048,1024]{1,0:T(8,128)(2,1)} %convolution_convert_fusion.9.proj_ref.before_ref, ...), custom_call_target="tpu_custom_call" | custom-call | tf_op jit(solution)/shard_map/pallas_call | solution.py:511
  697.6 14.0 %fusion.6 = bf16[2048,1024]{1,0:T(8,128)(2,1)} fusion(bf16[2048,2048]{1,0:T(8,128)(2,1)} %copy-done, bf16[2048,1664]{1,0:T(8,128)(2,1)} %fusion.71), kind=kOutput, calls=%fused_computation.35 | convolution fusion | flops 8592031744 | bytes 16777216 | tf_op jit(solution)/shard_map/dot_general | solution.py:584
  711.6 12.2 %convolution_convert_fusion.2 = bf16[1024,2048]{1,0:T(8,128)(2,1)} fusion(bf16[1664,2048]{1,0:T(8,128)(2,1)} %constant_dynamic-update-slice_fusion.5, bf16[2048,1664]{1,0:T(8,128)(2,1)} %fusion.71), kind=kOutput, calls=%fused_computation.34 | convolution fusion | flops 6981419008 | bytes 14417920 | tf_op jit(solution)/shard_map/dot_general | solution.py:580
  723.9 11.2 %convolution_convert_fusion.1 = bf16[1024,2048]{1,0:T(8,128)(2,1)S(1)} fusion(bf16[1664,2048]{1,0:T(8,128)(2,1)} %constant_dynamic-update-slice_fusion.5, bf16[2048,1664]{1,0:T(8,128)(2,1)} %fusion.71), kind=kOutput, calls=%fused_computation.33 | convolution fusion | flops 6981419008 | bytes 14417920 | tf_op jit(solution)/shard_map/dot_general | solution.py:580
  755.4 12.1 %collective-permute-done.54 = bf16[256,2048]{1,0:T(8,128)(2,1)} collective-permute-done((bf16[256,2048]{1,0:T(8,128)(2,1)}, bf16[256,2048]{1,0:T(8,128)(2,1)}, u32[]{:S(2)}, u32[]{:S(2)}) %collective-permute-start.54) | collective-permute-done | bytes 1048608 | tf_op jit(solution)/shard_map/ppermute | solution.py:617
  810.2 13.4 %collective-permute-done.60 = bf16[256,2048]{1,0:T(8,128)(2,1)S(1)} collective-permute-done((bf16[256,2048]{1,0:T(8,128)(2,1)S(1)}, bf16[256,2048]{1,0:T(8,128)(2,1)S(1)}, u32[]{:S(2)}, u32[]{:S(2)}) %collective-permute-start.60) | collective-permute-done | bytes 1048608 | tf_op jit(solution)/shard_map/ppermute | solution.py:621
  (596 shorter events, 360.1 us)
Async XLA Ops:
  7.2 106.9 %all-gather.5.cloned.1.call-start = ((), (), s32[]{:S(2)}) async-start(), calls=%async_computation.4 | async-start | bytes 5242880 | tf_op jit(solution)/shard_map/all_gather | solution.py:790
  27.5 171.4 %all-gather.7.cloned.1.call-start = ((), (), s32[]{:S(2)}) async-start(), calls=%async_computation.5 | async-start | bytes 5242880 | tf_op jit(solution)/shard_map/all_gather | solution.py:790
  29.5 62.3 %collective-permute-start.12 = (bf16[1024,256]{1,0:T(8,128)(2,1)}, bf16[1024,256]{1,0:T(8,128)(2,1)}, u32[]{:S(2)}, u32[]{:S(2)}) collective-permute-start(bf16[1024,256]{1,0:T(8,128)(2,1)} %pad_maximum_fusion.33), channel_id=1, source_target_pairs={{0,4},{4,0},{8,12},{12,8},{16,20},{20,16},{24,28},{28,24},{1,5},{5... | collective-permute-start | bytes 1572872 | tf_op jit(solution)/shard_map/ppermute | solution.py:617
  35.7 52.4 %collective-permute-start.1 = (bf16[512,2048]{1,0:T(8,128)(2,1)S(1)}, bf16[512,2048]{1,0:T(8,128)(2,1)S(1)}, u32[]{:S(2)}, u32[]{:S(2)}) collective-permute-start(bf16[512,2048]{1,0:T(8,128)(2,1)S(1)} %constant_dynamic-slice_fusion.40), channel_id=1, source_target_pairs={{0,4},{4,0},{8,12},{12,8},{16,20},{20,16},{24,28},{28,24},{1,5},{5... | collective-permute-start | bytes 6291464 | tf_op jit(solution)/shard_map/ppermute | solution.py:617
  49.2 41.4 %collective-permute-start.5 = (bf16[4,4096]{1,0:T(4,128)(2,1)S(1)}, bf16[4,4096]{1,0:T(4,128)(2,1)S(1)}, u32[]{:S(2)}, u32[]{:S(2)}) collective-permute-start(bf16[4,4096]{1,0:T(4,128)(2,1)S(1)} %pad_maximum_fusion.37), channel_id=1, source_target_pairs={{0,16},{4,20},{8,24},{12,28},{16,0},{20,4},{24,8},{28,12},{1,17},{... | collective-permute-start | bytes 98312 | tf_op jit(solution)/shard_map/ppermute | solution.py:757
  89.0 90.6 %collective-permute-start.16 = (bf16[1376,256]{1,0:T(8,128)(2,1)}, bf16[1376,256]{1,0:T(8,128)(2,1)}, u32[]{:S(2)}, u32[]{:S(2)}) collective-permute-start(bf16[1376,256]{1,0:T(8,128)(2,1)} %pad_maximum_fusion.28), channel_id=1, source_target_pairs={{0,4},{4,0},{8,12},{12,8},{16,20},{20,16},{24,28},{28,24},{1,5},{5... | collective-permute-start | bytes 2113544 | tf_op jit(solution)/shard_map/ppermute | solution.py:617
  94.2 206.7 %all-gather.9.cloned.1.call-start = ((), (), s32[]{:S(2)}) async-start(), calls=%async_computation.6 | async-start | bytes 7045120 | tf_op jit(solution)/shard_map/all_gather | solution.py:790
  129.6 49.9 %collective-permute-start.10 = (bf16[512,2048]{1,0:T(8,128)(2,1)}, bf16[512,2048]{1,0:T(8,128)(2,1)}, u32[]{:S(2)}, u32[]{:S(2)}) collective-permute-start(bf16[512,2048]{1,0:T(8,128)(2,1)} %constant_dynamic-slice_fusion.26), channel_id=1, source_target_pairs={{0,4},{4,0},{8,12},{12,8},{16,20},{20,16},{24,28},{28,24},{1,5},{5... | collective-permute-start | bytes 6291464 | tf_op jit(solution)/shard_map/ppermute | solution.py:617
  179.5 35.0 %collective-permute-start.11 = (bf16[512,2048]{1,0:T(8,128)(2,1)}, bf16[512,2048]{1,0:T(8,128)(2,1)S(1)}, u32[]{:S(2)}, u32[]{:S(2)}) collective-permute-start(bf16[512,2048]{1,0:T(8,128)(2,1)} %collective-permute-done.10), channel_id=1, source_target_pairs={{0,1},{1,0},{2,3},{3,2},{4,5},{5,4},{6,7},{7,6},{8,9},{9,8},{10,11... | collective-permute-start | bytes 6291464 | tf_op jit(solution)/shard_map/ppermute | solution.py:625
  187.7 179.7 %all-gather.11.cloned.1.call-start = ((), (), s32[]{:S(2)}) async-start(), calls=%async_computation.7 | async-start | bytes 3522560 | tf_op jit(solution)/shard_map/all_gather | solution.py:790
  211.2 33.6 %collective-permute-start.9 = (bf16[2,128,256]{2,1,0:T(8,128)(2,1)}, bf16[2,128,256]{2,1,0:T(8,128)(2,1)S(1)}, u32[]{:S(2)}, u32[]{:S(2)}) collective-permute-start(bf16[2,128,256]{2,1,0:T(8,128)(2,1)} %fusion.33), channel_id=1, source_target_pairs={{0,8},{4,12},{8,16},{12,20},{16,24},{20,28},{1,9},{5,13},{9,17},{1... | collective-permute-start | bytes 393224 | tf_op jit(solution)/shard_map/ppermute | solution.py:820
  267.7 33.3 %collective-permute-start.14 = (bf16[256,2048]{1,0:T(8,128)(2,1)}, bf16[256,2048]{1,0:T(8,128)(2,1)}, u32[]{:S(2)}, u32[]{:S(2)}) collective-permute-start(bf16[256,2048]{1,0:T(8,128)(2,1)} %get-tuple-element.206), channel_id=1, source_target_pairs={{0,4},{4,0},{8,12},{12,8},{16,20},{20,16},{24,28},{28,24},{1,5},{5... | collective-permute-start | bytes 3145736 | tf_op jit(solution)/shard_map/ppermute | solution.py:617
  269.4 31.6 %collective-permute-start.15 = (bf16[256,2048]{1,0:T(8,128)(2,1)}, bf16[256,2048]{1,0:T(8,128)(2,1)}, u32[]{:S(2)}, u32[]{:S(2)}) collective-permute-start(bf16[256,2048]{1,0:T(8,128)(2,1)} %pad_maximum_fusion.13), channel_id=1, source_target_pairs={{0,2},{1,3},{2,0},{3,1},{4,6},{5,7},{6,4},{7,5},{8,10},{9,11},{10,... | collective-permute-start | bytes 3145736 | tf_op jit(solution)/shard_map/ppermute | solution.py:621
  271.7 36.4 %collective-permute-start.23 = (bf16[688,256]{1,0:T(8,128)(2,1)}, bf16[688,256]{1,0:T(8,128)(2,1)}, u32[]{:S(2)}, u32[]{:S(2)}) collective-permute-start(bf16[688,256]{1,0:T(8,128)(2,1)} %broadcast_select_fusion.30), channel_id=1, source_target_pairs={{0,4},{4,0},{8,12},{12,8},{16,20},{20,16},{24,28},{28,24},{1,5},{5... | collective-permute-start | bytes 1056776 | tf_op jit(solution)/shard_map/ppermute | solution.py:617
  310.1 194.4 %reduce-scatter.5.cloned.1.call-start = ((), (), s32[]{:S(2)}) async-start(), calls=%async_computation.8 | async-start | bytes 3522560 | tf_op jit(solution)/shard_map/reduce_scatter | solution.py:794
  337.5 29.9 %collective-permute-start.21 = (bf16[256,2048]{1,0:T(8,128)(2,1)S(1)}, bf16[256,2048]{1,0:T(8,128)(2,1)S(1)}, u32[]{:S(2)}, u32[]{:S(2)}) collective-permute-start(bf16[256,2048]{1,0:T(8,128)(2,1)S(1)} %pad_maximum_fusion.14.refs_0_), channel_id=1, source_target_pairs={{0,4},{4,0},{8,12},{12,8},{16,20},{20,16},{24,28},{28,24},{1,5},{5... | collective-permute-start | bytes 3145736 | tf_op jit(solution)/shard_map/ppermute | solution.py:617
  339.0 28.3 %collective-permute-start.22 = (bf16[256,2048]{1,0:T(8,128)(2,1)S(1)}, bf16[256,2048]{1,0:T(8,128)(2,1)}, u32[]{:S(2)}, u32[]{:S(2)}) collective-permute-start(bf16[256,2048]{1,0:T(8,128)(2,1)S(1)} %pad_maximum_fusion.15.refs_2_), channel_id=1, source_target_pairs={{0,2},{1,3},{2,0},{3,1},{4,6},{5,7},{6,4},{7,5},{8,10},{9,11},{10,... | collective-permute-start | bytes 3145736 | tf_op jit(solution)/shard_map/ppermute | solution.py:621
  441.9 28.8 %collective-permute-start.29 = (bf16[256,2048]{1,0:T(8,128)(2,1)}, bf16[256,2048]{1,0:T(8,128)(2,1)S(1)}, u32[]{:S(2)}, u32[]{:S(2)}) collective-permute-start(bf16[256,2048]{1,0:T(8,128)(2,1)} %get-tuple-element.237), channel_id=1, source_target_pairs={{0,4},{4,0},{8,12},{12,8},{16,20},{20,16},{24,28},{28,24},{1,5},{5... | collective-permute-start | bytes 3145736 | tf_op jit(solution)/shard_map/ppermute | solution.py:617
  443.4 27.3 %collective-permute-start.30 = (bf16[256,2048]{1,0:T(8,128)(2,1)}, bf16[256,2048]{1,0:T(8,128)(2,1)}, u32[]{:S(2)}, u32[]{:S(2)}) collective-permute-start(bf16[256,2048]{1,0:T(8,128)(2,1)} %pad_maximum_fusion.17), channel_id=1, source_target_pairs={{0,2},{1,3},{2,0},{3,1},{4,6},{5,7},{6,4},{7,5},{8,10},{9,11},{10,... | collective-permute-start | bytes 3145736 | tf_op jit(solution)/shard_map/ppermute | solution.py:621
  452.3 174.9 %reduce-scatter.7.cloned.1.call-start = ((), (), s32[]{:S(2)}) async-start(), calls=%async_computation.9 | async-start | bytes 7045120 | tf_op jit(solution)/shard_map/reduce_scatter | solution.py:794
  512.4 25.6 %collective-permute-start.35 = (bf16[256,2048]{1,0:T(8,128)(2,1)S(1)}, bf16[256,2048]{1,0:T(8,128)(2,1)S(1)}, u32[]{:S(2)}, u32[]{:S(2)}) collective-permute-start(bf16[256,2048]{1,0:T(8,128)(2,1)S(1)} %pad_maximum_fusion.18.refs_0_), channel_id=1, source_target_pairs={{0,4},{4,0},{8,12},{12,8},{16,20},{20,16},{24,28},{28,24},{1,5},{5... | collective-permute-start | bytes 3145736 | tf_op jit(solution)/shard_map/ppermute | solution.py:617
  513.9 25.4 %collective-permute-start.36 = (bf16[256,2048]{1,0:T(8,128)(2,1)S(1)}, bf16[256,2048]{1,0:T(8,128)(2,1)}, u32[]{:S(2)}, u32[]{:S(2)}) collective-permute-start(bf16[256,2048]{1,0:T(8,128)(2,1)S(1)} %pad_maximum_fusion.19.refs_2_), channel_id=1, source_target_pairs={{0,2},{1,3},{2,0},{3,1},{4,6},{5,7},{6,4},{7,5},{8,10},{9,11},{10,... | collective-permute-start | bytes 3145736 | tf_op jit(solution)/shard_map/ppermute | solution.py:621
  520.4 191.2 %reduce-scatter.9.cloned.1.call-start = ((), (), s32[]{:S(2)}) async-start(), calls=%async_computation.10 | async-start | bytes 5242880 | tf_op jit(solution)/shard_map/reduce_scatter | solution.py:794
  551.1 25.5 %collective-permute-start.43 = (bf16[256,2048]{1,0:T(8,128)(2,1)}, bf16[256,2048]{1,0:T(8,128)(2,1)}, u32[]{:S(2)}, u32[]{:S(2)}) collective-permute-start(bf16[256,2048]{1,0:T(8,128)(2,1)} %get-tuple-element.279), channel_id=1, source_target_pairs={{0,4},{4,0},{8,12},{12,8},{16,20},{20,16},{24,28},{28,24},{1,5},{5... | collective-permute-start | bytes 3145736 | tf_op jit(solution)/shard_map/ppermute | solution.py:617
  551.7 25.2 %collective-permute-start.44 = (bf16[256,2048]{1,0:T(8,128)(2,1)}, bf16[256,2048]{1,0:T(8,128)(2,1)}, u32[]{:S(2)}, u32[]{:S(2)}) collective-permute-start(bf16[256,2048]{1,0:T(8,128)(2,1)} %pad_maximum_fusion.21), channel_id=1, source_target_pairs={{0,2},{1,3},{2,0},{3,1},{4,6},{5,7},{6,4},{7,5},{8,10},{9,11},{10,... | collective-permute-start | bytes 3145736 | tf_op jit(solution)/shard_map/ppermute | solution.py:621
  627.9 182.3 %reduce-scatter.11.cloned.1.call-start = ((), (), s32[]{:S(2)}) async-start(), calls=%async_computation.11 | async-start | bytes 5242880 | tf_op jit(solution)/shard_map/reduce_scatter | solution.py:794
  630.9 64.1 %collective-permute-start.51 = (bf16[256,2048]{1,0:T(8,128)(2,1)S(1)}, bf16[256,2048]{1,0:T(8,128)(2,1)S(1)}, u32[]{:S(2)}, u32[]{:S(2)}) collective-permute-start(bf16[256,2048]{1,0:T(8,128)(2,1)S(1)} %constant_dynamic-update-slice_fusion.3), channel_id=1, source_target_pairs={{0,2},{1,3},{2,0},{3,1},{4,6},{5,7},{6,4},{7,5},{8,10},{9,11},{10,... | collective-permute-start | bytes 3145736 | tf_op jit(solution)/shard_map/ppermute | solution.py:621
  632.5 62.5 %collective-permute-start.49 = (bf16[1376,256]{1,0:T(8,128)(2,1)S(1)}, bf16[1376,256]{1,0:T(8,128)(2,1)S(1)}, u32[]{:S(2)}, u32[]{:S(2)}) collective-permute-start(bf16[1376,256]{1,0:T(8,128)(2,1)S(1)} %constant_dynamic-slice_fusion.24), channel_id=1, source_target_pairs={{0,4},{4,0},{8,12},{12,8},{16,20},{20,16},{24,28},{28,24},{1,5},{5... | collective-permute-start | bytes 2113544 | tf_op jit(solution)/shard_map/ppermute | solution.py:617
  637.3 57.6 %collective-permute-start.50 = (bf16[688,256]{1,0:T(8,128)(2,1)S(1)}, bf16[688,256]{1,0:T(8,128)(2,1)S(1)}, u32[]{:S(2)}, u32[]{:S(2)}) collective-permute-start(bf16[688,256]{1,0:T(8,128)(2,1)S(1)} %constant_dynamic-slice_fusion.23), channel_id=1, source_target_pairs={{0,4},{4,0},{8,12},{12,8},{16,20},{20,16},{24,28},{28,24},{1,5},{5... | collective-permute-start | bytes 1056776 | tf_op jit(solution)/shard_map/ppermute | solution.py:617
  741.6 25.9 %collective-permute-start.54 = (bf16[256,2048]{1,0:T(8,128)(2,1)}, bf16[256,2048]{1,0:T(8,128)(2,1)}, u32[]{:S(2)}, u32[]{:S(2)}) collective-permute-start(bf16[256,2048]{1,0:T(8,128)(2,1)} %get-tuple-element.328), channel_id=1, source_target_pairs={{0,4},{4,0},{8,12},{12,8},{16,20},{20,16},{24,28},{28,24},{1,5},{5... | collective-permute-start | bytes 3145736 | tf_op jit(solution)/shard_map/ppermute | solution.py:617
  743.0 25.6 %collective-permute-start.55 = (bf16[256,2048]{1,0:T(8,128)(2,1)}, bf16[256,2048]{1,0:T(8,128)(2,1)}, u32[]{:S(2)}, u32[]{:S(2)}) collective-permute-start(bf16[256,2048]{1,0:T(8,128)(2,1)} %pad_maximum_fusion.23), channel_id=1, source_target_pairs={{0,2},{1,3},{2,0},{3,1},{4,6},{5,7},{6,4},{7,5},{8,10},{9,11},{10,... | collective-permute-start | bytes 3145736 | tf_op jit(solution)/shard_map/ppermute | solution.py:621
  799.3 24.3 %collective-permute-start.60 = (bf16[256,2048]{1,0:T(8,128)(2,1)S(1)}, bf16[256,2048]{1,0:T(8,128)(2,1)S(1)}, u32[]{:S(2)}, u32[]{:S(2)}) collective-permute-start(bf16[256,2048]{1,0:T(8,128)(2,1)S(1)} %pad_maximum_fusion.24), channel_id=1, source_target_pairs={{0,2},{1,3},{2,0},{3,1},{4,6},{5,7},{6,4},{7,5},{8,10},{9,11},{10,... | collective-permute-start | bytes 3145736 | tf_op jit(solution)/shard_map/ppermute | solution.py:621
  (135 other events, 1853.8 us)
Sparse Core Ops, SparseCore 0:
  27.6 83.6 all-gather.4
  113.4 79.1 all-gather.6
  194.7 106.2 all-gather.8
  310.2 57.1 all-gather.10
  452.4 52.0 reduce-scatter.4
  520.6 106.5 reduce-scatter.6
  629.5 77.8 reduce-scatter.8
  724.1 77.9 reduce-scatter.10
